TPU v7x, 512 devices: a whole 4x8x8 slice. The times are simulated.
512 devices in a mesh: dp: 32 (over x_hi, y, core), mp: 16 (over x_lo, z).
Axes of the slice: x: 4 (x_hi: 2, x_lo: 2; x = x_hi * 2 + x_lo), y: 8, z: 8, core: 2. Of those that a mesh axis runs over, the one named last changes fastest.
Arguments:
- tokens: bfloat16 [8192, 6144], P('dp', 'mp'), may hold values from -200 to 200
- ln_gain: bfloat16 [6144], P('mp'), may hold values from 0.2 to 2.8
- qkv_weight: bfloat16 [3, 6144, 4096], P(None, 'dp', 'mp'), may hold values from -0.08292543 to 0.08292543
- qk_gain: float32 [2, 128], replicated, may hold values from 0.5 to 2
- cotangent: bfloat16 [8192, 4096], P('dp', 'mp'), may hold values from -6 to 6
Outputs:
- attended: bfloat16 [8192, 4096], P('dp', 'mp')
- grad_tokens: bfloat16 [8192, 6144], P('dp', 'mp')
All inputs are finite; a program needn't handle non-finite values.
Results may differ from a plain program's by a relative error of at most 0.034.
Values may be sent and summed in bfloat16 or wider, within the bound.
No kernel may reach another device: no remote copies, remote signals or barrier semaphores. Data moves between devices by JAX's collectives and lax.ppermute only.
A program may use at most 64 MiB of HBM per device.

v0:
```python
import jax
import jax.numpy as jnp
from jax import lax
from jax.sharding import PartitionSpec as P

HEADSZ = 128
PATCH = 256


def norm_rows(field):
    row_mean = jnp.mean(field, axis=-1, keepdims=True)
    centred = field - row_mean
    inv_std = lax.rsqrt(jnp.mean(centred * centred, axis=-1, keepdims=True) + 1e-06)
    return (centred * inv_std, inv_std)


def norm_back(grad_hat, x_hat, inv_std):
    first = jnp.mean(grad_hat, axis=-1, keepdims=True)
    second = jnp.mean(grad_hat * x_hat, axis=-1, keepdims=True)
    return inv_std * (grad_hat - first - x_hat * second)


def per_device(tokens, ln_gain, qkv_weight, qk_gain, cotangent):
    f32 = jnp.float32
    bf16 = jnp.bfloat16
    tok_rows = tokens.shape[0]
    feat_dev = tokens.shape[1]
    width = qkv_weight.shape[2]
    gathered, gain_full = (
        lax.all_gather(tokens, "mp", axis=1, tiled=True),
        lax.all_gather(ln_gain, "mp", axis=0, tiled=True),
    )
    x_hat, inv_std = norm_rows(gathered.astype(f32))
    normed = (x_hat * gain_full.astype(f32)).astype(bf16)
    weights_full = lax.all_gather(qkv_weight, "dp", axis=1, tiled=True)
    projected = jnp.einsum("td,idf->itf", normed, weights_full, preferred_element_type=f32)
    heads_dev = width // HEADSZ
    images = tok_rows // PATCH
    split = projected.reshape(3, images, PATCH, heads_dev, HEADSZ)
    q_hat, q_inv = norm_rows(split[0])
    k_hat, k_inv = norm_rows(split[1])
    queries = (q_hat * qk_gain[0]).astype(bf16)
    keys_n = (k_hat * qk_gain[1]).astype(bf16)
    values = split[2].astype(bf16)
    scale = HEADSZ ** (-0.5)
    scores = jnp.einsum("bqhe,bkhe->bhqk", queries, keys_n, preferred_element_type=f32) * scale
    expo = jnp.exp(scores)
    probs = expo / jnp.sum(expo, axis=-1, keepdims=True)
    weights_b = probs.astype(bf16)
    attended = (
        jnp.einsum("bhqk,bkhe->bqhe", weights_b, values, preferred_element_type=f32)
        .astype(bf16)
        .reshape(tok_rows, width)
    )
    upstream = cotangent.reshape(images, PATCH, heads_dev, HEADSZ)
    d_probs = jnp.einsum("bqhe,bkhe->bhqk", upstream, values, preferred_element_type=f32)
    d_values = jnp.einsum(
        "bhqk,bqhe->bkhe", weights_b, upstream, preferred_element_type=f32
    ).astype(bf16)
    inner = jnp.sum(probs * d_probs, axis=-1, keepdims=True)
    d_scores = (probs * (d_probs - inner) * scale).astype(bf16)
    d_queries = jnp.einsum("bhqk,bkhe->bqhe", d_scores, keys_n, preferred_element_type=f32)
    d_keys = jnp.einsum("bhqk,bqhe->bkhe", d_scores, queries, preferred_element_type=f32)
    grad_q = norm_back(d_queries * qk_gain[0], q_hat, q_inv).astype(bf16)
    grad_k = norm_back(d_keys * qk_gain[1], k_hat, k_inv).astype(bf16)
    grads = jnp.stack([grad_q, grad_k, d_values]).reshape(3, tok_rows, width)
    partial_sum = jnp.einsum("itf,idf->td", grads, weights_full, preferred_element_type=f32)
    d_normed = lax.psum(partial_sum.astype(jnp.bfloat16), "mp").astype(jnp.float32)
    grad_full = norm_back(d_normed * gain_full.astype(f32), x_hat, inv_std)
    grad_own = lax.dynamic_slice_in_dim(grad_full, lax.axis_index("mp") * feat_dev, feat_dev, 1)
    return (attended, grad_own.astype(bf16))


def solution(mesh):
    return jax.shard_map(
        per_device,
        mesh=mesh,
        in_specs=(P("dp", "mp"), P("mp"), P(None, "dp", "mp"), P(), P("dp", "mp")),
        out_specs=(P("dp", "mp"), P("dp", "mp")),
        check_vma=False,
    )
```

profile of v0, /device:TPU:6, one launch (start us, length us, event | category | flops | bytes accessed | tf_op | source)
XLA Modules:
  0.0 404.1 jit_solution(798788939850172581)
XLA Ops:
  7.2 0.7 all-gather.4.cloned.1.call-update
  7.9 0.7 all-gather.6.cloned.1.call-update
  8.7 0.7 reshape.264
  9.4 38.9 %all-gather = bf16[16,1,384]{2,1,0:T(2,128)(2,1)S(1)} all-gather(bf16[1,1,384]{2,1,0:T(2,128)(2,1)S(1)} %reshape.264), channel_id=1, replica_groups=mesh['dp'=32,'mp'=16] {'mp'}, dimensions={0}, use_global_device_ids=true | all-gather | bytes 13056 | tf_op jit(solution)/shard_map/all_gather | solution.py:31
  48.3 1.7 copy.40
  50.0 1.3 slice_bitcast_fusion
  51.3 40.3 %all-gather.4.cloned.1.call-done = bf16[256,6144]{1,0:T(8,128)(2,1)} async-done(((bf16[256,384]{1,0:T(8,128)(2,1)}), bf16[256,6144]{1,0:T(8,128)(2,1)}) %all-gather.4.cloned.1.call-update) | async-done | bytes 3145744 | tf_op jit(solution)/shard_map/all_gather | solution.py:30
  91.7 2.5 convert_reduce_fusion
  94.2 2.9 fusion.4
  97.1 104.5 %all-gather.6.cloned.1.call-done = bf16[3,6144,256]{2,1,0:T(8,128)(2,1)} async-done(((bf16[3,192,256]{2,1,0:T(8,128)(2,1)}), bf16[3,6144,256]{2,1,0:T(8,128)(2,1)}) %all-gather.6.cloned.1.call-update) | async-done | bytes 9437200 | tf_op jit(solution)/shard_map/all_gather | solution.py:35
  201.6 6.9 %fusion.10 = f32[3,256,256]{1,2,0:T(8,128)S(1)} fusion(bf16[3,6144,256]{2,1,0:T(8,128)(2,1)} %all-gather.6.cloned.1.call-done, f32[6144]{0:T(1024)S(1)} %bitcast.86, bf16[256,6144]{1,0:T(8,128)(2,1)S(1)} %copy-done, f32[256]{0:T(256)S(1)} %add_rsqrt_fusion.2, f32[256]{0:T(256)S(1)} %broadcast_multiply_fusion.8), kind=kOutput, calls=%fused_computation.15 | convolution fusion | flops 2423783424 | bytes 13395968 | tf_op jit(solution)/shard_map/td,idf->itf/dot_general | solution.py:36
  208.6 0.7 slice.34
  209.5 0.7 fusion.51
  210.4 1.0 reduce_sum.128
  211.4 1.0 multiply_reduce_fusion.5
  212.4 1.1 multiply_convert_fusion.3
  214.1 1.1 fusion.13
  215.2 2.0 fusion.35
  217.2 2.0 convolution_bitcast_fusion.1
  219.3 3.2 fusion.49
  222.5 3.1 fusion.50
  225.6 1.5 convolution_convert_fusion
  227.2 0.7 broadcast_multiply_fusion.2
  228.6 0.7 broadcast_multiply_fusion
  229.9 1.3 multiply_convert_fusion.2
  231.2 0.8 copy.30
  232.1 8.1 %fusion.1 = bf16[256,6144]{1,0:T(8,128)(2,1)} fusion(bf16[3,6144,256]{2,1,0:T(8,128)(2,1)} %all-gather.6.cloned.1.call-done, bf16[1,256,256]{2,1,0:T(8,128)(2,1)S(1)} %copy.31, bf16[1,256,256]{2,1,0:T(8,128)(2,1)} %copy.30, bf16[1,256,256]{2,1,0:T(8,128)(2,1)S(1)} %copy.29), kind=kOutput, calls=%fused_computation.4 | convolution fusion | flops 2417885184 | bytes 12976128 | tf_op jit(solution)/shard_map/itf,idf->td/dot_general | solution.py:67
  240.2 1.4 convolution_convert_fusion.1
  241.7 0.8 copy.32
  242.5 150.2 %all-reduce.2.cloned.1.call-done = bf16[256,6144]{1,0:T(8,128)(2,1)} async-done(((bf16[256,6144]{1,0:T(8,128)(2,1)}), bf16[256,6144]{1,0:T(8,128)(2,1)}) %all-reduce.2.cloned.1.call-update) | async-done | bytes 3145744 | tf_op jit(solution)/shard_map/psum | solution.py:68
  392.6 4.1 %fusion.9 = (f32[256]{0:T(256)S(1)}, f32[256]{0:T(256)S(1)}, f32[256,6144]{1,0:T(8,128)S(1)}, f32[256,6144]{1,0:T(8,128)S(1)}) fusion(f32[6144]{0:T(1024)} %bitcast.87, bf16[256,6144]{1,0:T(8,128)(2,1)} %all-reduce.2.cloned.1.call-done, f32[256]{0:T(256)S(1)} %copy-done.8, f32[256]{0:T(256)S(1)} %copy-done.6, bf16[256,6144]{1,0:T(8,128)(2,1)S(1)} %copy-done), kind=kLoop, calls=%fused_computation.14 | loop fusion | flops 12582400 | bytes 18903040 | tf_op jit(solution)/shard_map/reduce_sum | solution.py:18
  396.8 0.9 fusion.28
  (37 shorter events, 2.7 us)
Async XLA Ops:
  7.2 84.5 %all-gather.4.cloned.1.call-start = ((), (), s32[]{:S(2)}) async-start(), calls=%async_computation | async-start | bytes 3342336 | tf_op jit(solution)/shard_map/all_gather | solution.py:30
  7.9 193.7 %all-gather.6.cloned.1.call-start = ((), (), s32[]{:S(2)}) async-start(), calls=%async_computation.1 | async-start | bytes 9732096 | tf_op jit(solution)/shard_map/all_gather | solution.py:35
  8.6 384.0 %all-reduce.2.cloned.1.call-start = ((), (), s32[]{:S(2)}) async-start(), calls=%async_computation.2 | async-start | bytes 6291456 | tf_op jit(solution)/shard_map/psum | solution.py:68
  48.3 160.2 %copy-start.4 = (f32[16,1,384]{2,1,0:T(1,128)}, f32[16,1,384]{2,1,0:T(1,128)S(1)}, u32[]{:S(2)}) copy-start(f32[16,1,384]{2,1,0:T(1,128)S(1)} %convert_element_type.96) | copy-start | bytes 73732
  91.7 109.9 %copy-start = (bf16[256,6144]{1,0:T(8,128)(2,1)S(1)}, bf16[256,6144]{1,0:T(8,128)(2,1)}, u32[]{:S(2)}) copy-start(bf16[256,6144]{1,0:T(8,128)(2,1)} %all-gather.4.cloned.1.call-done) | copy-start | bytes 9437188
  94.2 114.3 %copy-start.5 = (f32[256]{0:T(256)}, f32[256]{0:T(256)S(1)}, u32[]{:S(2)}) copy-start(f32[256]{0:T(256)S(1)} %broadcast_multiply_fusion.8) | copy-start | bytes 3076
  97.1 111.5 %copy-start.7 = (f32[256]{0:T(256)}, f32[256]{0:T(256)S(1)}, u32[]{:S(2)}) copy-start(f32[256]{0:T(256)S(1)} %add_rsqrt_fusion.2) | copy-start | bytes 3076
  208.6 0.9 copy-start.1
  213.4 0.6 copy-start.2
  232.1 8.1 %copy-start.3 = (bf16[1,256,256]{1,2,0:T(8,128)(2,1)S(1)}, bf16[1,256,256]{1,2,0:T(8,128)(2,1)}, u32[]{:S(2)}) copy-start(bf16[1,256,256]{1,2,0:T(8,128)(2,1)} %slice.34) | copy-start | bytes 393220
  232.1 160.5 %copy-start.6 = (f32[256]{0:T(256)S(1)}, f32[256]{0:T(256)}, u32[]{:S(2)}) copy-start(f32[256]{0:T(256)} %copy-done.5) | copy-start | bytes 3076
  232.1 160.5 %copy-start.8 = (f32[256]{0:T(256)S(1)}, f32[256]{0:T(256)}, u32[]{:S(2)}) copy-start(f32[256]{0:T(256)} %copy-done.7) | copy-start | bytes 3076
Sparse Core Ops, SparseCore 0:
  10.1 81.5 all-gather.3
  95.0 106.6 all-gather.5
  240.4 152.2 all-reduce.1
where the time goes:
time: 406 us; the launch traced here: 404 us
  waiting for transfers between devices  296 us (73%)
  blocking collectives  38.9 us (10%)
  matrix products  29.4 us (7%)
  other arithmetic  17.6 us (4%)
  between operations  13.9 us (3%)
  local copies, waits for them, and re-layouts  7.75 us (2%)
    psum x1, waiting for transfers between devices, per_device(): lax.psum(partial_sum.astype(jnp.bfloat16), 'mp').astype(jnp.float32)  150 us
    all_gather x1, waiting for transfers between devices, per_device(): weights_full = lax.all_gather(qkv_weight, 'dp', axis=1, tiled=True)  105 us
    all_gather x1, waiting for transfers between devices, per_device(): lax.all_gather(tokens, 'mp', axis=1, tiled=True)  40.3 us
    all_gather x1, blocking collectives, per_device(): lax.all_gather(ln_gain, 'mp', axis=0, tiled=True)  38.9 us
  transfers between devices with their start and end apart: 3, of which 3 were waited for; matrix products, arithmetic and copies ran while one was open for 3% of the time, Pallas kernels for 0%

commit v1 on v0

v1 whole, which is shorter than its diff:
```python
import jax
import jax.numpy as jnp
from jax import lax
from jax.experimental import pallas as pl
from jax.experimental.pallas import tpu as pltpu
from jax.sharding import Mesh, PartitionSpec as P

HEADSZ = 128
PATCH = 256
EPS = 1e-06
GAIN_ROWS = 16
F32 = jnp.float32
BF16 = jnp.bfloat16
VMEM = pl.BlockSpec(memory_space=pltpu.VMEM)
SMEM = pl.BlockSpec(memory_space=pltpu.SMEM)


def params(mib):
    return pltpu.CompilerParams(vmem_limit_bytes=mib * 1024 * 1024)


def dot(a, b, ca, cb):
    return lax.dot_general(a, b, (((ca,), (cb,)), ((), ())), preferred_element_type=F32)


def lane_fold(x):
    total = x[:, :128]
    for at in range(128, x.shape[1], 128):
        total = total + x[:, at : at + 128]
    return total


def normalise_kernel(feat_all, z_ref, *refs):
    pieces = refs[:-2]
    normed_ref, stat_ref = refs[-2:]
    z = z_ref[0]
    zs = 8
    blocks = []
    own = pieces[0]
    for xl in range(2):
        blocks.append((own, xl, xl * zs + z))
    for step in range(1, 4):
        for xl in range(2):
            blocks.append((pieces[2 * step - 1], xl, xl * zs + lax.rem(z + zs - step, zs)))
            blocks.append((pieces[2 * step], xl, xl * zs + lax.rem(z + step, zs)))
    far = lax.rem(z + 4, zs)
    blocks.append((pieces[7], 0, far))
    blocks.append((pieces[8], 0, zs + far))
    rows = PATCH
    total = jnp.zeros((rows, 128), F32)
    for ref, at, _ in blocks:
        total = total + lane_fold(ref[at, :rows, :].astype(F32))
    mean = jnp.sum(total, axis=1, keepdims=True) / feat_all
    total = jnp.zeros((rows, 128), F32)
    for ref, at, _ in blocks:
        centred = ref[at, :rows, :].astype(F32) - mean
        total = total + lane_fold(centred * centred)
    inv = lax.rsqrt(jnp.sum(total, axis=1, keepdims=True) / feat_all + EPS)
    for ref, at, place in blocks:
        x_hat = (ref[at, :rows, :].astype(F32) - mean) * inv
        gain = ref[at, rows : rows + 1, :].astype(F32)
        normed_ref[place, :rows, :] = (x_hat * gain).astype(BF16)
        normed_ref[place, rows:, :] = ref[at, rows:, :]
    stat_ref[0] = jnp.broadcast_to(mean, (rows, 128))
    stat_ref[1] = jnp.broadcast_to(inv, (rows, 128))


def norm128(x):
    mean = jnp.mean(x, axis=1, keepdims=True)
    centred = x - mean
    inv = lax.rsqrt(jnp.mean(centred * centred, axis=1, keepdims=True) + EPS)
    return centred * inv, inv


def norm128_back(grad_hat, x_hat, inv):
    first = jnp.mean(grad_hat, axis=1, keepdims=True)
    second = jnp.mean(grad_hat * x_hat, axis=1, keepdims=True)
    return inv * (grad_hat - first - x_hat * second)


def attention_kernel(normed_ref, w_ref, qk_ref, cot_ref, out_ref, grads_ref, stat_ref, acc):
    n_m = normed_ref.shape[0]
    third = w_ref.shape[2] // 3
    width = w_ref.shape[3]
    heads = width // HEADSZ
    acc[...] = jnp.zeros_like(acc)

    def step(m, carry):
        xh = m // 8
        y = lax.rem(m, 8)
        x = normed_ref[m]
        for i in range(3):
            w = jnp.concatenate(
                [w_ref[2 * y + c, xh, i * third : (i + 1) * third, :] for c in range(2)], axis=0
            )
            acc[:, i * width : (i + 1) * width] += dot(x, w, 1, 0)
        return carry

    lax.fori_loop(0, n_m, step, 0)
    rows = PATCH
    scale = HEADSZ ** (-0.5)
    gain_q = qk_ref[0:1, :]
    gain_k = qk_ref[1:2, :]
    first = jnp.zeros((rows, 128), F32)
    second = jnp.zeros((rows, 128), F32)
    for h in range(heads):
        cols = [slice(i * width + h * HEADSZ, i * width + (h + 1) * HEADSZ) for i in range(3)]
        own = slice(h * HEADSZ, (h + 1) * HEADSZ)
        proj = [acc[:rows, c] for c in cols]
        q_hat, q_inv = norm128(proj[0])
        k_hat, k_inv = norm128(proj[1])
        queries = (q_hat * gain_q).astype(BF16)
        keys = (k_hat * gain_k).astype(BF16)
        values = proj[2].astype(BF16)
        expo = jnp.exp(dot(queries, keys, 1, 1) * scale)
        probs = expo / jnp.sum(expo, axis=1, keepdims=True)
        weights_b = probs.astype(BF16)
        out_ref[:, own] = dot(weights_b, values, 1, 0).astype(BF16)
        upstream = cot_ref[:, own]
        d_probs = dot(upstream, values, 1, 1)
        d_values = dot(weights_b, upstream, 0, 0).astype(BF16)
        inner = jnp.sum(probs * d_probs, axis=1, keepdims=True)
        d_scores = (probs * (d_probs - inner) * scale).astype(BF16)
        d_queries = dot(d_scores, keys, 1, 0)
        d_keys = dot(d_scores, queries, 0, 0)
        grad_q = norm128_back(d_queries * gain_q, q_hat, q_inv).astype(BF16)
        grad_k = norm128_back(d_keys * gain_k, k_hat, k_inv).astype(BF16)
        for i, grad in enumerate((grad_q, grad_k, d_values)):
            grads_ref[i, :, own] = grad
            wide = grad.astype(F32)
            first = first + wide * acc[rows : rows + 1, cols[i]]
            second = second + wide * proj[i]
    stat_ref[0:1, :] = jnp.sum(first, axis=1)[None, :]
    stat_ref[1:2, :] = jnp.sum(second, axis=1)[None, :]


def backward_kernel(grads_ref, w_ref, out_ref):
    third = w_ref.shape[2] // 3

    def step(m, carry):
        xh = m // 8
        y = lax.rem(m, 8)
        total = None
        for i in range(3):
            w = jnp.concatenate(
                [w_ref[2 * y + c, xh, i * third : (i + 1) * third, :] for c in range(2)], axis=0
            )
            term = dot(grads_ref[i], w, 1, 1)
            total = term if total is None else total + term
        out_ref[2 * y + xh] = total.astype(BF16)
        return carry

    lax.fori_loop(0, out_ref.shape[0], step, 0)


def final_kernel(feat_all, mine_ref, other_ref, tok_ref, gain_ref, stat_ref, sums_ref, out_ref):
    b = (mine_ref[...].astype(F32) + other_ref[...].astype(F32)) * gain_ref[0:1, :].astype(F32)
    mean = stat_ref[0, :, 0:1]
    inv = stat_ref[1, :, 0:1]
    x_hat = (tok_ref[...].astype(F32) - mean) * inv
    first = sums_ref[:, 0:1] / feat_all
    second = sums_ref[:, 1:2] / feat_all
    out_ref[...] = (inv * (b - first - x_hat * second)).astype(BF16)


def ring(n, step):
    return [(i, (i + step) % n) for i in range(n)]


def per_device(tokens, ln_gain, qkv_weight, qk_gain, cotangent):
    rows, feat = tokens.shape
    width = qkv_weight.shape[2]
    feat_all = feat * 16
    z = lax.axis_index("z").astype(jnp.int32)

    weights = qkv_weight.reshape(-1, width)
    weights = lax.all_gather(weights, "xh", axis=0)
    weights = lax.all_gather(weights, ("y", "c"), axis=0)

    gain = jnp.broadcast_to(ln_gain[None, :], (GAIN_ROWS, feat))
    own = lax.all_gather(jnp.concatenate([tokens, gain], axis=0), "xl", axis=0)
    pieces = [own]
    ahead = behind = own
    for _ in range(3):
        ahead = lax.ppermute(ahead, "z", ring(8, 1))
        behind = lax.ppermute(behind, "z", ring(8, -1))
        pieces += [ahead, behind]
    pieces.append(lax.ppermute(ahead[:1], "z", ring(8, 1)))
    pieces.append(lax.ppermute(behind[1:], "z", ring(8, -1)))

    normed, stats = pl.pallas_call(
        lambda *refs: normalise_kernel(feat_all, *refs),
        out_shape=(
            jax.ShapeDtypeStruct((16, rows + GAIN_ROWS, feat), BF16),
            jax.ShapeDtypeStruct((2, rows, 128), F32),
        ),
        in_specs=[SMEM] + [VMEM] * len(pieces),
        out_specs=(VMEM, VMEM),
        compiler_params=params(32),
        name="normalise",
    )(z[None], *pieces)

    attended, grads, sums = pl.pallas_call(
        attention_kernel,
        out_shape=(
            jax.ShapeDtypeStruct((rows, width), BF16),
            jax.ShapeDtypeStruct((3, rows, width), BF16),
            jax.ShapeDtypeStruct((2, rows), F32),
        ),
        in_specs=[VMEM] * 4,
        out_specs=(VMEM,) * 3,
        scratch_shapes=[pltpu.VMEM((rows + GAIN_ROWS, 3 * width), F32)],
        compiler_params=params(40),
        name="attention",
    )(normed, weights, qk_gain, cotangent)

    partial = pl.pallas_call(
        backward_kernel,
        out_shape=jax.ShapeDtypeStruct((16, rows, feat), BF16),
        in_specs=[VMEM] * 2,
        out_specs=VMEM,
        compiler_params=params(40),
        name="backward",
    )(grads, weights)

    sums = lax.psum(sums, ("xl", "z"))
    reduced = lax.psum_scatter(partial.reshape(8, 2, rows, feat), "z", scatter_dimension=0, tiled=True)
    xl = lax.axis_index("xl")
    mine = lax.dynamic_index_in_dim(reduced[0], xl, 0, keepdims=False)
    other = lax.dynamic_index_in_dim(reduced[0], 1 - xl, 0, keepdims=False)
    other = lax.ppermute(other, "xl", ring(2, 1))
    grad_tokens = pl.pallas_call(
        lambda *refs: final_kernel(feat_all, *refs),
        out_shape=jax.ShapeDtypeStruct((rows, feat), BF16),
        in_specs=[VMEM] * 6,
        out_specs=VMEM,
        name="final_norm",
    )(mine, other, tokens, gain, stats, sums.T)
    return (attended, grad_tokens)


def solution(mesh):
    fine = Mesh(mesh.devices.reshape(2, 8, 2, 2, 8), ("xh", "y", "c", "xl", "z"))
    dp, mp = ("xh", "y", "c"), ("xl", "z")
    return jax.shard_map(
        per_device,
        mesh=fine,
        in_specs=(P(dp, mp), P(mp), P(None, dp, mp), P(), P(dp, mp)),
        out_specs=(P(dp, mp), P(dp, mp)),
        check_vma=False,
    )
```

time: 406 us -> 239 us (0.59)
  waiting for transfers between devices: 296 us -> 69.6 us
  blocking collectives: 38.9 us -> 83.3 us
  starting transfers between devices: 0.11 us -> 36.3 us
  matrix products: 29.4 us -> 0 us
  Pallas kernels: 0 us -> 19.9 us
  other arithmetic: 17.6 us -> 0.95 us
  local copies, waits for them, and re-layouts: 7.75 us -> 14.4 us
    psum x1 -> x0, waiting for transfers between devices: 150 us -> none  [per_device(): lax.psum(partial_sum.astype(jnp.bfloat16), 'mp').astype(jnp.float32)]
    all_gather x2 -> x1, waiting for transfers between devices: 145 us -> 0.01 us  [per_device(): weights = lax.all_gather(weights, ('y', 'c'), axis=0)]
    psum x0 -> x1, blocking collectives: none -> 63.3 us  [per_device(): sums = lax.psum(sums, ('xl', 'z'))]
    reduce_scatter x0 -> x1, waiting for transfers between devices: none -> 49.8 us  [per_device(): lax.psum_scatter(partial.reshape(8, 2, rows, feat), 'z', scatter_dimensio...]
    ppermute x0 -> x9, starting transfers between devices: none -> 36.2 us  [the longest x3 18.9 us: per_device(): behind = lax.ppermute(behind, 'z', ring(8, -1))]
    dot_general x8 -> x0, matrix products: 27.4 us -> none  [the longest x1 8.07 us: per_device(): jnp.einsum('itf,idf->td', grads, weights_full, preferred_element_type=f32)]
    pallas_call x0 -> x4, Pallas kernels: none -> 19.9 us  [the longest x1 8.54 us: per_device(): pl.pallas_call(attention_kernel, out_shape=(jax.ShapeDtypeStruct((rows, w...]
    ppermute x0 -> x9, waiting for transfers between devices: none -> 19.8 us  [the longest x3 16.2 us: per_device(): ahead = lax.ppermute(ahead, 'z', ring(8, 1))]
  transfers between devices with their start and end apart: 3 -> 11, of which waited for: 3 -> 6; matrix products, arithmetic and copies ran while one was open for 3% -> 1% of each run, Pallas kernels for 0% -> 1%
where the time goes in v1:
time: 239 us
  blocking collectives  83.3 us (35%)
  waiting for transfers between devices  69.6 us (29%)
  starting transfers between devices  36.3 us (15%)
  Pallas kernels  19.9 us (8%)
  local copies, waits for them, and re-layouts  14.4 us (6%)
  between operations  14.2 us (6%)
    psum x1, blocking collectives, per_device(): sums = lax.psum(sums, ('xl', 'z'))  63.3 us
    reduce_scatter x1, waiting for transfers between devices, per_device(): lax.psum_scatter(partial.reshape(8, 2, rows, feat), 'z', scatter_dimensio...  49.8 us
    ppermute x3, starting transfers between devices, per_device(): behind = lax.ppermute(behind, 'z', ring(8, -1))  18.9 us
    ppermute x3, waiting for transfers between devices, per_device(): ahead = lax.ppermute(ahead, 'z', ring(8, 1))  16.2 us
    all_gather x1, blocking collectives, per_device(): weights = lax.all_gather(weights, 'xh', axis=0)  12.6 us
    unnamed x20, local copies, waits for them, and re-layouts  10.4 us
    pallas_call x1, Pallas kernels, per_device(): pl.pallas_call(attention_kernel, out_shape=(jax.ShapeDtypeStruct((rows, w...  8.54 us
    ppermute x3, starting transfers between devices, per_device(): ahead = lax.ppermute(ahead, 'z', ring(8, 1))  7.67 us
  transfers between devices with their start and end apart: 11, of which 6 were waited for; matrix products, arithmetic and copies ran while one was open for 1% of the time, Pallas kernels for 1%

profile of v1, /device:TPU:6, one launch (start us, length us, event | category | flops | bytes accessed | tf_op | source)
XLA Modules:
  0.0 238.6 jit_solution(9625291566315259478)
XLA Ops:
  7.2 12.6 %all_gather.17 = bf16[2,576,256]{2,1,0:T(8,128)(2,1)} all-gather(bf16[1,576,256]{2,1,0:T(8,128)(2,1)} %bitcast.17), channel_id=1, replica_groups=mesh['xh'=2,'y'=8,'c'=2,'xl'=2,'z'=8] {'xh'}, dimensions={0}, use_global_device_ids=true | all-gather | bytes 884736 | tf_op jit(solution)/shard_map/all_gather | solution.py:177
  19.9 0.7 broadcast_in_dim.10.refs_3_
  20.6 1.0 pad_maximum_fusion
  21.6 7.4 %all-gather = bf16[544,384]{1,0:T(8,128)(2,1)S(1)} all-gather(bf16[272,384]{1,0:T(8,128)(2,1)S(1)} %pad_maximum_fusion), channel_id=2, replica_groups=mesh['xh'=2,'y'=8,'c'=2,'xl'=2,'z'=8] {'xl'}, dimensions={0}, use_global_device_ids=true | all-gather | bytes 626688 | tf_op jit(solution)/shard_map/all_gather | solution.py:181
  29.0 3.9 %collective-permute-start = (bf16[2,272,384]{2,1,0:T(8,128)(2,1)S(1)}, bf16[2,272,384]{2,1,0:T(8,128)(2,1)S(1)}, u32[]{:S(2)}, u32[]{:S(2)}) collective-permute-start(bf16[2,272,384]{2,1,0:T(8,128)(2,1)S(1)} %bitcast.13), channel_id=1, source_target_pairs={{0,1},{1,2},{2,3},{3,4},{4,5},{5,6},{6,7},{7,0},{8,9},{9,10},{10,1... | collective-permute-start | bytes 1253384 | tf_op jit(solution)/shard_map/ppermute | solution.py:185
  32.9 8.6 %collective-permute-start.1 = (bf16[2,272,384]{2,1,0:T(8,128)(2,1)S(1)}, bf16[2,272,384]{2,1,0:T(8,128)(2,1)S(1)}, u32[]{:S(2)}, u32[]{:S(2)}) collective-permute-start(bf16[2,272,384]{2,1,0:T(8,128)(2,1)S(1)} %bitcast.14), channel_id=1, source_target_pairs={{0,7},{1,0},{2,1},{3,2},{4,3},{5,4},{6,5},{7,6},{8,15},{9,8},{10,9... | collective-permute-start | bytes 1253384 | tf_op jit(solution)/shard_map/ppermute | solution.py:186
  41.5 6.2 %collective-permute-done.refs_2_ = bf16[2,272,384]{2,1,0:T(8,128)(2,1)S(1)} collective-permute-done((bf16[2,272,384]{2,1,0:T(8,128)(2,1)S(1)}, bf16[2,272,384]{2,1,0:T(8,128)(2,1)S(1)}, u32[]{:S(2)}, u32[]{:S(2)}) %collective-permute-start) | collective-permute-done | bytes 417824 | tf_op jit(solution)/shard_map/ppermute | solution.py:185
  47.7 1.9 collective-permute-start.2
  49.6 5.1 %collective-permute-start.3 = (bf16[2,272,384]{2,1,0:T(8,128)(2,1)S(1)}, bf16[2,272,384]{2,1,0:T(8,128)(2,1)S(1)}, u32[]{:S(2)}, u32[]{:S(2)}) collective-permute-start(bf16[2,272,384]{2,1,0:T(8,128)(2,1)S(1)} %collective-permute-done.1.refs_3_), channel_id=1, source_target_pairs={{0,7},{1,0},{2,1},{3,2},{4,3},{5,4},{6,5},{7,6},{8,15},{9,8},{10,9... | collective-permute-start | bytes 1253384 | tf_op jit(solution)/shard_map/ppermute | solution.py:186
  54.7 5.4 %collective-permute-done.2.refs_4_ = bf16[2,272,384]{2,1,0:T(8,128)(2,1)S(1)} collective-permute-done((bf16[2,272,384]{2,1,0:T(8,128)(2,1)S(1)}, bf16[2,272,384]{2,1,0:T(8,128)(2,1)S(1)}, u32[]{:S(2)}, u32[]{:S(2)}) %collective-permute-start.2) | collective-permute-done | bytes 417824 | tf_op jit(solution)/shard_map/ppermute | solution.py:185
  60.1 1.9 collective-permute-start.4
  62.1 5.1 %collective-permute-start.5 = (bf16[2,272,384]{2,1,0:T(8,128)(2,1)S(1)}, bf16[2,272,384]{2,1,0:T(8,128)(2,1)S(1)}, u32[]{:S(2)}, u32[]{:S(2)}) collective-permute-start(bf16[2,272,384]{2,1,0:T(8,128)(2,1)S(1)} %collective-permute-done.3.refs_5_), channel_id=1, source_target_pairs={{0,7},{1,0},{2,1},{3,2},{4,3},{5,4},{6,5},{7,6},{8,15},{9,8},{10,9... | collective-permute-start | bytes 1253384 | tf_op jit(solution)/shard_map/ppermute | solution.py:186
  67.2 4.6 %collective-permute-done.4.refs_6_ = bf16[2,272,384]{2,1,0:T(8,128)(2,1)S(1)} collective-permute-done((bf16[2,272,384]{2,1,0:T(8,128)(2,1)S(1)}, bf16[2,272,384]{2,1,0:T(8,128)(2,1)S(1)}, u32[]{:S(2)}, u32[]{:S(2)}) %collective-permute-start.4) | collective-permute-done | bytes 417824 | tf_op jit(solution)/shard_map/ppermute | solution.py:185
  71.8 0.7 slice.8
  72.5 1.9 collective-permute-start.6
  74.4 0.7 slice.9
  75.1 5.1 %collective-permute-start.7 = (bf16[1,272,384]{2,1,0:T(8,128)(2,1)}, bf16[1,272,384]{2,1,0:T(8,128)(2,1)S(1)}, u32[]{:S(2)}, u32[]{:S(2)}) collective-permute-start(bf16[1,272,384]{2,1,0:T(8,128)(2,1)} %slice.9), channel_id=1, source_target_pairs={{0,7},{1,0},{2,1},{3,2},{4,3},{5,4},{6,5},{7,6},{8,15},{9,8},{10,9... | collective-permute-start | bytes 626696 | tf_op jit(solution)/shard_map/ppermute | solution.py:189
  80.3 1.3 collective-permute-done.6.refs_8_
  81.6 2.3 collective-permute-done.7.refs_9_
  83.9 2.8 %normalise.1 = (bf16[16,272,384]{2,1,0:T(8,128)(2,1)S(1)}, f32[2,256,128]{2,1,0:T(8,128)S(1)}) custom-call(s32[1]{0:T(128)} %bitcast.refs_0_, bf16[2,272,384]{2,1,0:T(8,128)(2,1)S(1)} %bitcast.15, bf16[2,272,384]{2,1,0:T(8,128)(2,1)S(1)} %collective-permute-done.refs_2_, bf16[2,272,384]{2,1,0:T(8,128)(2,1)S(1)} %collective-permute-done.1.refs_3_, ...), custom_call_target="tpu_custom_call" | custom-call | tf_op jit(solution)/shard_map/normalise/pallas_call | solution.py:191
  86.7 1.7 copy-done.3
  88.5 0.7 copy-done.5
  89.2 3.7 %copy-done = bf16[32,576,256]{2,1,0:T(8,128)(2,1)S(1)} copy-done((bf16[32,576,256]{2,1,0:T(8,128)(2,1)S(1)}, bf16[32,576,256]{2,1,0:T(8,128)(2,1)}, u32[]{:S(2)}) %copy-start) | copy-done | bytes 9437208
  92.9 1.9 copy-done.4
  94.8 8.5 %attention.1 = (bf16[256,256]{1,0:T(8,128)(2,1)}, bf16[3,256,256]{2,1,0:T(8,128)(2,1)S(1)}, f32[2,256]{1,0:T(2,128)S(1)}) custom-call(bf16[16,272,384]{2,1,0:T(8,128)(2,1)S(1)} %copy-done.4, bf16[16,2,576,256]{3,2,1,0:T(8,128)(2,1)S(1)} %bitcast.10, f32[2,128]{1,0:T(2,128)S(1)} %copy-done.7, bf16[256,256]{1,0:T(8,128)(2,1)S(1)} %copy-done.6), custom_call_target="tpu_custom_call" | custom-call | tf_op jit(solution)/shard_map/attention/pallas_call | solution.py:203
  103.3 6.3 %backward.1 = bf16[16,256,384]{2,1,0:T(8,128)(2,1)S(1)} custom-call(bf16[3,256,256]{2,1,0:T(8,128)(2,1)S(1)} %get-tuple-element.9.grads_ref, bf16[16,2,576,256]{3,2,1,0:T(8,128)(2,1)S(1)} %bitcast.11), custom_call_target="tpu_custom_call" | custom-call | tf_op jit(solution)/shard_map/backward/pallas_call | solution.py:217
  109.6 1.6 copy-done.2
  111.3 49.8 %reduce-scatter.2.cloned.1.call-done = bf16[1,2,256,384]{3,2,1,0:T(8,128)(2,1)} async-done(((bf16[8,2,256,384]{3,2,1,0:T(8,128)(2,1)}), bf16[1,2,256,384]{3,2,1,0:T(8,128)(2,1)}) %reduce-scatter.2.cloned.1.call-update) | async-done | bytes 393232 | tf_op jit(solution)/shard_map/reduce_scatter | solution.py:227
  161.1 1.7 dynamic-slice_bitcast_fusion
  162.8 2.6 %collective-permute-start.8 = (bf16[256,384]{1,0:T(8,128)(2,1)S(1)}, bf16[256,384]{1,0:T(8,128)(2,1)S(1)}, u32[]{:S(2)}, u32[]{:S(2)}) collective-permute-start(bf16[256,384]{1,0:T(8,128)(2,1)S(1)} %get-tuple-element.12), channel_id=1, source_target_pairs={{0,8},{8,0},{1,9},{9,1},{2,10},{10,2},{3,11},{11,3},{4,12},{12,4},... | collective-permute-start | bytes 589832 | tf_op jit(solution)/shard_map/ppermute | solution.py:231
  165.6 63.3 %psum.7.refs_5_ = f32[256,2]{1,0:T(8,128)} all-reduce(f32[256,2]{1,0:T(8,128)S(1)} %bitcast.16), channel_id=1, replica_groups=mesh['xh'=2,'y'=8,'c'=2,'xl'=2,'z'=8] {'xl','z'}, use_global_device_ids=true, to_apply=%region_1.0 | all-reduce | flops 512 | bytes 4096 | tf_op jit(solution)/shard_map/psum | solution.py:226
  229.6 2.2 final_norm.1
  (25 shorter events, 1.0 us)
Async XLA Ops:
  7.2 82.0 %all-gather.4.cloned.1.call-start = ((), (), s32[]{:S(2)}) async-start(), calls=%async_computation.2 | async-start | bytes 10027008 | tf_op jit(solution)/shard_map/all_gather | solution.py:178
  7.2 82.0 %copy-start.6 = (bf16[256,256]{1,0:T(8,128)(2,1)S(1)}, bf16[256,256]{1,0:T(8,128)(2,1)}, u32[]{:S(2)}) copy-start(bf16[256,256]{1,0:T(8,128)(2,1)} %cot_ref.1) | copy-start | bytes 393220
  7.2 82.0 %copy-start.7 = (f32[2,128]{1,0:T(2,128)S(1)}, f32[2,128]{1,0:T(2,128)}, u32[]{:S(2)}) copy-start(f32[2,128]{1,0:T(2,128)} %qk_ref.1) | copy-start | bytes 3076
  19.9 141.2 %reduce-scatter.2.cloned.1.call-start = ((), (), s32[]{:S(2)}) async-start(), calls=%async_computation.1 | async-start | bytes 3538944 | tf_op jit(solution)/shard_map/reduce_scatter | solution.py:227
  20.6 82.7 %copy-start.9 = (bf16[16,384]{1,0:T(8,128)(2,1)}, bf16[16,384]{1,0:T(8,128)(2,1)S(1)}, u32[]{:S(2)}) copy-start(bf16[16,384]{1,0:T(8,128)(2,1)S(1)} %broadcast_in_dim.10.refs_3_) | copy-start | bytes 36868
  29.0 18.7 %collective-permute-start = (bf16[2,272,384]{2,1,0:T(8,128)(2,1)S(1)}, bf16[2,272,384]{2,1,0:T(8,128)(2,1)S(1)}, u32[]{:S(2)}, u32[]{:S(2)}) collective-permute-start(bf16[2,272,384]{2,1,0:T(8,128)(2,1)S(1)} %bitcast.13), channel_id=1, source_target_pairs={{0,1},{1,2},{2,3},{3,4},{4,5},{5,6},{6,7},{7,0},{8,9},{9,10},{10,1... | collective-permute-start | bytes 1253384 | tf_op jit(solution)/shard_map/ppermute | solution.py:185
  32.9 16.7 %collective-permute-start.1 = (bf16[2,272,384]{2,1,0:T(8,128)(2,1)S(1)}, bf16[2,272,384]{2,1,0:T(8,128)(2,1)S(1)}, u32[]{:S(2)}, u32[]{:S(2)}) collective-permute-start(bf16[2,272,384]{2,1,0:T(8,128)(2,1)S(1)} %bitcast.14), channel_id=1, source_target_pairs={{0,7},{1,0},{2,1},{3,2},{4,3},{5,4},{6,5},{7,6},{8,15},{9,8},{10,9... | collective-permute-start | bytes 1253384 | tf_op jit(solution)/shard_map/ppermute | solution.py:186
  47.7 12.5 %collective-permute-start.2 = (bf16[2,272,384]{2,1,0:T(8,128)(2,1)S(1)}, bf16[2,272,384]{2,1,0:T(8,128)(2,1)S(1)}, u32[]{:S(2)}, u32[]{:S(2)}) collective-permute-start(bf16[2,272,384]{2,1,0:T(8,128)(2,1)S(1)} %collective-permute-done.refs_2_), channel_id=1, source_target_pairs={{0,1},{1,2},{2,3},{3,4},{4,5},{5,6},{6,7},{7,0},{8,9},{9,10},{10,1... | collective-permute-start | bytes 1253384 | tf_op jit(solution)/shard_map/ppermute | solution.py:185
  49.6 12.5 %collective-permute-start.3 = (bf16[2,272,384]{2,1,0:T(8,128)(2,1)S(1)}, bf16[2,272,384]{2,1,0:T(8,128)(2,1)S(1)}, u32[]{:S(2)}, u32[]{:S(2)}) collective-permute-start(bf16[2,272,384]{2,1,0:T(8,128)(2,1)S(1)} %collective-permute-done.1.refs_3_), channel_id=1, source_target_pairs={{0,7},{1,0},{2,1},{3,2},{4,3},{5,4},{6,5},{7,6},{8,15},{9,8},{10,9... | collective-permute-start | bytes 1253384 | tf_op jit(solution)/shard_map/ppermute | solution.py:186
  60.1 11.6 %collective-permute-start.4 = (bf16[2,272,384]{2,1,0:T(8,128)(2,1)S(1)}, bf16[2,272,384]{2,1,0:T(8,128)(2,1)S(1)}, u32[]{:S(2)}, u32[]{:S(2)}) collective-permute-start(bf16[2,272,384]{2,1,0:T(8,128)(2,1)S(1)} %collective-permute-done.2.refs_4_), channel_id=1, source_target_pairs={{0,1},{1,2},{2,3},{3,4},{4,5},{5,6},{6,7},{7,0},{8,9},{9,10},{10,1... | collective-permute-start | bytes 1253384 | tf_op jit(solution)/shard_map/ppermute | solution.py:185
  62.1 12.3 %collective-permute-start.5 = (bf16[2,272,384]{2,1,0:T(8,128)(2,1)S(1)}, bf16[2,272,384]{2,1,0:T(8,128)(2,1)S(1)}, u32[]{:S(2)}, u32[]{:S(2)}) collective-permute-start(bf16[2,272,384]{2,1,0:T(8,128)(2,1)S(1)} %collective-permute-done.3.refs_5_), channel_id=1, source_target_pairs={{0,7},{1,0},{2,1},{3,2},{4,3},{5,4},{6,5},{7,6},{8,15},{9,8},{10,9... | collective-permute-start | bytes 1253384 | tf_op jit(solution)/shard_map/ppermute | solution.py:186
  72.5 9.1 %collective-permute-start.6 = (bf16[1,272,384]{2,1,0:T(8,128)(2,1)}, bf16[1,272,384]{2,1,0:T(8,128)(2,1)S(1)}, u32[]{:S(2)}, u32[]{:S(2)}) collective-permute-start(bf16[1,272,384]{2,1,0:T(8,128)(2,1)} %slice.8), channel_id=1, source_target_pairs={{0,1},{1,2},{2,3},{3,4},{4,5},{5,6},{6,7},{7,0},{8,9},{9,10},{10,1... | collective-permute-start | bytes 626696 | tf_op jit(solution)/shard_map/ppermute | solution.py:188
  75.1 8.7 %collective-permute-start.7 = (bf16[1,272,384]{2,1,0:T(8,128)(2,1)}, bf16[1,272,384]{2,1,0:T(8,128)(2,1)S(1)}, u32[]{:S(2)}, u32[]{:S(2)}) collective-permute-start(bf16[1,272,384]{2,1,0:T(8,128)(2,1)} %slice.9), channel_id=1, source_target_pairs={{0,7},{1,0},{2,1},{3,2},{4,3},{5,4},{6,5},{7,6},{8,15},{9,8},{10,9... | collective-permute-start | bytes 626696 | tf_op jit(solution)/shard_map/ppermute | solution.py:189
  86.7 1.7 copy-start.3
  88.5 0.7 copy-start.5
  89.2 3.7 %copy-start = (bf16[32,576,256]{2,1,0:T(8,128)(2,1)S(1)}, bf16[32,576,256]{2,1,0:T(8,128)(2,1)}, u32[]{:S(2)}) copy-start(bf16[32,576,256]{2,1,0:T(8,128)(2,1)} %all-gather.4.cloned.1.call-done) | copy-start | bytes 28311556
  92.9 1.9 copy-start.4
  94.8 8.5 %copy-start.1 = (bf16[32,576,256]{2,1,0:T(8,128)(2,1)S(1)}, bf16[32,576,256]{2,1,0:T(8,128)(2,1)}, u32[]{:S(2)}) copy-start(bf16[32,576,256]{2,1,0:T(8,128)(2,1)} %all-gather.4.cloned.1.call-done) | copy-start | bytes 28311556
  109.6 1.6 copy-start.2
  162.8 66.1 %collective-permute-start.8 = (bf16[256,384]{1,0:T(8,128)(2,1)S(1)}, bf16[256,384]{1,0:T(8,128)(2,1)S(1)}, u32[]{:S(2)}, u32[]{:S(2)}) collective-permute-start(bf16[256,384]{1,0:T(8,128)(2,1)S(1)} %get-tuple-element.12), channel_id=1, source_target_pairs={{0,8},{8,0},{1,9},{9,1},{2,10},{10,2},{3,11},{11,3},{4,12},{12,4},... | collective-permute-start | bytes 589832 | tf_op jit(solution)/shard_map/ppermute | solution.py:231
  228.9 0.7 copy-start.8
Sparse Core Ops, SparseCore 0:
  20.0 67.4 all-gather.3
  111.4 49.6 reduce-scatter.1

commit v2 on v1

--- a/solution.py
+++ b/solution.py
@@ -78,7 +78,7 @@
     return inv * (grad_hat - first - x_hat * second)
 
 
-def attention_kernel(normed_ref, w_ref, qk_ref, cot_ref, out_ref, grads_ref, stat_ref, acc):
+def attention_kernel(normed_ref, w_ref, qk_ref, cot_ref, out_ref, grads_ref, sums_ref, acc):
     n_m = normed_ref.shape[0]
     third = w_ref.shape[2] // 3
     width = w_ref.shape[3]
@@ -130,36 +130,78 @@
             wide = grad.astype(F32)
             first = first + wide * acc[rows : rows + 1, cols[i]]
             second = second + wide * proj[i]
-    stat_ref[0:1, :] = jnp.sum(first, axis=1)[None, :]
-    stat_ref[1:2, :] = jnp.sum(second, axis=1)[None, :]
-
-
-def backward_kernel(grads_ref, w_ref, out_ref):
+    sums_ref[...] = jnp.zeros_like(sums_ref)
+    sums_ref[0:1, :rows] = jnp.sum(first, axis=1)[None, :]
+    sums_ref[1:2, :rows] = jnp.sum(second, axis=1)[None, :]
+
+
+def split_sums(sums):
+    high = sums.astype(BF16).astype(F32)
+    return jnp.concatenate([high, sums - high], axis=0).astype(BF16)
+
+
+def join_sums(rows):
+    wide = rows.astype(F32)
+    return wide[:8] + wide[8:]
+
+
+def backward_kernel(plan, z_ref, grads_ref, w_ref, sums_ref, *out_refs):
     third = w_ref.shape[2] // 3
-
-    def step(m, carry):
-        xh = m // 8
-        y = lax.rem(m, 8)
-        total = None
-        for i in range(3):
-            w = jnp.concatenate(
-                [w_ref[2 * y + c, xh, i * third : (i + 1) * third, :] for c in range(2)], axis=0
+    rows = PATCH
+    tail = split_sums(sums_ref[...])
+    for out_ref, places in zip(out_refs, plan):
+        for at, (xl, offset) in enumerate(places):
+            y = lax.rem(z_ref[0] + offset, 8)
+            total = None
+            for i in range(3):
+                w = jnp.concatenate(
+                    [w_ref[2 * y + c, xl, i * third : (i + 1) * third, :] for c in range(2)], axis=0
+                )
+                term = dot(grads_ref[i], w, 1, 1)
+                total = term if total is None else total + term
+            out_ref[at, :rows, :] = total.astype(BF16)
+            out_ref[at, rows:, :] = tail
+
+
+def add_kernel(first, got_ref, part_ref, out_ref):
+    rows = PATCH
+    for at in range(part_ref.shape[0]):
+        if first <= at < first + got_ref.shape[0]:
+            got = at - first
+            out_ref[at, :rows, :] = (
+                got_ref[got, :rows, :].astype(F32) + part_ref[at, :rows, :].astype(F32)
+            ).astype(BF16)
+            out_ref[at, rows:, :] = split_sums(
+                join_sums(got_ref[got, rows:, :]) + join_sums(part_ref[at, rows:, :])
             )
-            term = dot(grads_ref[i], w, 1, 1)
-            total = term if total is None else total + term
-        out_ref[2 * y + xh] = total.astype(BF16)
-        return carry
-
-    lax.fori_loop(0, out_ref.shape[0], step, 0)
-
-
-def final_kernel(feat_all, mine_ref, other_ref, tok_ref, gain_ref, stat_ref, sums_ref, out_ref):
-    b = (mine_ref[...].astype(F32) + other_ref[...].astype(F32)) * gain_ref[0:1, :].astype(F32)
+        else:
+            out_ref[at] = part_ref[at]
+
+
+def join_kernel(xl_ref, ahead_ref, behind_ref, own_ref, mine_ref, other_ref):
+    rows = PATCH
+    for ref, at in ((mine_ref, xl_ref[0]), (other_ref, 1 - xl_ref[0])):
+        refs = (ahead_ref, behind_ref, own_ref)
+        total = sum(r[at, :rows, :].astype(F32) for r in refs)
+        ref[:rows, :] = total.astype(BF16)
+        ref[rows:, :] = split_sums(sum(join_sums(r[at, rows:, :]) for r in refs))
+
+
+def final_kernel(feat_all, mine_ref, other_ref, tok_ref, gain_ref, stat_ref, out_ref):
+    rows = PATCH
+    b = mine_ref[:rows, :].astype(F32) + other_ref[:rows, :].astype(F32)
+    b = b * gain_ref[0:1, :].astype(F32)
+    sums = join_sums(mine_ref[rows:, :]) + join_sums(other_ref[rows:, :])
+    diagonal = lax.broadcasted_iota(jnp.int32, (rows, rows), 0) == lax.broadcasted_iota(
+        jnp.int32, (rows, rows), 1
+    )
+    first, second = (
+        jnp.sum(jnp.where(diagonal, sums[i : i + 1, :rows], 0.0), axis=1, keepdims=True) / feat_all
+        for i in range(2)
+    )
     mean = stat_ref[0, :, 0:1]
     inv = stat_ref[1, :, 0:1]
     x_hat = (tok_ref[...].astype(F32) - mean) * inv
-    first = sums_ref[:, 0:1] / feat_all
-    second = sums_ref[:, 1:2] / feat_all
     out_ref[...] = (inv * (b - first - x_hat * second)).astype(BF16)
 
 
@@ -205,7 +247,7 @@
         out_shape=(
             jax.ShapeDtypeStruct((rows, width), BF16),
             jax.ShapeDtypeStruct((3, rows, width), BF16),
-            jax.ShapeDtypeStruct((2, rows), F32),
+            jax.ShapeDtypeStruct((8, feat), F32),
         ),
         in_specs=[VMEM] * 4,
         out_specs=(VMEM,) * 3,
@@ -214,28 +256,55 @@
         name="attention",
     )(normed, weights, qk_gain, cotangent)
 
-    partial = pl.pallas_call(
-        backward_kernel,
-        out_shape=jax.ShapeDtypeStruct((16, rows, feat), BF16),
-        in_specs=[VMEM] * 2,
-        out_specs=VMEM,
-        compiler_params=params(40),
-        name="backward",
-    )(grads, weights)
-
-    sums = lax.psum(sums, ("xl", "z"))
-    reduced = lax.psum_scatter(partial.reshape(8, 2, rows, feat), "z", scatter_dimension=0, tiled=True)
-    xl = lax.axis_index("xl")
-    mine = lax.dynamic_index_in_dim(reduced[0], xl, 0, keepdims=False)
-    other = lax.dynamic_index_in_dim(reduced[0], 1 - xl, 0, keepdims=False)
+    block = (rows + GAIN_ROWS, feat)
+
+    def backward(plan, name):
+        flops = 2 * rows * feat * 3 * width * sum(len(places) for places in plan)
+        return pl.pallas_call(
+            lambda *refs: backward_kernel(plan, *refs),
+            out_shape=tuple(jax.ShapeDtypeStruct((len(p),) + block, BF16) for p in plan),
+            in_specs=[SMEM] + [VMEM] * 3,
+            out_specs=(VMEM,) * len(plan),
+            compiler_params=params(32),
+            cost_estimate=pl.CostEstimate(flops=flops, bytes_accessed=2 * 2**20, transcendentals=0),
+            name=name,
+        )(z[None], grads, weights, sums)
+
+    def add(got, part, first, name):
+        return pl.pallas_call(
+            lambda *refs: add_kernel(first, *refs),
+            out_shape=jax.ShapeDtypeStruct(part.shape, BF16),
+            in_specs=[VMEM] * 2,
+            out_specs=VMEM,
+            cost_estimate=pl.CostEstimate(flops=10**6, bytes_accessed=2**20, transcendentals=0),
+            name=name,
+        )(got, part)
+
+    ahead, behind = backward((((0, 4),), ((1, 4),)), "backward_far")
+    near = [((0, off), (1, off)) for off in (3, 5, 2, 6, 1, 7, 0)]
+    parts = backward(tuple(near), "backward_near")
+    for step in range(3):
+        ahead = lax.ppermute(ahead, "z", ring(8, 1))
+        behind = lax.ppermute(behind, "z", ring(8, -1))
+        ahead = add(ahead, parts[2 * step], 0, "add_ahead")
+        behind = add(behind, parts[2 * step + 1], 1 if step == 0 else 0, "add_behind")
+    ahead = lax.ppermute(ahead, "z", ring(8, 1))
+    behind = lax.ppermute(behind, "z", ring(8, -1))
+    mine, other = pl.pallas_call(
+        join_kernel,
+        out_shape=(jax.ShapeDtypeStruct(block, BF16),) * 2,
+        in_specs=[SMEM] + [VMEM] * 3,
+        out_specs=(VMEM, VMEM),
+        name="join",
+    )(lax.axis_index("xl").astype(jnp.int32)[None], ahead, behind, parts[6])
     other = lax.ppermute(other, "xl", ring(2, 1))
     grad_tokens = pl.pallas_call(
         lambda *refs: final_kernel(feat_all, *refs),
         out_shape=jax.ShapeDtypeStruct((rows, feat), BF16),
-        in_specs=[VMEM] * 6,
+        in_specs=[VMEM] * 5,
         out_specs=VMEM,
         name="final_norm",
-    )(mine, other, tokens, gain, stats, sums.T)
+    )(mine, other, tokens, gain, stats)
     return (attended, grad_tokens)
 
 

time: 239 us -> 198 us (0.83)
  blocking collectives: 83.3 us -> 19.9 us
  starting transfers between devices: 36.3 us -> 64.1 us
  waiting for transfers between devices: 69.6 us -> 44.4 us
  Pallas kernels: 19.9 us -> 31.2 us
  local copies, waits for them, and re-layouts: 14.4 us -> 22.2 us
    psum x1 -> x0, blocking collectives: 63.3 us -> none  [per_device(): sums = lax.psum(sums, ('xl', 'z'))]
    reduce_scatter x1 -> x0, waiting for transfers between devices: 49.8 us -> none  [per_device(): lax.psum_scatter(partial.reshape(8, 2, rows, feat), 'z', scatter_dimensio...]
    ppermute x3 -> x7, waiting for transfers between devices: 0.01 us -> 23.9 us  [per_device(): behind = lax.ppermute(behind, 'z', ring(8, -1))]
    ppermute x3 -> x7, starting transfers between devices: 18.9 us -> 38.3 us  [per_device(): behind = lax.ppermute(behind, 'z', ring(8, -1))]
    pallas_call x1 -> x9, Pallas kernels: 6.26 us -> 17.6 us  [the longest x6 11.9 us: add(): pl.pallas_call(lambda *refs: add_kernel(first, *refs), out_shape=jax.Shap...]
    unnamed x20 -> x52, local copies, waits for them, and re-layouts: 10.4 us -> 20.8 us
    ppermute x3 -> x7, waiting for transfers between devices: 16.2 us -> 7.97 us  [per_device(): ahead = lax.ppermute(ahead, 'z', ring(8, 1))]
    ppermute x3 -> x7, starting transfers between devices: 7.67 us -> 15.8 us  [per_device(): ahead = lax.ppermute(ahead, 'z', ring(8, 1))]
  transfers between devices with their start and end apart: 11 -> 18, of which waited for: 6 -> 10; matrix products, arithmetic and copies ran while one was open for 1% -> 1% of each run, Pallas kernels for 1% -> 9%
where the time goes in v2:
time: 198 us; the launch traced here: 197 us
  starting transfers between devices  64.1 us (32%)
  waiting for transfers between devices  44.4 us (22%)
  Pallas kernels  31.2 us (16%)
  local copies, waits for them, and re-layouts  22.2 us (11%)
  blocking collectives  19.9 us (10%)
  between operations  14.4 us (7%)
    ppermute x7, starting transfers between devices, per_device(): behind = lax.ppermute(behind, 'z', ring(8, -1))  38.3 us
    ppermute x7, waiting for transfers between devices, per_device(): behind = lax.ppermute(behind, 'z', ring(8, -1))  23.9 us
    unnamed x52, local copies, waits for them, and re-layouts  20.8 us
    ppermute x7, starting transfers between devices, per_device(): ahead = lax.ppermute(ahead, 'z', ring(8, 1))  15.8 us
    all_gather x1, blocking collectives, per_device(): weights = lax.all_gather(weights, 'xh', axis=0)  12.5 us
    pallas_call x6, Pallas kernels, add(): pl.pallas_call(lambda *refs: add_kernel(first, *refs), out_shape=jax.Shap...  11.9 us
    pallas_call x1, Pallas kernels, per_device(): pl.pallas_call(attention_kernel, out_shape=(jax.ShapeDtypeStruct((rows, w...  8.5 us
    ppermute x7, waiting for transfers between devices, per_device(): ahead = lax.ppermute(ahead, 'z', ring(8, 1))  7.97 us
  transfers between devices with their start and end apart: 18, of which 10 were waited for; matrix products, arithmetic and copies ran while one was open for 1% of the time, Pallas kernels for 9%

profile of v2, /device:TPU:6, one launch (start us, length us, event | category | flops | bytes accessed | tf_op | source)
XLA Modules:
  0.0 197.2 jit_solution(10785931181504998852)
XLA Ops:
  7.2 12.5 %all_gather.17 = bf16[2,576,256]{2,1,0:T(8,128)(2,1)} all-gather(bf16[1,576,256]{2,1,0:T(8,128)(2,1)} %bitcast.13), channel_id=1, replica_groups=mesh['xh'=2,'y'=8,'c'=2,'xl'=2,'z'=8] {'xh'}, dimensions={0}, use_global_device_ids=true | all-gather | bytes 884736 | tf_op jit(solution)/shard_map/all_gather | solution.py:219
  21.3 7.4 %all-gather = bf16[544,384]{1,0:T(8,128)(2,1)S(1)} all-gather(bf16[272,384]{1,0:T(8,128)(2,1)S(1)} %pad_maximum_fusion), channel_id=2, replica_groups=mesh['xh'=2,'y'=8,'c'=2,'xl'=2,'z'=8] {'xl'}, dimensions={0}, use_global_device_ids=true | all-gather | bytes 626688 | tf_op jit(solution)/shard_map/all_gather | solution.py:223
  28.8 10.5 %collective-permute-start.1 = (bf16[2,272,384]{2,1,0:T(8,128)(2,1)S(1)}, bf16[2,272,384]{2,1,0:T(8,128)(2,1)S(1)}, u32[]{:S(2)}, u32[]{:S(2)}) collective-permute-start(bf16[2,272,384]{2,1,0:T(8,128)(2,1)S(1)} %bitcast.10), channel_id=1, source_target_pairs={{0,7},{1,0},{2,1},{3,2},{4,3},{5,4},{6,5},{7,6},{8,15},{9,8},{10,9... | collective-permute-start | bytes 1253384 | tf_op jit(solution)/shard_map/ppermute | solution.py:228
  41.2 5.5 %collective-permute-done.1.refs_3_ = bf16[2,272,384]{2,1,0:T(8,128)(2,1)S(1)} collective-permute-done((bf16[2,272,384]{2,1,0:T(8,128)(2,1)S(1)}, bf16[2,272,384]{2,1,0:T(8,128)(2,1)S(1)}, u32[]{:S(2)}, u32[]{:S(2)}) %collective-permute-start.1) | collective-permute-done | bytes 417824 | tf_op jit(solution)/shard_map/ppermute | solution.py:228
  46.7 5.6 %collective-permute-start.3 = (bf16[2,272,384]{2,1,0:T(8,128)(2,1)S(1)}, bf16[2,272,384]{2,1,0:T(8,128)(2,1)S(1)}, u32[]{:S(2)}, u32[]{:S(2)}) collective-permute-start(bf16[2,272,384]{2,1,0:T(8,128)(2,1)S(1)} %collective-permute-done.1.refs_3_), channel_id=1, source_target_pairs={{0,7},{1,0},{2,1},{3,2},{4,3},{5,4},{6,5},{7,6},{8,15},{9,8},{10,9... | collective-permute-start | bytes 1253384 | tf_op jit(solution)/shard_map/ppermute | solution.py:228
  54.3 4.6 %collective-permute-done.3.refs_5_ = bf16[2,272,384]{2,1,0:T(8,128)(2,1)S(1)} collective-permute-done((bf16[2,272,384]{2,1,0:T(8,128)(2,1)S(1)}, bf16[2,272,384]{2,1,0:T(8,128)(2,1)S(1)}, u32[]{:S(2)}, u32[]{:S(2)}) %collective-permute-start.3) | collective-permute-done | bytes 417824 | tf_op jit(solution)/shard_map/ppermute | solution.py:228
  58.9 5.6 %collective-permute-start.5 = (bf16[2,272,384]{2,1,0:T(8,128)(2,1)S(1)}, bf16[2,272,384]{2,1,0:T(8,128)(2,1)S(1)}, u32[]{:S(2)}, u32[]{:S(2)}) collective-permute-start(bf16[2,272,384]{2,1,0:T(8,128)(2,1)S(1)} %collective-permute-done.3.refs_5_), channel_id=1, source_target_pairs={{0,7},{1,0},{2,1},{3,2},{4,3},{5,4},{6,5},{7,6},{8,15},{9,8},{10,9... | collective-permute-start | bytes 1253384 | tf_op jit(solution)/shard_map/ppermute | solution.py:228
  66.4 3.8 %collective-permute-done.5.refs_7_ = bf16[2,272,384]{2,1,0:T(8,128)(2,1)S(1)} collective-permute-done((bf16[2,272,384]{2,1,0:T(8,128)(2,1)S(1)}, bf16[2,272,384]{2,1,0:T(8,128)(2,1)S(1)}, u32[]{:S(2)}, u32[]{:S(2)}) %collective-permute-start.5) | collective-permute-done | bytes 417824 | tf_op jit(solution)/shard_map/ppermute | solution.py:228
  70.3 5.6 %collective-permute-start.7 = (bf16[1,272,384]{2,1,0:T(8,128)(2,1)S(1)}, bf16[1,272,384]{2,1,0:T(8,128)(2,1)S(1)}, u32[]{:S(2)}, u32[]{:S(2)}) collective-permute-start(bf16[1,272,384]{2,1,0:T(8,128)(2,1)S(1)} %slice.9), channel_id=1, source_target_pairs={{0,7},{1,0},{2,1},{3,2},{4,3},{5,4},{6,5},{7,6},{8,15},{9,8},{10,9... | collective-permute-start | bytes 626696 | tf_op jit(solution)/shard_map/ppermute | solution.py:231
  79.2 6.5 %collective-permute-done.6.refs_8_ = bf16[1,272,384]{2,1,0:T(8,128)(2,1)S(1)} collective-permute-done((bf16[1,272,384]{2,1,0:T(8,128)(2,1)}, bf16[1,272,384]{2,1,0:T(8,128)(2,1)S(1)}, u32[]{:S(2)}, u32[]{:S(2)}) %collective-permute-start.6) | collective-permute-done | bytes 208928 | tf_op jit(solution)/shard_map/ppermute | solution.py:230
  85.7 2.9 %normalise.1 = (bf16[16,272,384]{2,1,0:T(8,128)(2,1)S(1)}, f32[2,256,128]{2,1,0:T(8,128)S(1)}) custom-call(s32[1]{0:T(128)} %bitcast.refs_0_, bf16[2,272,384]{2,1,0:T(8,128)(2,1)S(1)} %bitcast.12, bf16[2,272,384]{2,1,0:T(8,128)(2,1)S(1)} %collective-permute-done.refs_2_, bf16[2,272,384]{2,1,0:T(8,128)(2,1)S(1)} %collective-permute-done.1.refs_3_, ...), custom_call_target="tpu_custom_call" | custom-call | tf_op jit(solution)/shard_map/normalise/pallas_call | solution.py:233
  91.1 3.7 %copy-done = bf16[32,576,256]{2,1,0:T(8,128)(2,1)S(1)} copy-done((bf16[32,576,256]{2,1,0:T(8,128)(2,1)S(1)}, bf16[32,576,256]{2,1,0:T(8,128)(2,1)}, u32[]{:S(2)}) %copy-start) | copy-done | bytes 9437208
  98.3 8.5 %attention.1 = (bf16[256,256]{1,0:T(8,128)(2,1)}, bf16[3,256,256]{2,1,0:T(8,128)(2,1)S(1)}, f32[8,384]{1,0:T(8,128)S(1)}) custom-call(bf16[16,272,384]{2,1,0:T(8,128)(2,1)S(1)} %copy-done.2, bf16[16,2,576,256]{3,2,1,0:T(8,128)(2,1)S(1)} %bitcast.5, f32[2,128]{1,0:T(2,128)S(1)} %copy-done.12, bf16[256,256]{1,0:T(8,128)(2,1)S(1)} %copy-done.11), custom_call_target="tpu_custom_call" | custom-call | tf_op jit(solution)/shard_map/attention/pallas_call | solution.py:245
  107.4 2.3 %collective-permute-start.12 = (bf16[1,272,384]{2,1,0:T(8,128)(2,1)S(1)}, bf16[1,272,384]{2,1,0:T(8,128)(2,1)S(1)}, u32[]{:S(2)}, u32[]{:S(2)}) collective-permute-start(bf16[1,272,384]{2,1,0:T(8,128)(2,1)S(1)} %get-tuple-element.26), channel_id=1, source_target_pairs={{0,7},{1,0},{2,1},{3,2},{4,3},{5,4},{6,5},{7,6},{8,15},{9,8},{10,9... | collective-permute-start | bytes 626696 | tf_op jit(solution)/shard_map/ppermute | solution.py:288
  109.6 3.7 %collective-permute-start.8 = (bf16[1,272,384]{2,1,0:T(8,128)(2,1)S(1)}, bf16[1,272,384]{2,1,0:T(8,128)(2,1)S(1)}, u32[]{:S(2)}, u32[]{:S(2)}) collective-permute-start(bf16[1,272,384]{2,1,0:T(8,128)(2,1)S(1)} %get-tuple-element.22), channel_id=1, source_target_pairs={{0,1},{1,2},{2,3},{3,4},{4,5},{5,6},{6,7},{7,0},{8,9},{9,10},{10,1... | collective-permute-start | bytes 626696 | tf_op jit(solution)/shard_map/ppermute | solution.py:287
  113.4 3.0 %backward_near.1 = (bf16[2,272,384]{2,1,0:T(8,128)(2,1)S(1)}, bf16[2,272,384]{2,1,0:T(8,128)(2,1)S(1)}, bf16[2,272,384]{2,1,0:T(8,128)(2,1)S(1)}, bf16[2,272,384...) custom-call(s32[1]{0:T(128)} %bitcast.refs_0_, ...), custom_call_target="tpu_custom_call" | custom-call | flops 2113929216 | bytes 2097152 | tf_op jit(solution)/shard_map/backward_near/pallas_call | solution.py:263
  124.4 3.3 %collective-permute-start.13 = (bf16[2,272,384]{2,1,0:T(8,128)(2,1)}, bf16[2,272,384]{2,1,0:T(8,128)(2,1)S(1)}, u32[]{:S(2)}, u32[]{:S(2)}) collective-permute-start(bf16[2,272,384]{2,1,0:T(8,128)(2,1)} %add_behind.3), channel_id=1, source_target_pairs={{0,7},{1,0},{2,1},{3,2},{4,3},{5,4},{6,5},{7,6},{8,15},{9,8},{10,9... | collective-permute-start | bytes 1253384 | tf_op jit(solution)/shard_map/ppermute | solution.py:288
  130.4 2.5 %collective-permute-start.9 = (bf16[2,272,384]{2,1,0:T(8,128)(2,1)}, bf16[2,272,384]{2,1,0:T(8,128)(2,1)S(1)}, u32[]{:S(2)}, u32[]{:S(2)}) collective-permute-start(bf16[2,272,384]{2,1,0:T(8,128)(2,1)} %add_ahead.3), channel_id=1, source_target_pairs={{0,1},{1,2},{2,3},{3,4},{4,5},{5,6},{6,7},{7,0},{8,9},{9,10},{10,1... | collective-permute-start | bytes 1253384 | tf_op jit(solution)/shard_map/ppermute | solution.py:287
  132.9 3.9 %collective-permute-done.13.refs_0_ = bf16[2,272,384]{2,1,0:T(8,128)(2,1)S(1)} collective-permute-done((bf16[2,272,384]{2,1,0:T(8,128)(2,1)}, bf16[2,272,384]{2,1,0:T(8,128)(2,1)S(1)}, u32[]{:S(2)}, u32[]{:S(2)}) %collective-permute-start.13) | collective-permute-done | bytes 417824 | tf_op jit(solution)/shard_map/ppermute | solution.py:288
  137.6 2.0 %add_behind.4 = bf16[2,272,384]{2,1,0:T(8,128)(2,1)} custom-call(bf16[2,272,384]{2,1,0:T(8,128)(2,1)} %copy-done.15, bf16[2,272,384]{2,1,0:T(8,128)(2,1)} %copy-done.7), custom_call_target="tpu_custom_call" | custom-call | flops 1000000 | bytes 1048576 | tf_op jit(solution)/shard_map/add_behind/pallas_call | solution.py:274
  139.6 5.5 %collective-permute-start.14 = (bf16[2,272,384]{2,1,0:T(8,128)(2,1)}, bf16[2,272,384]{2,1,0:T(8,128)(2,1)S(1)}, u32[]{:S(2)}, u32[]{:S(2)}) collective-permute-start(bf16[2,272,384]{2,1,0:T(8,128)(2,1)} %add_behind.4), channel_id=1, source_target_pairs={{0,7},{1,0},{2,1},{3,2},{4,3},{5,4},{6,5},{7,6},{8,15},{9,8},{10,9... | collective-permute-start | bytes 1253384 | tf_op jit(solution)/shard_map/ppermute | solution.py:288
  145.8 2.0 %add_ahead.4 = bf16[2,272,384]{2,1,0:T(8,128)(2,1)} custom-call(bf16[2,272,384]{2,1,0:T(8,128)(2,1)} %copy-done.16, bf16[2,272,384]{2,1,0:T(8,128)(2,1)} %copy-done.6), custom_call_target="tpu_custom_call" | custom-call | flops 1000000 | bytes 1048576 | tf_op jit(solution)/shard_map/add_ahead/pallas_call | solution.py:274
  149.7 3.5 %collective-permute-done.14.refs_0_ = bf16[2,272,384]{2,1,0:T(8,128)(2,1)S(1)} collective-permute-done((bf16[2,272,384]{2,1,0:T(8,128)(2,1)}, bf16[2,272,384]{2,1,0:T(8,128)(2,1)S(1)}, u32[]{:S(2)}, u32[]{:S(2)}) %collective-permute-start.14) | collective-permute-done | bytes 417824 | tf_op jit(solution)/shard_map/ppermute | solution.py:288
  154.0 2.0 %add_behind.5 = bf16[2,272,384]{2,1,0:T(8,128)(2,1)} custom-call(bf16[2,272,384]{2,1,0:T(8,128)(2,1)} %copy-done.17, bf16[2,272,384]{2,1,0:T(8,128)(2,1)} %copy-done.5), custom_call_target="tpu_custom_call" | custom-call | flops 1000000 | bytes 1048576 | tf_op jit(solution)/shard_map/add_behind/pallas_call | solution.py:274
  156.0 5.5 %collective-permute-start.15 = (bf16[2,272,384]{2,1,0:T(8,128)(2,1)}, bf16[2,272,384]{2,1,0:T(8,128)(2,1)S(1)}, u32[]{:S(2)}, u32[]{:S(2)}) collective-permute-start(bf16[2,272,384]{2,1,0:T(8,128)(2,1)} %add_behind.5), channel_id=1, source_target_pairs={{0,7},{1,0},{2,1},{3,2},{4,3},{5,4},{6,5},{7,6},{8,15},{9,8},{10,9... | collective-permute-start | bytes 1253384 | tf_op jit(solution)/shard_map/ppermute | solution.py:292
  162.2 2.0 %add_ahead.5 = bf16[2,272,384]{2,1,0:T(8,128)(2,1)} custom-call(bf16[2,272,384]{2,1,0:T(8,128)(2,1)} %copy-done.18, bf16[2,272,384]{2,1,0:T(8,128)(2,1)} %copy-done.4), custom_call_target="tpu_custom_call" | custom-call | flops 1000000 | bytes 1048576 | tf_op jit(solution)/shard_map/add_ahead/pallas_call | solution.py:274
  166.1 2.6 %collective-permute-done.15.behind_ref = bf16[2,272,384]{2,1,0:T(8,128)(2,1)S(1)} collective-permute-done((bf16[2,272,384]{2,1,0:T(8,128)(2,1)}, bf16[2,272,384]{2,1,0:T(8,128)(2,1)S(1)}, u32[]{:S(2)}, u32[]{:S(2)}) %collective-permute-start.15) | collective-permute-done | bytes 417824 | tf_op jit(solution)/shard_map/ppermute | solution.py:292
  168.7 8.0 %collective-permute-done.11.ahead_ref = bf16[2,272,384]{2,1,0:T(8,128)(2,1)S(1)} collective-permute-done((bf16[2,272,384]{2,1,0:T(8,128)(2,1)}, bf16[2,272,384]{2,1,0:T(8,128)(2,1)S(1)}, u32[]{:S(2)}, u32[]{:S(2)}) %collective-permute-start.11) | collective-permute-done | bytes 417824 | tf_op jit(solution)/shard_map/ppermute | solution.py:291
  177.4 2.1 %join.1 = (bf16[272,384]{1,0:T(8,128)(2,1)}, bf16[272,384]{1,0:T(8,128)(2,1)}) custom-call(s32[1]{0:T(128)} %bitcast.4.xl_ref, bf16[2,272,384]{2,1,0:T(8,128)(2,1)} %copy-done.14, bf16[2,272,384]{2,1,0:T(8,128)(2,1)} %copy-done.13, bf16[2,272,384]{2,1,0:T(8,128)(2,1)} %copy-done.3), custom_call_target="tpu_custom_call" | custom-call | tf_op jit(solution)/shard_map/join/pallas_call | solution.py:293
  179.5 2.6 %collective-permute-start.16 = (bf16[272,384]{1,0:T(8,128)(2,1)}, bf16[272,384]{1,0:T(8,128)(2,1)S(1)}, u32[]{:S(2)}, u32[]{:S(2)}) collective-permute-start(bf16[272,384]{1,0:T(8,128)(2,1)} %get-tuple-element.32), channel_id=1, source_target_pairs={{0,8},{8,0},{1,9},{9,1},{2,10},{10,2},{3,11},{11,3},{4,12},{12,4},... | collective-permute-start | bytes 626696 | tf_op jit(solution)/shard_map/ppermute | solution.py:300
  182.1 5.3 %collective-permute-done.16.refs_1_ = bf16[272,384]{1,0:T(8,128)(2,1)S(1)} collective-permute-done((bf16[272,384]{1,0:T(8,128)(2,1)}, bf16[272,384]{1,0:T(8,128)(2,1)S(1)}, u32[]{:S(2)}, u32[]{:S(2)}) %collective-permute-start.16) | collective-permute-done | bytes 208928 | tf_op jit(solution)/shard_map/ppermute | solution.py:300
  188.1 2.3 %final_norm.1 = bf16[256,384]{1,0:T(8,128)(2,1)} custom-call(bf16[272,384]{1,0:T(8,128)(2,1)} %get-tuple-element.31.refs_0_, bf16[272,384]{1,0:T(8,128)(2,1)} %copy-done.21, bf16[256,384]{1,0:T(8,128)(2,1)} %refs_2_.1, bf16[16,384]{1,0:T(8,128)(2,1)} %copy-done.22, f32[2,256,128]{2,1,0:T(8,128)} %copy-done.10), custom_call_target="tpu_custom_call" | custom-call | tf_op jit(solution)/shard_map/final_norm/pallas_call | solution.py:301
  (76 shorter events, 36.2 us)
Async XLA Ops:
  7.2 83.9 %all-gather.4.cloned.1.call-start = ((), (), s32[]{:S(2)}) async-start(), calls=%async_computation | async-start | bytes 10027008 | tf_op jit(solution)/shard_map/all_gather | solution.py:220
  20.4 55.5 %copy-start.22 = (bf16[16,384]{1,0:T(8,128)(2,1)}, bf16[16,384]{1,0:T(8,128)(2,1)S(1)}, u32[]{:S(2)}) copy-start(bf16[16,384]{1,0:T(8,128)(2,1)S(1)} %broadcast_in_dim.7.refs_3_) | copy-start | bytes 36868
  28.8 17.9 %collective-permute-start.1 = (bf16[2,272,384]{2,1,0:T(8,128)(2,1)S(1)}, bf16[2,272,384]{2,1,0:T(8,128)(2,1)S(1)}, u32[]{:S(2)}, u32[]{:S(2)}) collective-permute-start(bf16[2,272,384]{2,1,0:T(8,128)(2,1)S(1)} %bitcast.10), channel_id=1, source_target_pairs={{0,7},{1,0},{2,1},{3,2},{4,3},{5,4},{6,5},{7,6},{8,15},{9,8},{10,9... | collective-permute-start | bytes 1253384 | tf_op jit(solution)/shard_map/ppermute | solution.py:228
  39.3 13.0 %collective-permute-start = (bf16[2,272,384]{2,1,0:T(8,128)(2,1)S(1)}, bf16[2,272,384]{2,1,0:T(8,128)(2,1)S(1)}, u32[]{:S(2)}, u32[]{:S(2)}) collective-permute-start(bf16[2,272,384]{2,1,0:T(8,128)(2,1)S(1)} %bitcast.11), channel_id=1, source_target_pairs={{0,1},{1,2},{2,3},{3,4},{4,5},{5,6},{6,7},{7,0},{8,9},{9,10},{10,1... | collective-permute-start | bytes 1253384 | tf_op jit(solution)/shard_map/ppermute | solution.py:227
  46.7 12.2 %collective-permute-start.3 = (bf16[2,272,384]{2,1,0:T(8,128)(2,1)S(1)}, bf16[2,272,384]{2,1,0:T(8,128)(2,1)S(1)}, u32[]{:S(2)}, u32[]{:S(2)}) collective-permute-start(bf16[2,272,384]{2,1,0:T(8,128)(2,1)S(1)} %collective-permute-done.1.refs_3_), channel_id=1, source_target_pairs={{0,7},{1,0},{2,1},{3,2},{4,3},{5,4},{6,5},{7,6},{8,15},{9,8},{10,9... | collective-permute-start | bytes 1253384 | tf_op jit(solution)/shard_map/ppermute | solution.py:228
  52.3 12.2 %collective-permute-start.2 = (bf16[2,272,384]{2,1,0:T(8,128)(2,1)S(1)}, bf16[2,272,384]{2,1,0:T(8,128)(2,1)S(1)}, u32[]{:S(2)}, u32[]{:S(2)}) collective-permute-start(bf16[2,272,384]{2,1,0:T(8,128)(2,1)S(1)} %collective-permute-done.refs_2_), channel_id=1, source_target_pairs={{0,1},{1,2},{2,3},{3,4},{4,5},{5,6},{6,7},{7,0},{8,9},{9,10},{10,1... | collective-permute-start | bytes 1253384 | tf_op jit(solution)/shard_map/ppermute | solution.py:227
  58.9 11.4 %collective-permute-start.5 = (bf16[2,272,384]{2,1,0:T(8,128)(2,1)S(1)}, bf16[2,272,384]{2,1,0:T(8,128)(2,1)S(1)}, u32[]{:S(2)}, u32[]{:S(2)}) collective-permute-start(bf16[2,272,384]{2,1,0:T(8,128)(2,1)S(1)} %collective-permute-done.3.refs_5_), channel_id=1, source_target_pairs={{0,7},{1,0},{2,1},{3,2},{4,3},{5,4},{6,5},{7,6},{8,15},{9,8},{10,9... | collective-permute-start | bytes 1253384 | tf_op jit(solution)/shard_map/ppermute | solution.py:228
  64.5 11.4 %collective-permute-start.4 = (bf16[2,272,384]{2,1,0:T(8,128)(2,1)S(1)}, bf16[2,272,384]{2,1,0:T(8,128)(2,1)S(1)}, u32[]{:S(2)}, u32[]{:S(2)}) collective-permute-start(bf16[2,272,384]{2,1,0:T(8,128)(2,1)S(1)} %collective-permute-done.2.refs_4_), channel_id=1, source_target_pairs={{0,1},{1,2},{2,3},{3,4},{4,5},{5,6},{6,7},{7,0},{8,9},{9,10},{10,1... | collective-permute-start | bytes 1253384 | tf_op jit(solution)/shard_map/ppermute | solution.py:227
  70.3 8.9 %collective-permute-start.7 = (bf16[1,272,384]{2,1,0:T(8,128)(2,1)S(1)}, bf16[1,272,384]{2,1,0:T(8,128)(2,1)S(1)}, u32[]{:S(2)}, u32[]{:S(2)}) collective-permute-start(bf16[1,272,384]{2,1,0:T(8,128)(2,1)S(1)} %slice.9), channel_id=1, source_target_pairs={{0,7},{1,0},{2,1},{3,2},{4,3},{5,4},{6,5},{7,6},{8,15},{9,8},{10,9... | collective-permute-start | bytes 626696 | tf_op jit(solution)/shard_map/ppermute | solution.py:231
  76.6 9.1 %collective-permute-start.6 = (bf16[1,272,384]{2,1,0:T(8,128)(2,1)}, bf16[1,272,384]{2,1,0:T(8,128)(2,1)S(1)}, u32[]{:S(2)}, u32[]{:S(2)}) collective-permute-start(bf16[1,272,384]{2,1,0:T(8,128)(2,1)} %slice.8), channel_id=1, source_target_pairs={{0,1},{1,2},{2,3},{3,4},{4,5},{5,6},{6,7},{7,0},{8,9},{9,10},{10,1... | collective-permute-start | bytes 626696 | tf_op jit(solution)/shard_map/ppermute | solution.py:230
  88.6 1.8 copy-start.1
  91.1 3.7 %copy-start = (bf16[32,576,256]{2,1,0:T(8,128)(2,1)S(1)}, bf16[32,576,256]{2,1,0:T(8,128)(2,1)}, u32[]{:S(2)}) copy-start(bf16[32,576,256]{2,1,0:T(8,128)(2,1)} %all-gather.4.cloned.1.call-done) | copy-start | bytes 28311556
  94.8 1.9 copy-start.2
  96.7 0.9 copy-start.11
  98.3 15.1 %slice-start = ((s8[9437184]{0:T(1024)(128)(4,1)}), s8[4194304]{0:T(1024)(128)(4,1)S(1)}, s32[]{:S(2)}) async-start(s8[9437184]{0:T(1024)(128)(4,1)} %bitcast.7), calls=%async_computation.1 | async-start | bytes 8388608
  98.3 15.1 %slice-start.1 = ((s8[9437184]{0:T(1024)(128)(4,1)}), s8[1048576]{0:T(1024)(128)(4,1)S(1)}, s32[]{:S(2)}) async-start(s8[9437184]{0:T(1024)(128)(4,1)} %bitcast.7), calls=%async_computation.2 | async-start | bytes 2097152
  106.8 6.6 %slice-start.2 = ((s8[9437184]{0:T(1024)(128)(4,1)}), s8[4194304]{0:T(1024)(128)(4,1)S(1)}, s32[]{:S(2)}) async-start(s8[9437184]{0:T(1024)(128)(4,1)} %bitcast.7), calls=%async_computation.3 | async-start | bytes 8388608
  107.4 14.4 %collective-permute-start.12 = (bf16[1,272,384]{2,1,0:T(8,128)(2,1)S(1)}, bf16[1,272,384]{2,1,0:T(8,128)(2,1)S(1)}, u32[]{:S(2)}, u32[]{:S(2)}) collective-permute-start(bf16[1,272,384]{2,1,0:T(8,128)(2,1)S(1)} %get-tuple-element.26), channel_id=1, source_target_pairs={{0,7},{1,0},{2,1},{3,2},{4,3},{5,4},{6,5},{7,6},{8,15},{9,8},{10,9... | collective-permute-start | bytes 626696 | tf_op jit(solution)/shard_map/ppermute | solution.py:288
  109.6 18.1 %collective-permute-start.8 = (bf16[1,272,384]{2,1,0:T(8,128)(2,1)S(1)}, bf16[1,272,384]{2,1,0:T(8,128)(2,1)S(1)}, u32[]{:S(2)}, u32[]{:S(2)}) collective-permute-start(bf16[1,272,384]{2,1,0:T(8,128)(2,1)S(1)} %get-tuple-element.22), channel_id=1, source_target_pairs={{0,1},{1,2},{2,3},{3,4},{4,5},{5,6},{6,7},{7,0},{8,9},{9,10},{10,1... | collective-permute-start | bytes 626696 | tf_op jit(solution)/shard_map/ppermute | solution.py:287
  116.4 0.8 copy-start.3
  120.2 0.8 copy-start.8
  121.0 0.8 copy-start.9
  124.4 12.4 %collective-permute-start.13 = (bf16[2,272,384]{2,1,0:T(8,128)(2,1)}, bf16[2,272,384]{2,1,0:T(8,128)(2,1)S(1)}, u32[]{:S(2)}, u32[]{:S(2)}) collective-permute-start(bf16[2,272,384]{2,1,0:T(8,128)(2,1)} %add_behind.3), channel_id=1, source_target_pairs={{0,7},{1,0},{2,1},{3,2},{4,3},{5,4},{6,5},{7,6},{8,15},{9,8},{10,9... | collective-permute-start | bytes 1253384 | tf_op jit(solution)/shard_map/ppermute | solution.py:288
  130.4 14.7 %collective-permute-start.9 = (bf16[2,272,384]{2,1,0:T(8,128)(2,1)}, bf16[2,272,384]{2,1,0:T(8,128)(2,1)S(1)}, u32[]{:S(2)}, u32[]{:S(2)}) collective-permute-start(bf16[2,272,384]{2,1,0:T(8,128)(2,1)} %add_ahead.3), channel_id=1, source_target_pairs={{0,1},{1,2},{2,3},{3,4},{4,5},{5,6},{6,7},{7,0},{8,9},{9,10},{10,1... | collective-permute-start | bytes 1253384 | tf_op jit(solution)/shard_map/ppermute | solution.py:287
  139.6 13.6 %collective-permute-start.14 = (bf16[2,272,384]{2,1,0:T(8,128)(2,1)}, bf16[2,272,384]{2,1,0:T(8,128)(2,1)S(1)}, u32[]{:S(2)}, u32[]{:S(2)}) collective-permute-start(bf16[2,272,384]{2,1,0:T(8,128)(2,1)} %add_behind.4), channel_id=1, source_target_pairs={{0,7},{1,0},{2,1},{3,2},{4,3},{5,4},{6,5},{7,6},{8,15},{9,8},{10,9... | collective-permute-start | bytes 1253384 | tf_op jit(solution)/shard_map/ppermute | solution.py:288
  145.1 0.8 copy-start.16
  147.8 13.6 %collective-permute-start.10 = (bf16[2,272,384]{2,1,0:T(8,128)(2,1)}, bf16[2,272,384]{2,1,0:T(8,128)(2,1)S(1)}, u32[]{:S(2)}, u32[]{:S(2)}) collective-permute-start(bf16[2,272,384]{2,1,0:T(8,128)(2,1)} %add_ahead.4), channel_id=1, source_target_pairs={{0,1},{1,2},{2,3},{3,4},{4,5},{5,6},{6,7},{7,0},{8,9},{9,10},{10,1... | collective-permute-start | bytes 1253384 | tf_op jit(solution)/shard_map/ppermute | solution.py:287
  153.2 0.8 copy-start.17
  156.0 12.7 %collective-permute-start.15 = (bf16[2,272,384]{2,1,0:T(8,128)(2,1)}, bf16[2,272,384]{2,1,0:T(8,128)(2,1)S(1)}, u32[]{:S(2)}, u32[]{:S(2)}) collective-permute-start(bf16[2,272,384]{2,1,0:T(8,128)(2,1)} %add_behind.5), channel_id=1, source_target_pairs={{0,7},{1,0},{2,1},{3,2},{4,3},{5,4},{6,5},{7,6},{8,15},{9,8},{10,9... | collective-permute-start | bytes 1253384 | tf_op jit(solution)/shard_map/ppermute | solution.py:292
  164.2 12.4 %collective-permute-start.11 = (bf16[2,272,384]{2,1,0:T(8,128)(2,1)}, bf16[2,272,384]{2,1,0:T(8,128)(2,1)S(1)}, u32[]{:S(2)}, u32[]{:S(2)}) collective-permute-start(bf16[2,272,384]{2,1,0:T(8,128)(2,1)} %add_ahead.5), channel_id=1, source_target_pairs={{0,1},{1,2},{2,3},{3,4},{4,5},{5,6},{6,7},{7,0},{8,9},{9,10},{10,1... | collective-permute-start | bytes 1253384 | tf_op jit(solution)/shard_map/ppermute | solution.py:291
  168.7 8.0 %copy-start.13 = (bf16[2,272,384]{2,1,0:T(8,128)(2,1)}, bf16[2,272,384]{2,1,0:T(8,128)(2,1)S(1)}, u32[]{:S(2)}) copy-start(bf16[2,272,384]{2,1,0:T(8,128)(2,1)S(1)} %collective-permute-done.15.behind_ref) | copy-start | bytes 1253380
  179.5 7.9 %collective-permute-start.16 = (bf16[272,384]{1,0:T(8,128)(2,1)}, bf16[272,384]{1,0:T(8,128)(2,1)S(1)}, u32[]{:S(2)}, u32[]{:S(2)}) collective-permute-start(bf16[272,384]{1,0:T(8,128)(2,1)} %get-tuple-element.32), channel_id=1, source_target_pairs={{0,8},{8,0},{1,9},{9,1},{2,10},{10,2},{3,11},{11,3},{4,12},{12,4},... | collective-permute-start | bytes 626696 | tf_op jit(solution)/shard_map/ppermute | solution.py:300
  (12 other events, 8.7 us)
Sparse Core Ops, SparseCore 0:
  19.8 67.4 all-gather.3

commit v3 on v2

--- a/solution.py
+++ b/solution.py
@@ -238,7 +238,7 @@
         ),
         in_specs=[SMEM] + [VMEM] * len(pieces),
         out_specs=(VMEM, VMEM),
-        compiler_params=params(32),
+        compiler_params=params(16),
         name="normalise",
     )(z[None], *pieces)
 
@@ -252,7 +252,7 @@
         in_specs=[VMEM] * 4,
         out_specs=(VMEM,) * 3,
         scratch_shapes=[pltpu.VMEM((rows + GAIN_ROWS, 3 * width), F32)],
-        compiler_params=params(40),
+        compiler_params=params(16),
         name="attention",
     )(normed, weights, qk_gain, cotangent)
 
@@ -265,7 +265,7 @@
             out_shape=tuple(jax.ShapeDtypeStruct((len(p),) + block, BF16) for p in plan),
             in_specs=[SMEM] + [VMEM] * 3,
             out_specs=(VMEM,) * len(plan),
-            compiler_params=params(32),
+            compiler_params=params(16),
             cost_estimate=pl.CostEstimate(flops=flops, bytes_accessed=2 * 2**20, transcendentals=0),
             name=name,
         )(z[None], grads, weights, sums)
@@ -276,6 +276,7 @@
             out_shape=jax.ShapeDtypeStruct(part.shape, BF16),
             in_specs=[VMEM] * 2,
             out_specs=VMEM,
+            compiler_params=params(16),
             cost_estimate=pl.CostEstimate(flops=10**6, bytes_accessed=2**20, transcendentals=0),
             name=name,
         )(got, part)
@@ -295,6 +296,7 @@
         out_shape=(jax.ShapeDtypeStruct(block, BF16),) * 2,
         in_specs=[SMEM] + [VMEM] * 3,
         out_specs=(VMEM, VMEM),
+        compiler_params=params(16),
         name="join",
     )(lax.axis_index("xl").astype(jnp.int32)[None], ahead, behind, parts[6])
     other = lax.ppermute(other, "xl", ring(2, 1))
@@ -303,6 +305,7 @@
         out_shape=jax.ShapeDtypeStruct((rows, feat), BF16),
         in_specs=[VMEM] * 5,
         out_specs=VMEM,
+        compiler_params=params(16),
         name="final_norm",
     )(mine, other, tokens, gain, stats)
     return (attended, grad_tokens)

time: 198 us -> 182 us (0.919)
  the two profiles are of different devices: /device:TPU:6 before, /device:TPU:40 now
where the time goes in v3:
time: 182 us; the launch traced here: 181 us
  starting transfers between devices  61.8 us (34%)
  waiting for transfers between devices  46 us (25%)
  blocking collectives  21.1 us (12%)
  local copies, waits for them, and re-layouts  19.9 us (11%)
  Pallas kernels  16.8 us (9%)
  between operations  14.4 us (8%)
    ppermute x7, starting transfers between devices, per_device(): behind = lax.ppermute(behind, 'z', ring(8, -1))  35.5 us
    ppermute x7, waiting for transfers between devices, per_device(): behind = lax.ppermute(behind, 'z', ring(8, -1))  27 us
    unnamed x50, local copies, waits for them, and re-layouts  19.2 us
    ppermute x7, starting transfers between devices, per_device(): ahead = lax.ppermute(ahead, 'z', ring(8, 1))  16.3 us
    all_gather x1, blocking collectives, per_device(): weights = lax.all_gather(weights, 'xh', axis=0)  14.1 us
    pallas_call x1, Pallas kernels, per_device(): pl.pallas_call(attention_kernel, out_shape=(jax.ShapeDtypeStruct((rows, w...  8.51 us
    all_gather x1, blocking collectives, per_device(): own = lax.all_gather(jnp.concatenate([tokens, gain], axis=0), 'xl', axis=0)  7.03 us
    ppermute x7, waiting for transfers between devices, per_device(): ahead = lax.ppermute(ahead, 'z', ring(8, 1))  6.83 us
  transfers between devices with their start and end apart: 18, of which 12 were waited for; matrix products, arithmetic and copies ran while one was open for 1% of the time, Pallas kernels for 4%

profile of v3, /device:TPU:40, one launch (start us, length us, event | category | flops | bytes accessed | tf_op | source)
XLA Modules:
  0.0 181.0 jit_solution(16101033433010016384)
XLA Ops:
  7.2 14.1 %all_gather.17 = bf16[2,576,256]{2,1,0:T(8,128)(2,1)} all-gather(bf16[1,576,256]{2,1,0:T(8,128)(2,1)} %bitcast.11), channel_id=1, replica_groups=mesh['xh'=2,'y'=8,'c'=2,'xl'=2,'z'=8] {'xh'}, dimensions={0}, use_global_device_ids=true | all-gather | bytes 884736 | tf_op jit(solution)/shard_map/all_gather | solution.py:219
  23.0 7.0 %all-gather = bf16[544,384]{1,0:T(8,128)(2,1)S(1)} all-gather(bf16[272,384]{1,0:T(8,128)(2,1)S(1)} %pad_maximum_fusion), channel_id=2, replica_groups=mesh['xh'=2,'y'=8,'c'=2,'xl'=2,'z'=8] {'xl'}, dimensions={0}, use_global_device_ids=true | all-gather | bytes 626688 | tf_op jit(solution)/shard_map/all_gather | solution.py:223
  30.0 10.9 %collective-permute-start.1 = (bf16[2,272,384]{2,1,0:T(8,128)(2,1)S(1)}, bf16[2,272,384]{2,1,0:T(8,128)(2,1)S(1)}, u32[]{:S(2)}, u32[]{:S(2)}) collective-permute-start(bf16[2,272,384]{2,1,0:T(8,128)(2,1)S(1)} %bitcast.8), channel_id=1, source_target_pairs={{0,7},{1,0},{2,1},{3,2},{4,3},{5,4},{6,5},{7,6},{8,15},{9,8},{10,9... | collective-permute-start | bytes 1253384 | tf_op jit(solution)/shard_map/ppermute | solution.py:228
  40.9 1.9 %collective-permute-start = (bf16[2,272,384]{2,1,0:T(8,128)(2,1)S(1)}, bf16[2,272,384]{2,1,0:T(8,128)(2,1)S(1)}, u32[]{:S(2)}, u32[]{:S(2)}) collective-permute-start(bf16[2,272,384]{2,1,0:T(8,128)(2,1)S(1)} %bitcast.9), channel_id=1, source_target_pairs={{0,1},{1,2},{2,3},{3,4},{4,5},{5,6},{6,7},{7,0},{8,9},{9,10},{10,1... | collective-permute-start | bytes 1253384 | tf_op jit(solution)/shard_map/ppermute | solution.py:227
  43.6 4.7 %collective-permute-done.1.refs_3_ = bf16[2,272,384]{2,1,0:T(8,128)(2,1)S(1)} collective-permute-done((bf16[2,272,384]{2,1,0:T(8,128)(2,1)S(1)}, bf16[2,272,384]{2,1,0:T(8,128)(2,1)S(1)}, u32[]{:S(2)}, u32[]{:S(2)}) %collective-permute-start.1) | collective-permute-done | bytes 417824 | tf_op jit(solution)/shard_map/ppermute | solution.py:228
  48.3 5.6 %collective-permute-start.3 = (bf16[2,272,384]{2,1,0:T(8,128)(2,1)S(1)}, bf16[2,272,384]{2,1,0:T(8,128)(2,1)S(1)}, u32[]{:S(2)}, u32[]{:S(2)}) collective-permute-start(bf16[2,272,384]{2,1,0:T(8,128)(2,1)S(1)} %collective-permute-done.1.refs_3_), channel_id=1, source_target_pairs={{0,7},{1,0},{2,1},{3,2},{4,3},{5,4},{6,5},{7,6},{8,15},{9,8},{10,9... | collective-permute-start | bytes 1253384 | tf_op jit(solution)/shard_map/ppermute | solution.py:228
  54.7 1.9 %collective-permute-start.2 = (bf16[2,272,384]{2,1,0:T(8,128)(2,1)S(1)}, bf16[2,272,384]{2,1,0:T(8,128)(2,1)S(1)}, u32[]{:S(2)}, u32[]{:S(2)}) collective-permute-start(bf16[2,272,384]{2,1,0:T(8,128)(2,1)S(1)} %collective-permute-done.refs_2_), channel_id=1, source_target_pairs={{0,1},{1,2},{2,3},{3,4},{4,5},{5,6},{6,7},{7,0},{8,9},{9,10},{10,1... | collective-permute-start | bytes 1253384 | tf_op jit(solution)/shard_map/ppermute | solution.py:227
  57.4 3.0 %collective-permute-done.3.refs_5_ = bf16[2,272,384]{2,1,0:T(8,128)(2,1)S(1)} collective-permute-done((bf16[2,272,384]{2,1,0:T(8,128)(2,1)S(1)}, bf16[2,272,384]{2,1,0:T(8,128)(2,1)S(1)}, u32[]{:S(2)}, u32[]{:S(2)}) %collective-permute-start.3) | collective-permute-done | bytes 417824 | tf_op jit(solution)/shard_map/ppermute | solution.py:228
  60.4 5.6 %collective-permute-start.5 = (bf16[2,272,384]{2,1,0:T(8,128)(2,1)S(1)}, bf16[2,272,384]{2,1,0:T(8,128)(2,1)S(1)}, u32[]{:S(2)}, u32[]{:S(2)}) collective-permute-start(bf16[2,272,384]{2,1,0:T(8,128)(2,1)S(1)} %collective-permute-done.3.refs_5_), channel_id=1, source_target_pairs={{0,7},{1,0},{2,1},{3,2},{4,3},{5,4},{6,5},{7,6},{8,15},{9,8},{10,9... | collective-permute-start | bytes 1253384 | tf_op jit(solution)/shard_map/ppermute | solution.py:228
  66.8 1.9 %collective-permute-start.4 = (bf16[2,272,384]{2,1,0:T(8,128)(2,1)S(1)}, bf16[2,272,384]{2,1,0:T(8,128)(2,1)S(1)}, u32[]{:S(2)}, u32[]{:S(2)}) collective-permute-start(bf16[2,272,384]{2,1,0:T(8,128)(2,1)S(1)} %collective-permute-done.2.refs_4_), channel_id=1, source_target_pairs={{0,1},{1,2},{2,3},{3,4},{4,5},{5,6},{6,7},{7,0},{8,9},{9,10},{10,1... | collective-permute-start | bytes 1253384 | tf_op jit(solution)/shard_map/ppermute | solution.py:227
  68.7 2.9 %collective-permute-done.5.refs_7_ = bf16[2,272,384]{2,1,0:T(8,128)(2,1)S(1)} collective-permute-done((bf16[2,272,384]{2,1,0:T(8,128)(2,1)S(1)}, bf16[2,272,384]{2,1,0:T(8,128)(2,1)S(1)}, u32[]{:S(2)}, u32[]{:S(2)}) %collective-permute-start.5) | collective-permute-done | bytes 417824 | tf_op jit(solution)/shard_map/ppermute | solution.py:228
  72.4 5.6 %collective-permute-start.7 = (bf16[1,272,384]{2,1,0:T(8,128)(2,1)S(1)}, bf16[1,272,384]{2,1,0:T(8,128)(2,1)S(1)}, u32[]{:S(2)}, u32[]{:S(2)}) collective-permute-start(bf16[1,272,384]{2,1,0:T(8,128)(2,1)S(1)} %slice.9), channel_id=1, source_target_pairs={{0,7},{1,0},{2,1},{3,2},{4,3},{5,4},{6,5},{7,6},{8,15},{9,8},{10,9... | collective-permute-start | bytes 626696 | tf_op jit(solution)/shard_map/ppermute | solution.py:231
  78.8 1.9 %collective-permute-start.6 = (bf16[1,272,384]{2,1,0:T(8,128)(2,1)S(1)}, bf16[1,272,384]{2,1,0:T(8,128)(2,1)S(1)}, u32[]{:S(2)}, u32[]{:S(2)}) collective-permute-start(bf16[1,272,384]{2,1,0:T(8,128)(2,1)S(1)} %slice.8), channel_id=1, source_target_pairs={{0,1},{1,2},{2,3},{3,4},{4,5},{5,6},{6,7},{7,0},{8,9},{9,10},{10,1... | collective-permute-start | bytes 626696 | tf_op jit(solution)/shard_map/ppermute | solution.py:230
  81.3 6.4 %collective-permute-done.6.refs_8_ = bf16[1,272,384]{2,1,0:T(8,128)(2,1)S(1)} collective-permute-done((bf16[1,272,384]{2,1,0:T(8,128)(2,1)S(1)}, bf16[1,272,384]{2,1,0:T(8,128)(2,1)S(1)}, u32[]{:S(2)}, u32[]{:S(2)}) %collective-permute-start.6) | collective-permute-done | bytes 208928 | tf_op jit(solution)/shard_map/ppermute | solution.py:230
  96.4 2.9 %normalise.1 = (bf16[16,272,384]{2,1,0:T(8,128)(2,1)S(1)}, f32[2,256,128]{2,1,0:T(8,128)S(1)}) custom-call(s32[1]{0:T(128)} %bitcast.refs_0_, bf16[2,272,384]{2,1,0:T(8,128)(2,1)S(1)} %bitcast.10, bf16[2,272,384]{2,1,0:T(8,128)(2,1)S(1)} %copy-done.12, bf16[2,272,384]{2,1,0:T(8,128)(2,1)S(1)} %copy-done.10, bf16[2,272,384]{2,1,0:T(8,128)(2,1)S(1)} %copy-done.16, ...), custom_call_target="tpu_custom_call" | custom-call | tf_op jit(solution)/shard_map/normalise/pallas_call | solution.py:233
  100.0 3.7 %copy-done = bf16[32,576,256]{2,1,0:T(8,128)(2,1)S(1)} copy-done((bf16[32,576,256]{2,1,0:T(8,128)(2,1)S(1)}, bf16[32,576,256]{2,1,0:T(8,128)(2,1)}, u32[]{:S(2)}) %copy-start) | copy-done | bytes 9437208
  105.2 8.5 %attention.1 = (bf16[256,256]{1,0:T(8,128)(2,1)}, bf16[3,256,256]{2,1,0:T(8,128)(2,1)S(1)}, f32[8,384]{1,0:T(8,128)S(1)}) custom-call(bf16[16,272,384]{2,1,0:T(8,128)(2,1)S(1)} %get-tuple-element.18.normed_ref, bf16[16,2,576,256]{3,2,1,0:T(8,128)(2,1)S(1)} %bitcast.5, f32[2,128]{1,0:T(2,128)S(1)} %copy-done.24, bf16[256,256]{1,0:T(8,128)(2,1)S(1)} %copy-done.21), custom_call_target="tpu_custom_call" | custom-call | tf_op jit(solution)/shard_map/attention/pallas_call | solution.py:245
  114.4 2.1 %collective-permute-start.12 = (bf16[1,272,384]{2,1,0:T(8,128)(2,1)S(1)}, bf16[1,272,384]{2,1,0:T(8,128)(2,1)S(1)}, u32[]{:S(2)}, u32[]{:S(2)}) collective-permute-start(bf16[1,272,384]{2,1,0:T(8,128)(2,1)S(1)} %get-tuple-element.26), channel_id=1, source_target_pairs={{0,7},{1,0},{2,1},{3,2},{4,3},{5,4},{6,5},{7,6},{8,15},{9,8},{10,9... | collective-permute-start | bytes 626696 | tf_op jit(solution)/shard_map/ppermute | solution.py:289
  116.4 3.9 %collective-permute-start.8 = (bf16[1,272,384]{2,1,0:T(8,128)(2,1)S(1)}, bf16[1,272,384]{2,1,0:T(8,128)(2,1)S(1)}, u32[]{:S(2)}, u32[]{:S(2)}) collective-permute-start(bf16[1,272,384]{2,1,0:T(8,128)(2,1)S(1)} %get-tuple-element.22), channel_id=1, source_target_pairs={{0,1},{1,2},{2,3},{3,4},{4,5},{5,6},{6,7},{7,0},{8,9},{9,10},{10,1... | collective-permute-start | bytes 626696 | tf_op jit(solution)/shard_map/ppermute | solution.py:288
  120.4 3.1 %backward_near.1 = (bf16[2,272,384]{2,1,0:T(8,128)(2,1)S(1)}, bf16[2,272,384]{2,1,0:T(8,128)(2,1)S(1)}, bf16[2,272,384]{2,1,0:T(8,128)(2,1)S(1)}, bf16[2,272,384...) custom-call(s32[1]{0:T(128)} %bitcast.refs_0_, ...), custom_call_target="tpu_custom_call" | custom-call | flops 2113929216 | bytes 2097152 | tf_op jit(solution)/shard_map/backward_near/pallas_call | solution.py:263
  123.5 3.1 %collective-permute-start.13 = (bf16[2,272,384]{2,1,0:T(8,128)(2,1)S(1)}, bf16[2,272,384]{2,1,0:T(8,128)(2,1)S(1)}, u32[]{:S(2)}, u32[]{:S(2)}) collective-permute-start(bf16[2,272,384]{2,1,0:T(8,128)(2,1)S(1)} %add_behind.3), channel_id=1, source_target_pairs={{0,7},{1,0},{2,1},{3,2},{4,3},{5,4},{6,5},{7,6},{8,15},{9,8},{10,9... | collective-permute-start | bytes 1253384 | tf_op jit(solution)/shard_map/ppermute | solution.py:289
  126.7 2.7 %collective-permute-start.9 = (bf16[2,272,384]{2,1,0:T(8,128)(2,1)S(1)}, bf16[2,272,384]{2,1,0:T(8,128)(2,1)S(1)}, u32[]{:S(2)}, u32[]{:S(2)}) collective-permute-start(bf16[2,272,384]{2,1,0:T(8,128)(2,1)S(1)} %add_ahead.3), channel_id=1, source_target_pairs={{0,1},{1,2},{2,3},{3,4},{4,5},{5,6},{6,7},{7,0},{8,9},{9,10},{10,1... | collective-permute-start | bytes 1253384 | tf_op jit(solution)/shard_map/ppermute | solution.py:288
  129.5 6.3 %collective-permute-done.13.refs_0_ = bf16[2,272,384]{2,1,0:T(8,128)(2,1)S(1)} collective-permute-done((bf16[2,272,384]{2,1,0:T(8,128)(2,1)S(1)}, bf16[2,272,384]{2,1,0:T(8,128)(2,1)S(1)}, u32[]{:S(2)}, u32[]{:S(2)}) %collective-permute-start.13) | collective-permute-done | bytes 417824 | tf_op jit(solution)/shard_map/ppermute | solution.py:289
  135.8 3.7 %collective-permute-start.14 = (bf16[2,272,384]{2,1,0:T(8,128)(2,1)S(1)}, bf16[2,272,384]{2,1,0:T(8,128)(2,1)S(1)}, u32[]{:S(2)}, u32[]{:S(2)}) collective-permute-start(bf16[2,272,384]{2,1,0:T(8,128)(2,1)S(1)} %add_behind.4), channel_id=1, source_target_pairs={{0,7},{1,0},{2,1},{3,2},{4,3},{5,4},{6,5},{7,6},{8,15},{9,8},{10,9... | collective-permute-start | bytes 1253384 | tf_op jit(solution)/shard_map/ppermute | solution.py:289
  139.9 2.0 %collective-permute-start.10 = (bf16[2,272,384]{2,1,0:T(8,128)(2,1)S(1)}, bf16[2,272,384]{2,1,0:T(8,128)(2,1)S(1)}, u32[]{:S(2)}, u32[]{:S(2)}) collective-permute-start(bf16[2,272,384]{2,1,0:T(8,128)(2,1)S(1)} %add_ahead.4), channel_id=1, source_target_pairs={{0,1},{1,2},{2,3},{3,4},{4,5},{5,6},{6,7},{7,0},{8,9},{9,10},{10,1... | collective-permute-start | bytes 1253384 | tf_op jit(solution)/shard_map/ppermute | solution.py:288
  141.8 7.0 %collective-permute-done.14.refs_0_ = bf16[2,272,384]{2,1,0:T(8,128)(2,1)S(1)} collective-permute-done((bf16[2,272,384]{2,1,0:T(8,128)(2,1)S(1)}, bf16[2,272,384]{2,1,0:T(8,128)(2,1)S(1)}, u32[]{:S(2)}, u32[]{:S(2)}) %collective-permute-start.14) | collective-permute-done | bytes 417824 | tf_op jit(solution)/shard_map/ppermute | solution.py:289
  149.0 4.5 %collective-permute-start.15 = (bf16[2,272,384]{2,1,0:T(8,128)(2,1)S(1)}, bf16[2,272,384]{2,1,0:T(8,128)(2,1)S(1)}, u32[]{:S(2)}, u32[]{:S(2)}) collective-permute-start(bf16[2,272,384]{2,1,0:T(8,128)(2,1)S(1)} %add_behind.5), channel_id=1, source_target_pairs={{0,7},{1,0},{2,1},{3,2},{4,3},{5,4},{6,5},{7,6},{8,15},{9,8},{10,9... | collective-permute-start | bytes 1253384 | tf_op jit(solution)/shard_map/ppermute | solution.py:293
  154.1 1.9 %collective-permute-start.11 = (bf16[2,272,384]{2,1,0:T(8,128)(2,1)S(1)}, bf16[2,272,384]{2,1,0:T(8,128)(2,1)S(1)}, u32[]{:S(2)}, u32[]{:S(2)}) collective-permute-start(bf16[2,272,384]{2,1,0:T(8,128)(2,1)S(1)} %add_ahead.5), channel_id=1, source_target_pairs={{0,1},{1,2},{2,3},{3,4},{4,5},{5,6},{6,7},{7,0},{8,9},{9,10},{10,1... | collective-permute-start | bytes 1253384 | tf_op jit(solution)/shard_map/ppermute | solution.py:292
  156.0 3.0 %collective-permute-done.15.behind_ref = bf16[2,272,384]{2,1,0:T(8,128)(2,1)S(1)} collective-permute-done((bf16[2,272,384]{2,1,0:T(8,128)(2,1)S(1)}, bf16[2,272,384]{2,1,0:T(8,128)(2,1)S(1)}, u32[]{:S(2)}, u32[]{:S(2)}) %collective-permute-start.15) | collective-permute-done | bytes 417824 | tf_op jit(solution)/shard_map/ppermute | solution.py:293
  159.1 6.2 %collective-permute-done.11.ahead_ref = bf16[2,272,384]{2,1,0:T(8,128)(2,1)S(1)} collective-permute-done((bf16[2,272,384]{2,1,0:T(8,128)(2,1)S(1)}, bf16[2,272,384]{2,1,0:T(8,128)(2,1)S(1)}, u32[]{:S(2)}, u32[]{:S(2)}) %collective-permute-start.11) | collective-permute-done | bytes 417824 | tf_op jit(solution)/shard_map/ppermute | solution.py:292
  165.4 2.4 %collective-permute-start.16 = (bf16[272,384]{1,0:T(8,128)(2,1)S(1)}, bf16[272,384]{1,0:T(8,128)(2,1)S(1)}, u32[]{:S(2)}, u32[]{:S(2)}) collective-permute-start(bf16[272,384]{1,0:T(8,128)(2,1)S(1)} %get-tuple-element.32), channel_id=1, source_target_pairs={{0,8},{8,0},{1,9},{9,1},{2,10},{10,2},{3,11},{11,3},{4,12},{12,4},... | collective-permute-start | bytes 626696 | tf_op jit(solution)/shard_map/ppermute | solution.py:302
  167.9 5.2 %collective-permute-done.16.refs_1_ = bf16[272,384]{1,0:T(8,128)(2,1)S(1)} collective-permute-done((bf16[272,384]{1,0:T(8,128)(2,1)S(1)}, bf16[272,384]{1,0:T(8,128)(2,1)S(1)}, u32[]{:S(2)}, u32[]{:S(2)}) %collective-permute-start.16) | collective-permute-done | bytes 208928 | tf_op jit(solution)/shard_map/ppermute | solution.py:302
  (73 shorter events, 20.8 us)
Async XLA Ops:
  7.2 92.8 %all-gather.4.cloned.1.call-start = ((), (), s32[]{:S(2)}) async-start(), calls=%async_computation | async-start | bytes 10027008 | tf_op jit(solution)/shard_map/all_gather | solution.py:220
  22.0 58.7 %copy-start.22 = (bf16[16,384]{1,0:T(8,128)(2,1)}, bf16[16,384]{1,0:T(8,128)(2,1)S(1)}, u32[]{:S(2)}) copy-start(bf16[16,384]{1,0:T(8,128)(2,1)S(1)} %broadcast_in_dim.7.refs_3_) | copy-start | bytes 36868
  30.0 18.3 %collective-permute-start.1 = (bf16[2,272,384]{2,1,0:T(8,128)(2,1)S(1)}, bf16[2,272,384]{2,1,0:T(8,128)(2,1)S(1)}, u32[]{:S(2)}, u32[]{:S(2)}) collective-permute-start(bf16[2,272,384]{2,1,0:T(8,128)(2,1)S(1)} %bitcast.8), channel_id=1, source_target_pairs={{0,7},{1,0},{2,1},{3,2},{4,3},{5,4},{6,5},{7,6},{8,15},{9,8},{10,9... | collective-permute-start | bytes 1253384 | tf_op jit(solution)/shard_map/ppermute | solution.py:228
  40.9 13.8 %collective-permute-start = (bf16[2,272,384]{2,1,0:T(8,128)(2,1)S(1)}, bf16[2,272,384]{2,1,0:T(8,128)(2,1)S(1)}, u32[]{:S(2)}, u32[]{:S(2)}) collective-permute-start(bf16[2,272,384]{2,1,0:T(8,128)(2,1)S(1)} %bitcast.9), channel_id=1, source_target_pairs={{0,1},{1,2},{2,3},{3,4},{4,5},{5,6},{6,7},{7,0},{8,9},{9,10},{10,1... | collective-permute-start | bytes 1253384 | tf_op jit(solution)/shard_map/ppermute | solution.py:227
  48.3 12.1 %collective-permute-start.3 = (bf16[2,272,384]{2,1,0:T(8,128)(2,1)S(1)}, bf16[2,272,384]{2,1,0:T(8,128)(2,1)S(1)}, u32[]{:S(2)}, u32[]{:S(2)}) collective-permute-start(bf16[2,272,384]{2,1,0:T(8,128)(2,1)S(1)} %collective-permute-done.1.refs_3_), channel_id=1, source_target_pairs={{0,7},{1,0},{2,1},{3,2},{4,3},{5,4},{6,5},{7,6},{8,15},{9,8},{10,9... | collective-permute-start | bytes 1253384 | tf_op jit(solution)/shard_map/ppermute | solution.py:228
  54.7 12.1 %collective-permute-start.2 = (bf16[2,272,384]{2,1,0:T(8,128)(2,1)S(1)}, bf16[2,272,384]{2,1,0:T(8,128)(2,1)S(1)}, u32[]{:S(2)}, u32[]{:S(2)}) collective-permute-start(bf16[2,272,384]{2,1,0:T(8,128)(2,1)S(1)} %collective-permute-done.refs_2_), channel_id=1, source_target_pairs={{0,1},{1,2},{2,3},{3,4},{4,5},{5,6},{6,7},{7,0},{8,9},{9,10},{10,1... | collective-permute-start | bytes 1253384 | tf_op jit(solution)/shard_map/ppermute | solution.py:227
  60.4 11.2 %collective-permute-start.5 = (bf16[2,272,384]{2,1,0:T(8,128)(2,1)S(1)}, bf16[2,272,384]{2,1,0:T(8,128)(2,1)S(1)}, u32[]{:S(2)}, u32[]{:S(2)}) collective-permute-start(bf16[2,272,384]{2,1,0:T(8,128)(2,1)S(1)} %collective-permute-done.3.refs_5_), channel_id=1, source_target_pairs={{0,7},{1,0},{2,1},{3,2},{4,3},{5,4},{6,5},{7,6},{8,15},{9,8},{10,9... | collective-permute-start | bytes 1253384 | tf_op jit(solution)/shard_map/ppermute | solution.py:228
  66.8 11.2 %copy-start.15 = (bf16[2,272,384]{2,1,0:T(8,128)(2,1)}, bf16[2,272,384]{2,1,0:T(8,128)(2,1)S(1)}, u32[]{:S(2)}) copy-start(bf16[2,272,384]{2,1,0:T(8,128)(2,1)S(1)} %collective-permute-done.2.refs_4_) | copy-start | bytes 1253380
  66.8 11.2 %collective-permute-start.4 = (bf16[2,272,384]{2,1,0:T(8,128)(2,1)S(1)}, bf16[2,272,384]{2,1,0:T(8,128)(2,1)S(1)}, u32[]{:S(2)}, u32[]{:S(2)}) collective-permute-start(bf16[2,272,384]{2,1,0:T(8,128)(2,1)S(1)} %collective-permute-done.2.refs_4_), channel_id=1, source_target_pairs={{0,1},{1,2},{2,3},{3,4},{4,5},{5,6},{6,7},{7,0},{8,9},{9,10},{10,1... | collective-permute-start | bytes 1253384 | tf_op jit(solution)/shard_map/ppermute | solution.py:227
  72.4 8.9 %collective-permute-start.7 = (bf16[1,272,384]{2,1,0:T(8,128)(2,1)S(1)}, bf16[1,272,384]{2,1,0:T(8,128)(2,1)S(1)}, u32[]{:S(2)}, u32[]{:S(2)}) collective-permute-start(bf16[1,272,384]{2,1,0:T(8,128)(2,1)S(1)} %slice.9), channel_id=1, source_target_pairs={{0,7},{1,0},{2,1},{3,2},{4,3},{5,4},{6,5},{7,6},{8,15},{9,8},{10,9... | collective-permute-start | bytes 626696 | tf_op jit(solution)/shard_map/ppermute | solution.py:231
  78.8 8.9 %collective-permute-start.6 = (bf16[1,272,384]{2,1,0:T(8,128)(2,1)S(1)}, bf16[1,272,384]{2,1,0:T(8,128)(2,1)S(1)}, u32[]{:S(2)}, u32[]{:S(2)}) collective-permute-start(bf16[1,272,384]{2,1,0:T(8,128)(2,1)S(1)} %slice.8), channel_id=1, source_target_pairs={{0,1},{1,2},{2,3},{3,4},{4,5},{5,6},{6,7},{7,0},{8,9},{9,10},{10,1... | collective-permute-start | bytes 626696 | tf_op jit(solution)/shard_map/ppermute | solution.py:230
  88.4 1.0 copy-start.3
  89.4 1.0 copy-start.5
  90.4 1.0 copy-start.7
  91.4 1.0 copy-start.10
  92.4 1.0 copy-start.12
  93.4 1.0 copy-start.14
  94.4 1.0 copy-start.16
  100.0 3.7 %copy-start = (bf16[32,576,256]{2,1,0:T(8,128)(2,1)S(1)}, bf16[32,576,256]{2,1,0:T(8,128)(2,1)}, u32[]{:S(2)}) copy-start(bf16[32,576,256]{2,1,0:T(8,128)(2,1)} %all-gather.4.cloned.1.call-done) | copy-start | bytes 28311556
  105.2 8.5 %copy-start.1 = (bf16[32,576,256]{2,1,0:T(8,128)(2,1)S(1)}, bf16[32,576,256]{2,1,0:T(8,128)(2,1)}, u32[]{:S(2)}) copy-start(bf16[32,576,256]{2,1,0:T(8,128)(2,1)} %all-gather.4.cloned.1.call-done) | copy-start | bytes 28311556
  114.3 58.8 %copy-start.8 = (bf16[256,384]{1,0:T(8,128)(2,1)S(1)}, bf16[256,384]{1,0:T(8,128)(2,1)}, u32[]{:S(2)}) copy-start(bf16[256,384]{1,0:T(8,128)(2,1)} %refs_2_.1) | copy-start | bytes 589828
  114.3 58.8 %copy-start.18 = (f32[2,256,128]{2,1,0:T(8,128)S(1)}, f32[2,256,128]{2,1,0:T(8,128)}, u32[]{:S(2)}) copy-start(f32[2,256,128]{2,1,0:T(8,128)} %copy-done.17) | copy-start | bytes 786436
  114.3 58.8 %copy-start.23 = (bf16[16,384]{1,0:T(8,128)(2,1)S(1)}, bf16[16,384]{1,0:T(8,128)(2,1)}, u32[]{:S(2)}) copy-start(bf16[16,384]{1,0:T(8,128)(2,1)} %copy-done.22) | copy-start | bytes 36868
  114.4 9.1 %collective-permute-start.12 = (bf16[1,272,384]{2,1,0:T(8,128)(2,1)S(1)}, bf16[1,272,384]{2,1,0:T(8,128)(2,1)S(1)}, u32[]{:S(2)}, u32[]{:S(2)}) collective-permute-start(bf16[1,272,384]{2,1,0:T(8,128)(2,1)S(1)} %get-tuple-element.26), channel_id=1, source_target_pairs={{0,7},{1,0},{2,1},{3,2},{4,3},{5,4},{6,5},{7,6},{8,15},{9,8},{10,9... | collective-permute-start | bytes 626696 | tf_op jit(solution)/shard_map/ppermute | solution.py:289
  116.4 10.2 %collective-permute-start.8 = (bf16[1,272,384]{2,1,0:T(8,128)(2,1)S(1)}, bf16[1,272,384]{2,1,0:T(8,128)(2,1)S(1)}, u32[]{:S(2)}, u32[]{:S(2)}) collective-permute-start(bf16[1,272,384]{2,1,0:T(8,128)(2,1)S(1)} %get-tuple-element.22), channel_id=1, source_target_pairs={{0,1},{1,2},{2,3},{3,4},{4,5},{5,6},{6,7},{7,0},{8,9},{9,10},{10,1... | collective-permute-start | bytes 626696 | tf_op jit(solution)/shard_map/ppermute | solution.py:288
  123.5 12.2 %collective-permute-start.13 = (bf16[2,272,384]{2,1,0:T(8,128)(2,1)S(1)}, bf16[2,272,384]{2,1,0:T(8,128)(2,1)S(1)}, u32[]{:S(2)}, u32[]{:S(2)}) collective-permute-start(bf16[2,272,384]{2,1,0:T(8,128)(2,1)S(1)} %add_behind.3), channel_id=1, source_target_pairs={{0,7},{1,0},{2,1},{3,2},{4,3},{5,4},{6,5},{7,6},{8,15},{9,8},{10,9... | collective-permute-start | bytes 1253384 | tf_op jit(solution)/shard_map/ppermute | solution.py:289
  126.7 13.0 %collective-permute-start.9 = (bf16[2,272,384]{2,1,0:T(8,128)(2,1)S(1)}, bf16[2,272,384]{2,1,0:T(8,128)(2,1)S(1)}, u32[]{:S(2)}, u32[]{:S(2)}) collective-permute-start(bf16[2,272,384]{2,1,0:T(8,128)(2,1)S(1)} %add_ahead.3), channel_id=1, source_target_pairs={{0,1},{1,2},{2,3},{3,4},{4,5},{5,6},{6,7},{7,0},{8,9},{9,10},{10,1... | collective-permute-start | bytes 1253384 | tf_op jit(solution)/shard_map/ppermute | solution.py:288
  135.8 13.0 %collective-permute-start.14 = (bf16[2,272,384]{2,1,0:T(8,128)(2,1)S(1)}, bf16[2,272,384]{2,1,0:T(8,128)(2,1)S(1)}, u32[]{:S(2)}, u32[]{:S(2)}) collective-permute-start(bf16[2,272,384]{2,1,0:T(8,128)(2,1)S(1)} %add_behind.4), channel_id=1, source_target_pairs={{0,7},{1,0},{2,1},{3,2},{4,3},{5,4},{6,5},{7,6},{8,15},{9,8},{10,9... | collective-permute-start | bytes 1253384 | tf_op jit(solution)/shard_map/ppermute | solution.py:289
  139.9 14.1 %collective-permute-start.10 = (bf16[2,272,384]{2,1,0:T(8,128)(2,1)S(1)}, bf16[2,272,384]{2,1,0:T(8,128)(2,1)S(1)}, u32[]{:S(2)}, u32[]{:S(2)}) collective-permute-start(bf16[2,272,384]{2,1,0:T(8,128)(2,1)S(1)} %add_ahead.4), channel_id=1, source_target_pairs={{0,1},{1,2},{2,3},{3,4},{4,5},{5,6},{6,7},{7,0},{8,9},{9,10},{10,1... | collective-permute-start | bytes 1253384 | tf_op jit(solution)/shard_map/ppermute | solution.py:288
  149.0 10.1 %collective-permute-start.15 = (bf16[2,272,384]{2,1,0:T(8,128)(2,1)S(1)}, bf16[2,272,384]{2,1,0:T(8,128)(2,1)S(1)}, u32[]{:S(2)}, u32[]{:S(2)}) collective-permute-start(bf16[2,272,384]{2,1,0:T(8,128)(2,1)S(1)} %add_behind.5), channel_id=1, source_target_pairs={{0,7},{1,0},{2,1},{3,2},{4,3},{5,4},{6,5},{7,6},{8,15},{9,8},{10,9... | collective-permute-start | bytes 1253384 | tf_op jit(solution)/shard_map/ppermute | solution.py:293
  154.1 11.1 %collective-permute-start.11 = (bf16[2,272,384]{2,1,0:T(8,128)(2,1)S(1)}, bf16[2,272,384]{2,1,0:T(8,128)(2,1)S(1)}, u32[]{:S(2)}, u32[]{:S(2)}) collective-permute-start(bf16[2,272,384]{2,1,0:T(8,128)(2,1)S(1)} %add_ahead.5), channel_id=1, source_target_pairs={{0,1},{1,2},{2,3},{3,4},{4,5},{5,6},{6,7},{7,0},{8,9},{9,10},{10,1... | collective-permute-start | bytes 1253384 | tf_op jit(solution)/shard_map/ppermute | solution.py:292
  165.4 7.7 %collective-permute-start.16 = (bf16[272,384]{1,0:T(8,128)(2,1)S(1)}, bf16[272,384]{1,0:T(8,128)(2,1)S(1)}, u32[]{:S(2)}, u32[]{:S(2)}) collective-permute-start(bf16[272,384]{1,0:T(8,128)(2,1)S(1)} %get-tuple-element.32), channel_id=1, source_target_pairs={{0,8},{8,0},{1,9},{9,1},{2,10},{10,2},{3,11},{11,3},{4,12},{12,4},... | collective-permute-start | bytes 626696 | tf_op jit(solution)/shard_map/ppermute | solution.py:302
  (11 other events, 8.5 us)
Sparse Core Ops, SparseCore 0:
  21.4 64.0 all-gather.3

commit v4 on v3

--- a/solution.py
+++ b/solution.py
@@ -12,7 +12,7 @@
 F32 = jnp.float32
 BF16 = jnp.bfloat16
 VMEM = pl.BlockSpec(memory_space=pltpu.VMEM)
-SMEM = pl.BlockSpec(memory_space=pltpu.SMEM)
+HBM = pl.BlockSpec(memory_space=pltpu.HBM)
 
 
 def params(mib):
@@ -30,23 +30,14 @@
     return total
 
 
-def normalise_kernel(feat_all, z_ref, *refs):
+def normalise_kernel(feat_all, offsets, which, *refs):
     pieces = refs[:-2]
     normed_ref, stat_ref = refs[-2:]
-    z = z_ref[0]
-    zs = 8
+    rows = PATCH
     blocks = []
-    own = pieces[0]
-    for xl in range(2):
-        blocks.append((own, xl, xl * zs + z))
-    for step in range(1, 4):
-        for xl in range(2):
-            blocks.append((pieces[2 * step - 1], xl, xl * zs + lax.rem(z + zs - step, zs)))
-            blocks.append((pieces[2 * step], xl, xl * zs + lax.rem(z + step, zs)))
-    far = lax.rem(z + 4, zs)
-    blocks.append((pieces[7], 0, far))
-    blocks.append((pieces[8], 0, zs + far))
-    rows = PATCH
+    for ref, offset, kinds in zip(pieces, offsets, which):
+        for at, xl in enumerate(kinds):
+            blocks.append((ref, at, xl * 8 + lax.rem(lax.axis_index("z") + offset, 8)))
     total = jnp.zeros((rows, 128), F32)
     for ref, at, _ in blocks:
         total = total + lane_fold(ref[at, :rows, :].astype(F32))
@@ -65,6 +56,11 @@
     stat_ref[1] = jnp.broadcast_to(inv, (rows, 128))
 
 
+def weight_block(w_ref, m, i):
+    third = w_ref.shape[2] // 3
+    return jnp.concatenate([w_ref[c, m, i * third : (i + 1) * third, :] for c in range(2)], axis=0)
+
+
 def norm128(x):
     mean = jnp.mean(x, axis=1, keepdims=True)
     centred = x - mean
@@ -78,25 +74,52 @@
     return inv * (grad_hat - first - x_hat * second)
 
 
-def attention_kernel(normed_ref, w_ref, qk_ref, cot_ref, out_ref, grads_ref, sums_ref, acc):
-    n_m = normed_ref.shape[0]
-    third = w_ref.shape[2] // 3
+def split_sums(sums):
+    high = sums.astype(BF16).astype(F32)
+    return jnp.concatenate([high, sums - high], axis=0).astype(BF16)
+
+
+def join_sums(rows):
+    wide = rows.astype(F32)
+    return wide[:8] + wide[8:]
+
+
+def core_kernel(plan, normed_hbm, w_hbm, qk_hbm, cot_hbm, *refs):
+    out_ref = refs[0]
+    part_refs = refs[1 : 1 + len(plan)]
+    w_ref, normed_ref, qk_ref, cot_ref, acc, grads_ref, sems, small_sems = refs[1 + len(plan) :]
     width = w_ref.shape[3]
     heads = width // HEADSZ
-    acc[...] = jnp.zeros_like(acc)
-
-    def step(m, carry):
-        xh = m // 8
-        y = lax.rem(m, 8)
+    n_m = normed_ref.shape[0]
+
+    def copies(m):
+        x_hi, y = divmod(m, 8)
+        found = [pltpu.make_async_copy(normed_hbm.at[m], normed_ref.at[m], sems.at[m, 2])]
+        for c in range(2):
+            found.append(
+                pltpu.make_async_copy(w_hbm.at[2 * y + c, x_hi], w_ref.at[c, m], sems.at[m, c])
+            )
+        return found
+
+    small = [
+        pltpu.make_async_copy(qk_hbm, qk_ref, small_sems.at[0]),
+        pltpu.make_async_copy(cot_hbm, cot_ref, small_sems.at[1]),
+    ]
+    for m in range(n_m):
+        for copy in copies(m):
+            copy.start()
+    for copy in small:
+        copy.start()
+    for m in range(n_m):
+        for copy in copies(m):
+            copy.wait()
         x = normed_ref[m]
         for i in range(3):
-            w = jnp.concatenate(
-                [w_ref[2 * y + c, xh, i * third : (i + 1) * third, :] for c in range(2)], axis=0
-            )
-            acc[:, i * width : (i + 1) * width] += dot(x, w, 1, 0)
-        return carry
-
-    lax.fori_loop(0, n_m, step, 0)
+            term = dot(x, weight_block(w_ref, m, i), 1, 0)
+            at = slice(i * width, (i + 1) * width)
+            acc[:, at] = term if m == 0 else acc[:, at] + term
+    for copy in small:
+        copy.wait()
     rows = PATCH
     scale = HEADSZ ** (-0.5)
     gain_q = qk_ref[0:1, :]
@@ -130,37 +153,25 @@
             wide = grad.astype(F32)
             first = first + wide * acc[rows : rows + 1, cols[i]]
             second = second + wide * proj[i]
-    sums_ref[...] = jnp.zeros_like(sums_ref)
-    sums_ref[0:1, :rows] = jnp.sum(first, axis=1)[None, :]
-    sums_ref[1:2, :rows] = jnp.sum(second, axis=1)[None, :]
-
-
-def split_sums(sums):
-    high = sums.astype(BF16).astype(F32)
-    return jnp.concatenate([high, sums - high], axis=0).astype(BF16)
-
-
-def join_sums(rows):
-    wide = rows.astype(F32)
-    return wide[:8] + wide[8:]
-
-
-def backward_kernel(plan, z_ref, grads_ref, w_ref, sums_ref, *out_refs):
-    third = w_ref.shape[2] // 3
-    rows = PATCH
-    tail = split_sums(sums_ref[...])
-    for out_ref, places in zip(out_refs, plan):
+    sums = jnp.concatenate(
+        [
+            jnp.sum(first, axis=1)[None, :],
+            jnp.sum(second, axis=1)[None, :],
+            jnp.zeros((6, rows), F32),
+        ],
+        axis=0,
+    )
+    tail = split_sums(sums)
+    for part_ref, places in zip(part_refs, plan):
         for at, (xl, offset) in enumerate(places):
-            y = lax.rem(z_ref[0] + offset, 8)
+            m = xl * 8 + lax.rem(lax.axis_index("z") + offset, 8)
             total = None
             for i in range(3):
-                w = jnp.concatenate(
-                    [w_ref[2 * y + c, xl, i * third : (i + 1) * third, :] for c in range(2)], axis=0
-                )
-                term = dot(grads_ref[i], w, 1, 1)
+                term = dot(grads_ref[i], weight_block(w_ref, m, i), 1, 1)
                 total = term if total is None else total + term
-            out_ref[at, :rows, :] = total.astype(BF16)
-            out_ref[at, rows:, :] = tail
+            part_ref[at, :rows, :] = total.astype(BF16)
+            part_ref[at, rows:, :rows] = tail
+            part_ref[at, rows:, rows:] = jnp.zeros((GAIN_ROWS, total.shape[1] - rows), BF16)
 
 
 def add_kernel(first, got_ref, part_ref, out_ref):
@@ -178,9 +189,10 @@
             out_ref[at] = part_ref[at]
 
 
-def join_kernel(xl_ref, ahead_ref, behind_ref, own_ref, mine_ref, other_ref):
-    rows = PATCH
-    for ref, at in ((mine_ref, xl_ref[0]), (other_ref, 1 - xl_ref[0])):
+def join_kernel(ahead_ref, behind_ref, own_ref, mine_ref, other_ref):
+    rows = PATCH
+    xl = lax.axis_index("xl")
+    for ref, at in ((mine_ref, xl), (other_ref, 1 - xl)):
         refs = (ahead_ref, behind_ref, own_ref)
         total = sum(r[at, :rows, :].astype(F32) for r in refs)
         ref[:rows, :] = total.astype(BF16)
@@ -213,62 +225,59 @@
     rows, feat = tokens.shape
     width = qkv_weight.shape[2]
     feat_all = feat * 16
-    z = lax.axis_index("z").astype(jnp.int32)
-
-    weights = qkv_weight.reshape(-1, width)
-    weights = lax.all_gather(weights, "xh", axis=0)
+
+    weights = lax.all_gather(qkv_weight.reshape(-1, width), "xh", axis=0)
     weights = lax.all_gather(weights, ("y", "c"), axis=0)
 
     gain = jnp.broadcast_to(ln_gain[None, :], (GAIN_ROWS, feat))
-    own = lax.all_gather(jnp.concatenate([tokens, gain], axis=0), "xl", axis=0)
-    pieces = [own]
-    ahead = behind = own
+    toks = lax.all_gather(jnp.concatenate([tokens, gain], axis=0), "xl", axis=0)
+    pieces = [toks]
+    ahead = behind = toks
     for _ in range(3):
         ahead = lax.ppermute(ahead, "z", ring(8, 1))
         behind = lax.ppermute(behind, "z", ring(8, -1))
         pieces += [ahead, behind]
     pieces.append(lax.ppermute(ahead[:1], "z", ring(8, 1)))
     pieces.append(lax.ppermute(behind[1:], "z", ring(8, -1)))
+    places = (0, 7, 1, 6, 2, 5, 3, 4, 4)
+    which = ((0, 1),) * 7 + ((0,), (1,))
 
     normed, stats = pl.pallas_call(
-        lambda *refs: normalise_kernel(feat_all, *refs),
+        lambda *refs: normalise_kernel(feat_all, places, which, *refs),
         out_shape=(
             jax.ShapeDtypeStruct((16, rows + GAIN_ROWS, feat), BF16),
             jax.ShapeDtypeStruct((2, rows, 128), F32),
         ),
-        in_specs=[SMEM] + [VMEM] * len(pieces),
+        in_specs=[VMEM] * len(pieces),
         out_specs=(VMEM, VMEM),
         compiler_params=params(16),
         name="normalise",
-    )(z[None], *pieces)
-
-    attended, grads, sums = pl.pallas_call(
-        attention_kernel,
+    )(*pieces)
+
+    block = (rows + GAIN_ROWS, feat)
+    near = [((0, off), (1, off)) for off in (3, 5, 2, 6, 1, 7, 0)]
+    plan = [((0, 4),), ((1, 4),)] + near
+    attended, ahead, behind, *parts = pl.pallas_call(
+        lambda *refs: core_kernel(plan, *refs),
         out_shape=(
             jax.ShapeDtypeStruct((rows, width), BF16),
-            jax.ShapeDtypeStruct((3, rows, width), BF16),
-            jax.ShapeDtypeStruct((8, feat), F32),
+            *(jax.ShapeDtypeStruct((len(p),) + block, BF16) for p in plan),
         ),
-        in_specs=[VMEM] * 4,
-        out_specs=(VMEM,) * 3,
-        scratch_shapes=[pltpu.VMEM((rows + GAIN_ROWS, 3 * width), F32)],
-        compiler_params=params(16),
-        name="attention",
+        in_specs=[HBM] * 4,
+        out_specs=(VMEM,) * (1 + len(plan)),
+        scratch_shapes=[
+            pltpu.VMEM((2, 16) + weights.shape[2:], BF16),
+            pltpu.VMEM(normed.shape, BF16),
+            pltpu.VMEM(qk_gain.shape, F32),
+            pltpu.VMEM(cotangent.shape, BF16),
+            pltpu.VMEM((rows + GAIN_ROWS, 3 * width), F32),
+            pltpu.VMEM((3, rows, width), BF16),
+            pltpu.SemaphoreType.DMA((16, 3)),
+            pltpu.SemaphoreType.DMA((2,)),
+        ],
+        compiler_params=params(50),
+        name="core",
     )(normed, weights, qk_gain, cotangent)
-
-    block = (rows + GAIN_ROWS, feat)
-
-    def backward(plan, name):
-        flops = 2 * rows * feat * 3 * width * sum(len(places) for places in plan)
-        return pl.pallas_call(
-            lambda *refs: backward_kernel(plan, *refs),
-            out_shape=tuple(jax.ShapeDtypeStruct((len(p),) + block, BF16) for p in plan),
-            in_specs=[SMEM] + [VMEM] * 3,
-            out_specs=(VMEM,) * len(plan),
-            compiler_params=params(16),
-            cost_estimate=pl.CostEstimate(flops=flops, bytes_accessed=2 * 2**20, transcendentals=0),
-            name=name,
-        )(z[None], grads, weights, sums)
 
     def add(got, part, first, name):
         return pl.pallas_call(
@@ -281,9 +290,6 @@
             name=name,
         )(got, part)
 
-    ahead, behind = backward((((0, 4),), ((1, 4),)), "backward_far")
-    near = [((0, off), (1, off)) for off in (3, 5, 2, 6, 1, 7, 0)]
-    parts = backward(tuple(near), "backward_near")
     for step in range(3):
         ahead = lax.ppermute(ahead, "z", ring(8, 1))
         behind = lax.ppermute(behind, "z", ring(8, -1))
@@ -294,11 +300,11 @@
     mine, other = pl.pallas_call(
         join_kernel,
         out_shape=(jax.ShapeDtypeStruct(block, BF16),) * 2,
-        in_specs=[SMEM] + [VMEM] * 3,
+        in_specs=[VMEM] * 3,
         out_specs=(VMEM, VMEM),
         compiler_params=params(16),
         name="join",
-    )(lax.axis_index("xl").astype(jnp.int32)[None], ahead, behind, parts[6])
+    )(ahead, behind, parts[6])
     other = lax.ppermute(other, "xl", ring(2, 1))
     grad_tokens = pl.pallas_call(
         lambda *refs: final_kernel(feat_all, *refs),

time: 182 us -> 175 us (0.962)
  the two profiles are of different devices: /device:TPU:40 before, /device:TPU:6 now
where the time goes in v4:
time: 175 us; the launch traced here: 174 us
  starting transfers between devices  66.1 us (38%)
  waiting for transfers between devices  50.7 us (29%)
  blocking collectives  19.9 us (11%)
  Pallas kernels  17.7 us (10%)
  between operations  14.3 us (8%)
  local copies, waits for them, and re-layouts  4.05 us (2%)
    ppermute x7, starting transfers between devices, per_device(): behind = lax.ppermute(behind, 'z', ring(8, -1))  42.3 us
    ppermute x7, waiting for transfers between devices, per_device(): behind = lax.ppermute(behind, 'z', ring(8, -1))  33.3 us
    ppermute x7, starting transfers between devices, per_device(): ahead = lax.ppermute(ahead, 'z', ring(8, 1))  13.6 us
    pallas_call x1, Pallas kernels, per_device(): pl.pallas_call(lambda *refs: core_kernel(plan, *refs), out_shape=(jax.Sha...  13 us
    all_gather x1, blocking collectives, per_device(): weights = lax.all_gather(qkv_weight.reshape(-1, width), 'xh', axis=0)  12.5 us
    all_gather x1, blocking collectives, per_device(): toks = lax.all_gather(jnp.concatenate([tokens, gain], axis=0), 'xl', axis=0)  7.44 us
    ppermute x1, waiting for transfers between devices, per_device(): pieces.append(lax.ppermute(ahead[:1], 'z', ring(8, 1)))  5.65 us
    ppermute x1, starting transfers between devices, per_device(): pieces.append(lax.ppermute(behind[1:], 'z', ring(8, -1)))  5.6 us
  transfers between devices with their start and end apart: 18, of which 11 were waited for; matrix products, arithmetic and copies ran while one was open for 1% of the time, Pallas kernels for 2%

profile of v4, /device:TPU:6, one launch (start us, length us, event | category | flops | bytes accessed | tf_op | source)
XLA Modules:
  0.0 173.7 jit_solution(10609875596752917779)
XLA Ops:
  7.2 12.5 %all_gather.17 = bf16[2,576,256]{2,1,0:T(8,128)(2,1)} all-gather(bf16[1,576,256]{2,1,0:T(8,128)(2,1)} %bitcast.7), channel_id=1, replica_groups=mesh['xh'=2,'y'=8,'c'=2,'xl'=2,'z'=8] {'xh'}, dimensions={0}, use_global_device_ids=true | all-gather | bytes 884736 | tf_op jit(solution)/shard_map/all_gather | solution.py:229
  21.3 7.4 %all-gather = bf16[544,384]{1,0:T(8,128)(2,1)S(1)} all-gather(bf16[272,384]{1,0:T(8,128)(2,1)S(1)} %pad_maximum_fusion), channel_id=2, replica_groups=mesh['xh'=2,'y'=8,'c'=2,'xl'=2,'z'=8] {'xl'}, dimensions={0}, use_global_device_ids=true | all-gather | bytes 626688 | tf_op jit(solution)/shard_map/all_gather | solution.py:233
  28.8 10.5 %collective-permute-start.1 = (bf16[2,272,384]{2,1,0:T(8,128)(2,1)S(1)}, bf16[2,272,384]{2,1,0:T(8,128)(2,1)S(1)}, u32[]{:S(2)}, u32[]{:S(2)}) collective-permute-start(bf16[2,272,384]{2,1,0:T(8,128)(2,1)S(1)} %bitcast.3), channel_id=1, source_target_pairs={{0,7},{1,0},{2,1},{3,2},{4,3},{5,4},{6,5},{7,6},{8,15},{9,8},{10,9... | collective-permute-start | bytes 1253384 | tf_op jit(solution)/shard_map/ppermute | solution.py:238
  39.3 1.9 %collective-permute-start = (bf16[2,272,384]{2,1,0:T(8,128)(2,1)S(1)}, bf16[2,272,384]{2,1,0:T(8,128)(2,1)S(1)}, u32[]{:S(2)}, u32[]{:S(2)}) collective-permute-start(bf16[2,272,384]{2,1,0:T(8,128)(2,1)S(1)} %bitcast.4), channel_id=1, source_target_pairs={{0,1},{1,2},{2,3},{3,4},{4,5},{5,6},{6,7},{7,0},{8,9},{9,10},{10,1... | collective-permute-start | bytes 1253384 | tf_op jit(solution)/shard_map/ppermute | solution.py:237
  41.2 5.5 %collective-permute-done.1.refs_2_ = bf16[2,272,384]{2,1,0:T(8,128)(2,1)S(1)} collective-permute-done((bf16[2,272,384]{2,1,0:T(8,128)(2,1)S(1)}, bf16[2,272,384]{2,1,0:T(8,128)(2,1)S(1)}, u32[]{:S(2)}, u32[]{:S(2)}) %collective-permute-start.1) | collective-permute-done | bytes 417824 | tf_op jit(solution)/shard_map/ppermute | solution.py:238
  46.7 5.6 %collective-permute-start.3 = (bf16[2,272,384]{2,1,0:T(8,128)(2,1)S(1)}, bf16[2,272,384]{2,1,0:T(8,128)(2,1)S(1)}, u32[]{:S(2)}, u32[]{:S(2)}) collective-permute-start(bf16[2,272,384]{2,1,0:T(8,128)(2,1)S(1)} %collective-permute-done.1.refs_2_), channel_id=1, source_target_pairs={{0,7},{1,0},{2,1},{3,2},{4,3},{5,4},{6,5},{7,6},{8,15},{9,8},{10,9... | collective-permute-start | bytes 1253384 | tf_op jit(solution)/shard_map/ppermute | solution.py:238
  52.3 1.9 %collective-permute-start.2 = (bf16[2,272,384]{2,1,0:T(8,128)(2,1)S(1)}, bf16[2,272,384]{2,1,0:T(8,128)(2,1)S(1)}, u32[]{:S(2)}, u32[]{:S(2)}) collective-permute-start(bf16[2,272,384]{2,1,0:T(8,128)(2,1)S(1)} %collective-permute-done.refs_1_), channel_id=1, source_target_pairs={{0,1},{1,2},{2,3},{3,4},{4,5},{5,6},{6,7},{7,0},{8,9},{9,10},{10,1... | collective-permute-start | bytes 1253384 | tf_op jit(solution)/shard_map/ppermute | solution.py:237
  54.3 4.6 %collective-permute-done.3.refs_4_ = bf16[2,272,384]{2,1,0:T(8,128)(2,1)S(1)} collective-permute-done((bf16[2,272,384]{2,1,0:T(8,128)(2,1)S(1)}, bf16[2,272,384]{2,1,0:T(8,128)(2,1)S(1)}, u32[]{:S(2)}, u32[]{:S(2)}) %collective-permute-start.3) | collective-permute-done | bytes 417824 | tf_op jit(solution)/shard_map/ppermute | solution.py:238
  58.9 5.6 %collective-permute-start.5 = (bf16[2,272,384]{2,1,0:T(8,128)(2,1)S(1)}, bf16[2,272,384]{2,1,0:T(8,128)(2,1)S(1)}, u32[]{:S(2)}, u32[]{:S(2)}) collective-permute-start(bf16[2,272,384]{2,1,0:T(8,128)(2,1)S(1)} %collective-permute-done.3.refs_4_), channel_id=1, source_target_pairs={{0,7},{1,0},{2,1},{3,2},{4,3},{5,4},{6,5},{7,6},{8,15},{9,8},{10,9... | collective-permute-start | bytes 1253384 | tf_op jit(solution)/shard_map/ppermute | solution.py:238
  64.5 1.9 %collective-permute-start.4 = (bf16[2,272,384]{2,1,0:T(8,128)(2,1)S(1)}, bf16[2,272,384]{2,1,0:T(8,128)(2,1)S(1)}, u32[]{:S(2)}, u32[]{:S(2)}) collective-permute-start(bf16[2,272,384]{2,1,0:T(8,128)(2,1)S(1)} %collective-permute-done.2.refs_3_), channel_id=1, source_target_pairs={{0,1},{1,2},{2,3},{3,4},{4,5},{5,6},{6,7},{7,0},{8,9},{9,10},{10,1... | collective-permute-start | bytes 1253384 | tf_op jit(solution)/shard_map/ppermute | solution.py:237
  66.4 3.8 %collective-permute-done.5.refs_6_ = bf16[2,272,384]{2,1,0:T(8,128)(2,1)S(1)} collective-permute-done((bf16[2,272,384]{2,1,0:T(8,128)(2,1)S(1)}, bf16[2,272,384]{2,1,0:T(8,128)(2,1)S(1)}, u32[]{:S(2)}, u32[]{:S(2)}) %collective-permute-start.5) | collective-permute-done | bytes 417824 | tf_op jit(solution)/shard_map/ppermute | solution.py:238
  70.3 5.6 %collective-permute-start.7 = (bf16[1,272,384]{2,1,0:T(8,128)(2,1)S(1)}, bf16[1,272,384]{2,1,0:T(8,128)(2,1)S(1)}, u32[]{:S(2)}, u32[]{:S(2)}) collective-permute-start(bf16[1,272,384]{2,1,0:T(8,128)(2,1)S(1)} %slice.9), channel_id=1, source_target_pairs={{0,7},{1,0},{2,1},{3,2},{4,3},{5,4},{6,5},{7,6},{8,15},{9,8},{10,9... | collective-permute-start | bytes 626696 | tf_op jit(solution)/shard_map/ppermute | solution.py:241
  75.9 1.9 %collective-permute-start.6 = (bf16[1,272,384]{2,1,0:T(8,128)(2,1)S(1)}, bf16[1,272,384]{2,1,0:T(8,128)(2,1)S(1)}, u32[]{:S(2)}, u32[]{:S(2)}) collective-permute-start(bf16[1,272,384]{2,1,0:T(8,128)(2,1)S(1)} %slice.8), channel_id=1, source_target_pairs={{0,1},{1,2},{2,3},{3,4},{4,5},{5,6},{6,7},{7,0},{8,9},{9,10},{10,1... | collective-permute-start | bytes 626696 | tf_op jit(solution)/shard_map/ppermute | solution.py:240
  79.2 5.6 %collective-permute-done.6.refs_7_ = bf16[1,272,384]{2,1,0:T(8,128)(2,1)S(1)} collective-permute-done((bf16[1,272,384]{2,1,0:T(8,128)(2,1)S(1)}, bf16[1,272,384]{2,1,0:T(8,128)(2,1)S(1)}, u32[]{:S(2)}, u32[]{:S(2)}) %collective-permute-start.6) | collective-permute-done | bytes 208928 | tf_op jit(solution)/shard_map/ppermute | solution.py:240
  84.8 2.8 %normalise.1 = (bf16[16,272,384]{2,1,0:T(8,128)(2,1)S(1)}, f32[2,256,128]{2,1,0:T(8,128)S(1)}) custom-call(bf16[2,272,384]{2,1,0:T(8,128)(2,1)S(1)} %bitcast.5, bf16[2,272,384]{2,1,0:T(8,128)(2,1)S(1)} %collective-permute-done.refs_1_, bf16[2,272,384]{2,1,0:T(8,128)(2,1)S(1)} %collective-permute-done.1.refs_2_, ...), custom_call_target="tpu_custom_call" | custom-call | tf_op jit(solution)/shard_map/normalise/pallas_call | solution.py:245
  87.7 1.7 copy-done
  91.0 13.0 %core.1 = (bf16[256,256]{1,0:T(8,128)(2,1)}, bf16[1,272,384]{2,1,0:T(8,128)(2,1)S(1)}, bf16[1,272,384]{2,1,0:T(8,128)(2,1)S(1)}, bf16[2,272,384]{2,1,0:T(8,128)(...) custom-call(bf16[16,272,384]{2,1,0:T(8,128)(2,1)} %copy-done, ...), custom_call_target="tpu_custom_call" | custom-call | tf_op jit(solution)/shard_map/core/pallas_call | solution.py:260
  104.1 3.8 %collective-permute-start.12 = (bf16[1,272,384]{2,1,0:T(8,128)(2,1)S(1)}, bf16[1,272,384]{2,1,0:T(8,128)(2,1)S(1)}, u32[]{:S(2)}, u32[]{:S(2)}) collective-permute-start(bf16[1,272,384]{2,1,0:T(8,128)(2,1)S(1)} %get-tuple-element.22), channel_id=1, source_target_pairs={{0,7},{1,0},{2,1},{3,2},{4,3},{5,4},{6,5},{7,6},{8,15},{9,8},{10,9... | collective-permute-start | bytes 626696 | tf_op jit(solution)/shard_map/ppermute | solution.py:295
  107.9 2.0 %collective-permute-start.8 = (bf16[1,272,384]{2,1,0:T(8,128)(2,1)S(1)}, bf16[1,272,384]{2,1,0:T(8,128)(2,1)S(1)}, u32[]{:S(2)}, u32[]{:S(2)}) collective-permute-start(bf16[1,272,384]{2,1,0:T(8,128)(2,1)S(1)} %get-tuple-element.18), channel_id=1, source_target_pairs={{0,1},{1,2},{2,3},{3,4},{4,5},{5,6},{6,7},{7,0},{8,9},{9,10},{10,1... | collective-permute-start | bytes 626696 | tf_op jit(solution)/shard_map/ppermute | solution.py:294
  109.9 2.8 %collective-permute-done.12.refs_0_ = bf16[1,272,384]{2,1,0:T(8,128)(2,1)S(1)} collective-permute-done((bf16[1,272,384]{2,1,0:T(8,128)(2,1)S(1)}, bf16[1,272,384]{2,1,0:T(8,128)(2,1)S(1)}, u32[]{:S(2)}, u32[]{:S(2)}) %collective-permute-start.12) | collective-permute-done | bytes 208928 | tf_op jit(solution)/shard_map/ppermute | solution.py:295
  112.8 5.6 %collective-permute-start.13 = (bf16[2,272,384]{2,1,0:T(8,128)(2,1)S(1)}, bf16[2,272,384]{2,1,0:T(8,128)(2,1)S(1)}, u32[]{:S(2)}, u32[]{:S(2)}) collective-permute-start(bf16[2,272,384]{2,1,0:T(8,128)(2,1)S(1)} %add_behind.3), channel_id=1, source_target_pairs={{0,7},{1,0},{2,1},{3,2},{4,3},{5,4},{6,5},{7,6},{8,15},{9,8},{10,9... | collective-permute-start | bytes 1253384 | tf_op jit(solution)/shard_map/ppermute | solution.py:295
  118.5 1.9 %collective-permute-start.9 = (bf16[2,272,384]{2,1,0:T(8,128)(2,1)S(1)}, bf16[2,272,384]{2,1,0:T(8,128)(2,1)S(1)}, u32[]{:S(2)}, u32[]{:S(2)}) collective-permute-start(bf16[2,272,384]{2,1,0:T(8,128)(2,1)S(1)} %add_ahead.3), channel_id=1, source_target_pairs={{0,1},{1,2},{2,3},{3,4},{4,5},{5,6},{6,7},{7,0},{8,9},{9,10},{10,1... | collective-permute-start | bytes 1253384 | tf_op jit(solution)/shard_map/ppermute | solution.py:294
  120.4 6.5 %collective-permute-done.13.refs_0_ = bf16[2,272,384]{2,1,0:T(8,128)(2,1)S(1)} collective-permute-done((bf16[2,272,384]{2,1,0:T(8,128)(2,1)S(1)}, bf16[2,272,384]{2,1,0:T(8,128)(2,1)S(1)}, u32[]{:S(2)}, u32[]{:S(2)}) %collective-permute-start.13) | collective-permute-done | bytes 417824 | tf_op jit(solution)/shard_map/ppermute | solution.py:295
  127.0 5.6 %collective-permute-start.14 = (bf16[2,272,384]{2,1,0:T(8,128)(2,1)S(1)}, bf16[2,272,384]{2,1,0:T(8,128)(2,1)S(1)}, u32[]{:S(2)}, u32[]{:S(2)}) collective-permute-start(bf16[2,272,384]{2,1,0:T(8,128)(2,1)S(1)} %add_behind.4), channel_id=1, source_target_pairs={{0,7},{1,0},{2,1},{3,2},{4,3},{5,4},{6,5},{7,6},{8,15},{9,8},{10,9... | collective-permute-start | bytes 1253384 | tf_op jit(solution)/shard_map/ppermute | solution.py:295
  132.7 1.9 %collective-permute-start.10 = (bf16[2,272,384]{2,1,0:T(8,128)(2,1)S(1)}, bf16[2,272,384]{2,1,0:T(8,128)(2,1)S(1)}, u32[]{:S(2)}, u32[]{:S(2)}) collective-permute-start(bf16[2,272,384]{2,1,0:T(8,128)(2,1)S(1)} %add_ahead.4), channel_id=1, source_target_pairs={{0,1},{1,2},{2,3},{3,4},{4,5},{5,6},{6,7},{7,0},{8,9},{9,10},{10,1... | collective-permute-start | bytes 1253384 | tf_op jit(solution)/shard_map/ppermute | solution.py:294
  134.7 5.5 %collective-permute-done.14.refs_0_ = bf16[2,272,384]{2,1,0:T(8,128)(2,1)S(1)} collective-permute-done((bf16[2,272,384]{2,1,0:T(8,128)(2,1)S(1)}, bf16[2,272,384]{2,1,0:T(8,128)(2,1)S(1)}, u32[]{:S(2)}, u32[]{:S(2)}) %collective-permute-start.14) | collective-permute-done | bytes 417824 | tf_op jit(solution)/shard_map/ppermute | solution.py:295
  140.3 5.6 %collective-permute-start.15 = (bf16[2,272,384]{2,1,0:T(8,128)(2,1)S(1)}, bf16[2,272,384]{2,1,0:T(8,128)(2,1)S(1)}, u32[]{:S(2)}, u32[]{:S(2)}) collective-permute-start(bf16[2,272,384]{2,1,0:T(8,128)(2,1)S(1)} %add_behind.5), channel_id=1, source_target_pairs={{0,7},{1,0},{2,1},{3,2},{4,3},{5,4},{6,5},{7,6},{8,15},{9,8},{10,9... | collective-permute-start | bytes 1253384 | tf_op jit(solution)/shard_map/ppermute | solution.py:299
  146.0 1.9 %collective-permute-start.11 = (bf16[2,272,384]{2,1,0:T(8,128)(2,1)S(1)}, bf16[2,272,384]{2,1,0:T(8,128)(2,1)S(1)}, u32[]{:S(2)}, u32[]{:S(2)}) collective-permute-start(bf16[2,272,384]{2,1,0:T(8,128)(2,1)S(1)} %add_ahead.5), channel_id=1, source_target_pairs={{0,1},{1,2},{2,3},{3,4},{4,5},{5,6},{6,7},{7,0},{8,9},{9,10},{10,1... | collective-permute-start | bytes 1253384 | tf_op jit(solution)/shard_map/ppermute | solution.py:298
  147.9 4.6 %collective-permute-done.15.behind_ref = bf16[2,272,384]{2,1,0:T(8,128)(2,1)S(1)} collective-permute-done((bf16[2,272,384]{2,1,0:T(8,128)(2,1)S(1)}, bf16[2,272,384]{2,1,0:T(8,128)(2,1)S(1)}, u32[]{:S(2)}, u32[]{:S(2)}) %collective-permute-start.15) | collective-permute-done | bytes 417824 | tf_op jit(solution)/shard_map/ppermute | solution.py:299
  152.5 5.5 %collective-permute-done.11.ahead_ref = bf16[2,272,384]{2,1,0:T(8,128)(2,1)S(1)} collective-permute-done((bf16[2,272,384]{2,1,0:T(8,128)(2,1)S(1)}, bf16[2,272,384]{2,1,0:T(8,128)(2,1)S(1)}, u32[]{:S(2)}, u32[]{:S(2)}) %collective-permute-start.11) | collective-permute-done | bytes 417824 | tf_op jit(solution)/shard_map/ppermute | solution.py:298
  158.2 2.7 %collective-permute-start.16 = (bf16[272,384]{1,0:T(8,128)(2,1)S(1)}, bf16[272,384]{1,0:T(8,128)(2,1)S(1)}, u32[]{:S(2)}, u32[]{:S(2)}) collective-permute-start(bf16[272,384]{1,0:T(8,128)(2,1)S(1)} %get-tuple-element.28), channel_id=1, source_target_pairs={{0,8},{8,0},{1,9},{9,1},{2,10},{10,2},{3,11},{11,3},{4,12},{12,4},... | collective-permute-start | bytes 626696 | tf_op jit(solution)/shard_map/ppermute | solution.py:308
  160.9 5.0 %collective-permute-done.16.refs_1_ = bf16[272,384]{1,0:T(8,128)(2,1)S(1)} collective-permute-done((bf16[272,384]{1,0:T(8,128)(2,1)S(1)}, bf16[272,384]{1,0:T(8,128)(2,1)S(1)}, u32[]{:S(2)}, u32[]{:S(2)}) %collective-permute-start.16) | collective-permute-done | bytes 208928 | tf_op jit(solution)/shard_map/ppermute | solution.py:308
  (29 shorter events, 6.4 us)
Async XLA Ops:
  7.2 82.3 %all-gather.4.cloned.1.call-start = ((), (), s32[]{:S(2)}) async-start(), calls=%async_computation | async-start | bytes 10027008 | tf_op jit(solution)/shard_map/all_gather | solution.py:230
  28.8 17.9 %collective-permute-start.1 = (bf16[2,272,384]{2,1,0:T(8,128)(2,1)S(1)}, bf16[2,272,384]{2,1,0:T(8,128)(2,1)S(1)}, u32[]{:S(2)}, u32[]{:S(2)}) collective-permute-start(bf16[2,272,384]{2,1,0:T(8,128)(2,1)S(1)} %bitcast.3), channel_id=1, source_target_pairs={{0,7},{1,0},{2,1},{3,2},{4,3},{5,4},{6,5},{7,6},{8,15},{9,8},{10,9... | collective-permute-start | bytes 1253384 | tf_op jit(solution)/shard_map/ppermute | solution.py:238
  39.3 13.0 %collective-permute-start = (bf16[2,272,384]{2,1,0:T(8,128)(2,1)S(1)}, bf16[2,272,384]{2,1,0:T(8,128)(2,1)S(1)}, u32[]{:S(2)}, u32[]{:S(2)}) collective-permute-start(bf16[2,272,384]{2,1,0:T(8,128)(2,1)S(1)} %bitcast.4), channel_id=1, source_target_pairs={{0,1},{1,2},{2,3},{3,4},{4,5},{5,6},{6,7},{7,0},{8,9},{9,10},{10,1... | collective-permute-start | bytes 1253384 | tf_op jit(solution)/shard_map/ppermute | solution.py:237
  46.7 12.2 %collective-permute-start.3 = (bf16[2,272,384]{2,1,0:T(8,128)(2,1)S(1)}, bf16[2,272,384]{2,1,0:T(8,128)(2,1)S(1)}, u32[]{:S(2)}, u32[]{:S(2)}) collective-permute-start(bf16[2,272,384]{2,1,0:T(8,128)(2,1)S(1)} %collective-permute-done.1.refs_2_), channel_id=1, source_target_pairs={{0,7},{1,0},{2,1},{3,2},{4,3},{5,4},{6,5},{7,6},{8,15},{9,8},{10,9... | collective-permute-start | bytes 1253384 | tf_op jit(solution)/shard_map/ppermute | solution.py:238
  52.3 12.2 %collective-permute-start.2 = (bf16[2,272,384]{2,1,0:T(8,128)(2,1)S(1)}, bf16[2,272,384]{2,1,0:T(8,128)(2,1)S(1)}, u32[]{:S(2)}, u32[]{:S(2)}) collective-permute-start(bf16[2,272,384]{2,1,0:T(8,128)(2,1)S(1)} %collective-permute-done.refs_1_), channel_id=1, source_target_pairs={{0,1},{1,2},{2,3},{3,4},{4,5},{5,6},{6,7},{7,0},{8,9},{9,10},{10,1... | collective-permute-start | bytes 1253384 | tf_op jit(solution)/shard_map/ppermute | solution.py:237
  58.9 11.4 %collective-permute-start.5 = (bf16[2,272,384]{2,1,0:T(8,128)(2,1)S(1)}, bf16[2,272,384]{2,1,0:T(8,128)(2,1)S(1)}, u32[]{:S(2)}, u32[]{:S(2)}) collective-permute-start(bf16[2,272,384]{2,1,0:T(8,128)(2,1)S(1)} %collective-permute-done.3.refs_4_), channel_id=1, source_target_pairs={{0,7},{1,0},{2,1},{3,2},{4,3},{5,4},{6,5},{7,6},{8,15},{9,8},{10,9... | collective-permute-start | bytes 1253384 | tf_op jit(solution)/shard_map/ppermute | solution.py:238
  64.5 11.4 %collective-permute-start.4 = (bf16[2,272,384]{2,1,0:T(8,128)(2,1)S(1)}, bf16[2,272,384]{2,1,0:T(8,128)(2,1)S(1)}, u32[]{:S(2)}, u32[]{:S(2)}) collective-permute-start(bf16[2,272,384]{2,1,0:T(8,128)(2,1)S(1)} %collective-permute-done.2.refs_3_), channel_id=1, source_target_pairs={{0,1},{1,2},{2,3},{3,4},{4,5},{5,6},{6,7},{7,0},{8,9},{9,10},{10,1... | collective-permute-start | bytes 1253384 | tf_op jit(solution)/shard_map/ppermute | solution.py:237
  70.3 8.9 %collective-permute-start.7 = (bf16[1,272,384]{2,1,0:T(8,128)(2,1)S(1)}, bf16[1,272,384]{2,1,0:T(8,128)(2,1)S(1)}, u32[]{:S(2)}, u32[]{:S(2)}) collective-permute-start(bf16[1,272,384]{2,1,0:T(8,128)(2,1)S(1)} %slice.9), channel_id=1, source_target_pairs={{0,7},{1,0},{2,1},{3,2},{4,3},{5,4},{6,5},{7,6},{8,15},{9,8},{10,9... | collective-permute-start | bytes 626696 | tf_op jit(solution)/shard_map/ppermute | solution.py:241
  75.9 8.9 %collective-permute-start.6 = (bf16[1,272,384]{2,1,0:T(8,128)(2,1)S(1)}, bf16[1,272,384]{2,1,0:T(8,128)(2,1)S(1)}, u32[]{:S(2)}, u32[]{:S(2)}) collective-permute-start(bf16[1,272,384]{2,1,0:T(8,128)(2,1)S(1)} %slice.8), channel_id=1, source_target_pairs={{0,1},{1,2},{2,3},{3,4},{4,5},{5,6},{6,7},{7,0},{8,9},{9,10},{10,1... | collective-permute-start | bytes 626696 | tf_op jit(solution)/shard_map/ppermute | solution.py:240
  87.7 1.7 %copy-start = (bf16[16,272,384]{2,1,0:T(8,128)(2,1)}, bf16[16,272,384]{2,1,0:T(8,128)(2,1)S(1)}, u32[]{:S(2)}) copy-start(bf16[16,272,384]{2,1,0:T(8,128)(2,1)S(1)} %get-tuple-element.16.refs_0_) | copy-start | bytes 10027012
  89.4 0.9 copy-start.2
  90.3 0.7 copy-start.3
  91.0 74.9 %copy-start.1 = (bf16[256,384]{1,0:T(8,128)(2,1)S(1)}, bf16[256,384]{1,0:T(8,128)(2,1)}, u32[]{:S(2)}) copy-start(bf16[256,384]{1,0:T(8,128)(2,1)} %refs_2_.3) | copy-start | bytes 589828
  104.1 8.6 %collective-permute-start.12 = (bf16[1,272,384]{2,1,0:T(8,128)(2,1)S(1)}, bf16[1,272,384]{2,1,0:T(8,128)(2,1)S(1)}, u32[]{:S(2)}, u32[]{:S(2)}) collective-permute-start(bf16[1,272,384]{2,1,0:T(8,128)(2,1)S(1)} %get-tuple-element.22), channel_id=1, source_target_pairs={{0,7},{1,0},{2,1},{3,2},{4,3},{5,4},{6,5},{7,6},{8,15},{9,8},{10,9... | collective-permute-start | bytes 626696 | tf_op jit(solution)/shard_map/ppermute | solution.py:295
  107.9 10.5 %collective-permute-start.8 = (bf16[1,272,384]{2,1,0:T(8,128)(2,1)S(1)}, bf16[1,272,384]{2,1,0:T(8,128)(2,1)S(1)}, u32[]{:S(2)}, u32[]{:S(2)}) collective-permute-start(bf16[1,272,384]{2,1,0:T(8,128)(2,1)S(1)} %get-tuple-element.18), channel_id=1, source_target_pairs={{0,1},{1,2},{2,3},{3,4},{4,5},{5,6},{6,7},{7,0},{8,9},{9,10},{10,1... | collective-permute-start | bytes 626696 | tf_op jit(solution)/shard_map/ppermute | solution.py:294
  112.8 14.1 %collective-permute-start.13 = (bf16[2,272,384]{2,1,0:T(8,128)(2,1)S(1)}, bf16[2,272,384]{2,1,0:T(8,128)(2,1)S(1)}, u32[]{:S(2)}, u32[]{:S(2)}) collective-permute-start(bf16[2,272,384]{2,1,0:T(8,128)(2,1)S(1)} %add_behind.3), channel_id=1, source_target_pairs={{0,7},{1,0},{2,1},{3,2},{4,3},{5,4},{6,5},{7,6},{8,15},{9,8},{10,9... | collective-permute-start | bytes 1253384 | tf_op jit(solution)/shard_map/ppermute | solution.py:295
  118.5 14.1 %collective-permute-start.9 = (bf16[2,272,384]{2,1,0:T(8,128)(2,1)S(1)}, bf16[2,272,384]{2,1,0:T(8,128)(2,1)S(1)}, u32[]{:S(2)}, u32[]{:S(2)}) collective-permute-start(bf16[2,272,384]{2,1,0:T(8,128)(2,1)S(1)} %add_ahead.3), channel_id=1, source_target_pairs={{0,1},{1,2},{2,3},{3,4},{4,5},{5,6},{6,7},{7,0},{8,9},{9,10},{10,1... | collective-permute-start | bytes 1253384 | tf_op jit(solution)/shard_map/ppermute | solution.py:294
  127.0 13.2 %collective-permute-start.14 = (bf16[2,272,384]{2,1,0:T(8,128)(2,1)S(1)}, bf16[2,272,384]{2,1,0:T(8,128)(2,1)S(1)}, u32[]{:S(2)}, u32[]{:S(2)}) collective-permute-start(bf16[2,272,384]{2,1,0:T(8,128)(2,1)S(1)} %add_behind.4), channel_id=1, source_target_pairs={{0,7},{1,0},{2,1},{3,2},{4,3},{5,4},{6,5},{7,6},{8,15},{9,8},{10,9... | collective-permute-start | bytes 1253384 | tf_op jit(solution)/shard_map/ppermute | solution.py:295
  132.7 13.2 %collective-permute-start.10 = (bf16[2,272,384]{2,1,0:T(8,128)(2,1)S(1)}, bf16[2,272,384]{2,1,0:T(8,128)(2,1)S(1)}, u32[]{:S(2)}, u32[]{:S(2)}) collective-permute-start(bf16[2,272,384]{2,1,0:T(8,128)(2,1)S(1)} %add_ahead.4), channel_id=1, source_target_pairs={{0,1},{1,2},{2,3},{3,4},{4,5},{5,6},{6,7},{7,0},{8,9},{9,10},{10,1... | collective-permute-start | bytes 1253384 | tf_op jit(solution)/shard_map/ppermute | solution.py:294
  140.3 12.3 %collective-permute-start.15 = (bf16[2,272,384]{2,1,0:T(8,128)(2,1)S(1)}, bf16[2,272,384]{2,1,0:T(8,128)(2,1)S(1)}, u32[]{:S(2)}, u32[]{:S(2)}) collective-permute-start(bf16[2,272,384]{2,1,0:T(8,128)(2,1)S(1)} %add_behind.5), channel_id=1, source_target_pairs={{0,7},{1,0},{2,1},{3,2},{4,3},{5,4},{6,5},{7,6},{8,15},{9,8},{10,9... | collective-permute-start | bytes 1253384 | tf_op jit(solution)/shard_map/ppermute | solution.py:299
  146.0 12.0 %collective-permute-start.11 = (bf16[2,272,384]{2,1,0:T(8,128)(2,1)S(1)}, bf16[2,272,384]{2,1,0:T(8,128)(2,1)S(1)}, u32[]{:S(2)}, u32[]{:S(2)}) collective-permute-start(bf16[2,272,384]{2,1,0:T(8,128)(2,1)S(1)} %add_ahead.5), channel_id=1, source_target_pairs={{0,1},{1,2},{2,3},{3,4},{4,5},{5,6},{6,7},{7,0},{8,9},{9,10},{10,1... | collective-permute-start | bytes 1253384 | tf_op jit(solution)/shard_map/ppermute | solution.py:298
  158.2 7.7 %collective-permute-start.16 = (bf16[272,384]{1,0:T(8,128)(2,1)S(1)}, bf16[272,384]{1,0:T(8,128)(2,1)S(1)}, u32[]{:S(2)}, u32[]{:S(2)}) collective-permute-start(bf16[272,384]{1,0:T(8,128)(2,1)S(1)} %get-tuple-element.28), channel_id=1, source_target_pairs={{0,8},{8,0},{1,9},{9,1},{2,10},{10,2},{3,11},{11,3},{4,12},{12,4},... | collective-permute-start | bytes 626696 | tf_op jit(solution)/shard_map/ppermute | solution.py:308
Sparse Core Ops, SparseCore 0:
  19.8 67.4 all-gather.3

commit v5 on v4

v5 whole, which is shorter than its diff:
```python
import jax
import jax.numpy as jnp
from jax import lax
from jax.experimental import pallas as pl
from jax.experimental.pallas import tpu as pltpu
from jax.sharding import Mesh, PartitionSpec as P

HEADSZ = 128
PATCH = 256
EPS = 1e-06
GAIN_ROWS = 16
F32 = jnp.float32
BF16 = jnp.bfloat16
VMEM = pl.BlockSpec(memory_space=pltpu.VMEM)
HBM = pl.BlockSpec(memory_space=pltpu.HBM)


def params(mib):
    return pltpu.CompilerParams(vmem_limit_bytes=mib * 1024 * 1024)


def dot(a, b, ca, cb):
    return lax.dot_general(a, b, (((ca,), (cb,)), ((), ())), preferred_element_type=F32)


def lane_fold(x):
    total = x[:, :128]
    for at in range(128, x.shape[1], 128):
        total = total + x[:, at : at + 128]
    return total


def normalise_kernel(feat_all, offsets, which, qk_ref, cot_ref, *refs):
    pieces = refs[:-2]
    normed_ref, stat_ref = refs[-2:]
    rows = PATCH
    blocks = []
    for ref, offset, kinds in zip(pieces, offsets, which):
        for at, xl in enumerate(kinds):
            blocks.append((ref, at, xl * 8 + lax.rem(lax.axis_index("z") + offset, 8)))
    total = jnp.zeros((rows, 128), F32)
    for ref, at, _ in blocks:
        total = total + lane_fold(ref[at, :rows, :].astype(F32))
    mean = jnp.sum(total, axis=1, keepdims=True) / feat_all
    total = jnp.zeros((rows, 128), F32)
    for ref, at, _ in blocks:
        centred = ref[at, :rows, :].astype(F32) - mean
        total = total + lane_fold(centred * centred)
    inv = lax.rsqrt(jnp.sum(total, axis=1, keepdims=True) / feat_all + EPS)
    for ref, at, place in blocks:
        x_hat = (ref[at, :rows, :].astype(F32) - mean) * inv
        gain = ref[at, rows : rows + 1, :].astype(F32)
        normed_ref[place, :rows, :] = (x_hat * gain).astype(BF16)
        normed_ref[place, rows:, :] = ref[at, rows:, :]
    normed_ref[16, :rows, :rows] = cot_ref[...]
    high = qk_ref[...].astype(BF16).astype(F32)
    middle = (qk_ref[...] - high).astype(BF16).astype(F32)
    low = qk_ref[...] - high - middle
    rest = jnp.zeros((GAIN_ROWS - 6, 128), F32)
    normed_ref[16, rows:, :128] = jnp.concatenate([high, middle, low, rest], axis=0).astype(BF16)
    stat_ref[0] = jnp.broadcast_to(mean, (rows, 128))
    stat_ref[1] = jnp.broadcast_to(inv, (rows, 128))


def weight_rows(blocks):
    third = blocks[0].shape[0] // 3
    return jnp.concatenate(
        [
            jnp.concatenate([w[i * third : (i + 1) * third, :] for w in blocks], axis=0)
            for i in range(3)
        ],
        axis=1,
    )


def norm128(x):
    mean = jnp.mean(x, axis=1, keepdims=True)
    centred = x - mean
    inv = lax.rsqrt(jnp.mean(centred * centred, axis=1, keepdims=True) + EPS)
    return centred * inv, inv


def norm128_back(grad_hat, x_hat, inv):
    first = jnp.mean(grad_hat, axis=1, keepdims=True)
    second = jnp.mean(grad_hat * x_hat, axis=1, keepdims=True)
    return inv * (grad_hat - first - x_hat * second)


def split_sums(sums):
    high = sums.astype(BF16).astype(F32)
    return jnp.concatenate([high, sums - high], axis=0).astype(BF16)


def join_sums(rows):
    wide = rows.astype(F32)
    return wide[:8] + wide[8:]


def backward(offsets, grads, tail, fetch, part_refs):
    rows = PATCH
    for offset, refs in zip(offsets, part_refs):
        total = dot(grads, weight_rows(fetch(offset)), 1, 1)
        feat = total.shape[1] // 2
        for xl, (ref, at) in enumerate(refs):
            ref[at, :rows, :] = total[:, xl * feat : (xl + 1) * feat].astype(BF16)
            ref[at, rows:, :rows] = tail
            ref[at, rows:, rows:] = jnp.zeros((GAIN_ROWS, feat - rows), BF16)


def core_kernel(
    normed_hbm,
    w_hbm,
    out_ref,
    far_ahead_ref,
    far_behind_ref,
    ahead_ref,
    behind_ref,
    grads_ref,
    tail_ref,
    w_ref,
    normed_ref,
    acc,
    sems,
):
    width = w_ref.shape[3]
    heads = width // HEADSZ
    n_m = w_ref.shape[1]

    def copies(m):
        x_hi, y = divmod(m, 8)
        found = [pltpu.make_async_copy(normed_hbm.at[m], normed_ref.at[m], sems.at[m, 2])]
        if m == n_m:
            return found
        for c in range(2):
            found.append(
                pltpu.make_async_copy(w_hbm.at[2 * y + c, x_hi], w_ref.at[c, m], sems.at[m, c])
            )
        return found

    for m in range(n_m + 1):
        for copy in copies(m):
            copy.start()
    for m in range(0, n_m, 2):
        for k in range(2):
            for copy in copies(m + k):
                copy.wait()
        x = jnp.concatenate([normed_ref[m], normed_ref[m + 1]], axis=1)
        term = dot(x, weight_rows([w_ref[c, m + k] for k in range(2) for c in range(2)]), 1, 0)
        acc[...] = term if m == 0 else acc[...] + term
    for copy in copies(n_m):
        copy.wait()
    gains = normed_ref[n_m, PATCH:, :HEADSZ].astype(F32)
    rows = PATCH
    scale = HEADSZ ** (-0.5)
    gain_q, gain_k = (gains[i : i + 1] + gains[i + 2 : i + 3] + gains[i + 4 : i + 5] for i in range(2))
    first = jnp.zeros((rows, 128), F32)
    second = jnp.zeros((rows, 128), F32)
    for h in range(heads):
        cols = [slice(i * width + h * HEADSZ, i * width + (h + 1) * HEADSZ) for i in range(3)]
        own = slice(h * HEADSZ, (h + 1) * HEADSZ)
        proj = [acc[:rows, c] for c in cols]
        q_hat, q_inv = norm128(proj[0])
        k_hat, k_inv = norm128(proj[1])
        queries = (q_hat * gain_q).astype(BF16)
        keys = (k_hat * gain_k).astype(BF16)
        values = proj[2].astype(BF16)
        expo = jnp.exp(dot(queries, keys, 1, 1) * scale)
        probs = expo / jnp.sum(expo, axis=1, keepdims=True)
        weights_b = probs.astype(BF16)
        out_ref[:, own] = dot(weights_b, values, 1, 0).astype(BF16)
        upstream = normed_ref[n_m, :rows, own]
        d_probs = dot(upstream, values, 1, 1)
        d_values = dot(weights_b, upstream, 0, 0).astype(BF16)
        inner = jnp.sum(probs * d_probs, axis=1, keepdims=True)
        d_scores = (probs * (d_probs - inner) * scale).astype(BF16)
        d_queries = dot(d_scores, keys, 1, 0)
        d_keys = dot(d_scores, queries, 0, 0)
        grad_q = norm128_back(d_queries * gain_q, q_hat, q_inv).astype(BF16)
        grad_k = norm128_back(d_keys * gain_k, k_hat, k_inv).astype(BF16)
        for i, grad in enumerate((grad_q, grad_k, d_values)):
            grads_ref[:, cols[i]] = grad
            wide = grad.astype(F32)
            first = first + wide * acc[rows : rows + 1, cols[i]]
            second = second + wide * proj[i]
    sums = jnp.concatenate(
        [
            jnp.sum(first, axis=1)[None, :],
            jnp.sum(second, axis=1)[None, :],
            jnp.zeros((6, rows), F32),
        ],
        axis=0,
    )
    tail = split_sums(sums)
    tail_ref[...] = tail

    def fetch(offset):
        y = lax.rem(lax.axis_index("z") + offset, 8)
        return [w_ref[c, xl * 8 + y] for xl in range(2) for c in range(2)]

    part_refs = [((far_ahead_ref, 0), (far_behind_ref, 0))]
    part_refs += [((ref, 0), (ref, 1)) for ref in (ahead_ref, behind_ref)]
    backward((4, 3, 5), grads_ref[...], tail, fetch, part_refs)


def rest_kernel(grads_ref, tail_ref, w_hbm, *refs):
    part_refs = refs[:4]
    mine_ref, other_ref, w_ref, own_ref, sems = refs[4:]
    offsets = (2, 6, 1, 7, 0)

    def copies(at):
        y = lax.rem(lax.axis_index("z") + offsets[at], 8)
        return [
            pltpu.make_async_copy(w_hbm.at[2 * y + c, xl], w_ref.at[at, c, xl], sems.at[at, c, xl])
            for xl in range(2)
            for c in range(2)
        ]

    def fetch(offset):
        at = offsets.index(offset)
        for copy in copies(at):
            copy.wait()
        return [w_ref[at, c, xl] for xl in range(2) for c in range(2)]

    for at in range(len(offsets)):
        for copy in copies(at):
            copy.start()
    places = [((ref, 0), (ref, 1)) for ref in (*part_refs, own_ref)]
    backward(offsets, grads_ref[...], tail_ref[...], fetch, places)
    xl = lax.axis_index("xl")
    mine_ref[...] = own_ref[xl]
    other_ref[...] = own_ref[1 - xl]


def add_kernel(first, got_ref, part_ref, *out_refs):
    rows = PATCH
    n = part_ref.shape[0]
    for k in range(n):
        if len(out_refs) == 1:
            at, store = k, out_refs[0].at[k]
        else:
            at, store = (lax.axis_index("xl") + k) % n, out_refs[k]
        if len(out_refs) > 1 or first <= at < first + got_ref.shape[0]:
            got = at - first
            store[:rows, :] = (
                got_ref[got, :rows, :].astype(F32) + part_ref[at, :rows, :].astype(F32)
            ).astype(BF16)
            store[rows:, :] = split_sums(
                join_sums(got_ref[got, rows:, :]) + join_sums(part_ref[at, rows:, :])
            )
        else:
            store[...] = part_ref[at]


def final_kernel(feat_all, tok_ref, gain_ref, stat_ref, *refs):
    rows = PATCH
    out_ref = refs[-1]
    b = sum(ref[:rows, :].astype(F32) for ref in refs[:-1])
    b = b * gain_ref[0:1, :].astype(F32)
    sums = sum(join_sums(ref[rows:, :]) for ref in refs[:-1])
    diagonal = lax.broadcasted_iota(jnp.int32, (rows, rows), 0) == lax.broadcasted_iota(
        jnp.int32, (rows, rows), 1
    )
    first, second = (
        jnp.sum(jnp.where(diagonal, sums[i : i + 1, :rows], 0.0), axis=1, keepdims=True) / feat_all
        for i in range(2)
    )
    mean = stat_ref[0, :, 0:1]
    inv = stat_ref[1, :, 0:1]
    x_hat = (tok_ref[...].astype(F32) - mean) * inv
    out_ref[...] = (inv * (b - first - x_hat * second)).astype(BF16)


def ring(n, step):
    return [(i, (i + step) % n) for i in range(n)]


def per_device(tokens, ln_gain, qkv_weight, qk_gain, cotangent):
    rows, feat = tokens.shape
    width = qkv_weight.shape[2]
    feat_all = feat * 16

    weights = lax.all_gather(qkv_weight.reshape(-1, width), "xh", axis=0)
    weights = lax.all_gather(weights, ("y", "c"), axis=0)

    gain = jnp.broadcast_to(ln_gain[None, :], (GAIN_ROWS, feat))
    toks = lax.all_gather(jnp.concatenate([tokens, gain], axis=0), "xl", axis=0)
    pieces = [toks]
    ahead = behind = toks
    for _ in range(3):
        ahead = lax.ppermute(ahead, "z", ring(8, 1))
        behind = lax.ppermute(behind, "z", ring(8, -1))
        pieces += [ahead, behind]
    pieces.append(lax.ppermute(ahead[:1], "z", ring(8, 1)))
    pieces.append(lax.ppermute(behind[1:], "z", ring(8, -1)))
    places = (0, 7, 1, 6, 2, 5, 3, 4, 4)
    which = ((0, 1),) * 7 + ((0,), (1,))

    normed, stats = pl.pallas_call(
        lambda *refs: normalise_kernel(feat_all, places, which, *refs),
        out_shape=(
            jax.ShapeDtypeStruct((17, rows + GAIN_ROWS, feat), BF16),
            jax.ShapeDtypeStruct((2, rows, 128), F32),
        ),
        in_specs=[VMEM] * (2 + len(pieces)),
        out_specs=(VMEM, VMEM),
        compiler_params=params(16),
        name="normalise",
    )(qk_gain, cotangent, *pieces)

    block = (rows + GAIN_ROWS, feat)

    def blocks(n):
        return jax.ShapeDtypeStruct((n,) + block, BF16)

    def cost(flops, nbytes):
        return pl.CostEstimate(flops=flops, bytes_accessed=nbytes, transcendentals=0)

    attended, ahead, behind, part_ahead, part_behind, grads, tail = pl.pallas_call(
        core_kernel,
        out_shape=(
            jax.ShapeDtypeStruct((rows, width), BF16),
            *(blocks(n) for n in (1, 1, 2, 2)),
            jax.ShapeDtypeStruct((rows, 3 * width), BF16),
            jax.ShapeDtypeStruct((GAIN_ROWS, rows), BF16),
        ),
        in_specs=[HBM] * 2,
        out_specs=(VMEM,) * 7,
        scratch_shapes=[
            pltpu.VMEM((2, 16) + weights.shape[2:], BF16),
            pltpu.VMEM(normed.shape, BF16),
            pltpu.VMEM((rows + GAIN_ROWS, 3 * width), F32),
            pltpu.SemaphoreType.DMA((17, 3)),
        ],
        compiler_params=params(50),
        name="core",
    )(normed, weights)
    *near, mine, other = pl.pallas_call(
        rest_kernel,
        out_shape=(*(blocks(2) for _ in range(4)),) + (jax.ShapeDtypeStruct(block, BF16),) * 2,
        in_specs=[VMEM] * 2 + [HBM],
        out_specs=(VMEM,) * 6,
        scratch_shapes=[
            pltpu.VMEM((5, 2, 2) + weights.shape[2:], BF16),
            pltpu.VMEM((2,) + block, BF16),
            pltpu.SemaphoreType.DMA((5, 2, 2)),
        ],
        compiler_params=params(50),
        cost_estimate=cost(2 * rows * 10 * feat * 3 * width, 6 * 2**20),
        name="rest",
    )(grads, tail, weights)

    def add(got, part, first, n_out, name):
        out = (blocks(2),) if n_out == 1 else (jax.ShapeDtypeStruct(block, BF16),) * 2
        return pl.pallas_call(
            lambda *refs: add_kernel(first, *refs),
            out_shape=out,
            in_specs=[VMEM] * 2,
            out_specs=(VMEM,) * n_out,
            compiler_params=params(16),
            cost_estimate=cost(10**6, 2**20),
            name=name,
        )(got, part)

    parts = [(part_ahead, part_behind), near[:2], near[2:]]
    for step in range(3):
        ahead = lax.ppermute(ahead, "z", ring(8, 1))
        behind = lax.ppermute(behind, "z", ring(8, -1))
        n_out = 2 if step == 2 else 1
        ahead, *ahead_other = add(ahead, parts[step][0], 0, n_out, "add_ahead")
        behind, *behind_other = add(behind, parts[step][1], 1 if step == 0 else 0, n_out, "add_behind")

    def across(step):
        return [(8 * k + i, 8 * (1 - k) + (i + step) % 8) for k in range(2) for i in range(8)]

    terms = (
        mine,
        lax.ppermute(other, "xl", ring(2, 1)),
        lax.ppermute(ahead, "z", ring(8, 1)),
        lax.ppermute(behind, "z", ring(8, -1)),
        lax.ppermute(ahead_other[0], ("xl", "z"), across(1)),
        lax.ppermute(behind_other[0], ("xl", "z"), across(-1)),
    )
    grad_tokens = pl.pallas_call(
        lambda *refs: final_kernel(feat_all, *refs),
        out_shape=jax.ShapeDtypeStruct((rows, feat), BF16),
        in_specs=[VMEM] * (3 + len(terms)),
        out_specs=VMEM,
        compiler_params=params(16),
        name="final_norm",
    )(tokens, gain, stats, *terms)
    return (attended, grad_tokens)


def solution(mesh):
    fine = Mesh(mesh.devices.reshape(2, 8, 2, 2, 8), ("xh", "y", "c", "xl", "z"))
    dp, mp = ("xh", "y", "c"), ("xl", "z")
    return jax.shard_map(
        per_device,
        mesh=fine,
        in_specs=(P(dp, mp), P(mp), P(None, dp, mp), P(), P(dp, mp)),
        out_specs=(P(dp, mp), P(dp, mp)),
        check_vma=False,
    )
```

time: 175 us -> 166 us (0.949)
  waiting for transfers between devices: 50.7 us -> 34.4 us
  starting transfers between devices: 66.1 us -> 72.1 us
    ppermute x1 -> x5, starting transfers between devices: 2.7 us -> 16.8 us  [the longest x1 5.6 us: per_device(): lax.ppermute(behind, 'z', ring(8, -1))]
    ppermute x7 -> x6, waiting for transfers between devices: 33.3 us -> 20.6 us  [per_device(): behind = lax.ppermute(behind, 'z', ring(8, -1))]
    ppermute x7 -> x6, starting transfers between devices: 42.3 us -> 34.2 us  [per_device(): behind = lax.ppermute(behind, 'z', ring(8, -1))]
    ppermute x7 -> x6, waiting for transfers between devices: 5.47 us -> 0.02 us  [per_device(): ahead = lax.ppermute(ahead, 'z', ring(8, 1))]
    ppermute x1 -> x5, waiting for transfers between devices: 4.98 us -> 6.75 us  [the longest x1 3.79 us: per_device(): lax.ppermute(ahead, 'z', ring(8, 1))]
    ppermute x7 -> x6, starting transfers between devices: 13.6 us -> 13.6 us  [per_device(): ahead = lax.ppermute(ahead, 'z', ring(8, 1))]
  transfers between devices with their start and end apart: 18 -> 20, of which waited for: 11 -> 10; matrix products, arithmetic and copies ran while one was open for 1% -> 1% of each run, Pallas kernels for 2% -> 5%
where the time goes in v5:
time: 166 us; the launch traced here: 164 us
  starting transfers between devices  72.1 us (43%)
  waiting for transfers between devices  34.4 us (21%)
  blocking collectives  19.9 us (12%)
  Pallas kernels  18.5 us (11%)
  between operations  14.3 us (9%)
  local copies, waits for them, and re-layouts  4.21 us (3%)
    ppermute x6, starting transfers between devices, per_device(): behind = lax.ppermute(behind, 'z', ring(8, -1))  34.2 us
    ppermute x6, waiting for transfers between devices, per_device(): behind = lax.ppermute(behind, 'z', ring(8, -1))  20.6 us
    ppermute x6, starting transfers between devices, per_device(): ahead = lax.ppermute(ahead, 'z', ring(8, 1))  13.6 us
    all_gather x1, blocking collectives, per_device(): weights = lax.all_gather(qkv_weight.reshape(-1, width), 'xh', axis=0)  12.5 us
    pallas_call x1, Pallas kernels, per_device(): pl.pallas_call(core_kernel, out_shape=(jax.ShapeDtypeStruct((rows, width)...  9.55 us
    all_gather x1, blocking collectives, per_device(): toks = lax.all_gather(jnp.concatenate([tokens, gain], axis=0), 'xl', axis=0)  7.44 us
    ppermute x1, waiting for transfers between devices, per_device(): pieces.append(lax.ppermute(ahead[:1], 'z', ring(8, 1)))  5.65 us
    ppermute x1, starting transfers between devices, per_device(): pieces.append(lax.ppermute(behind[1:], 'z', ring(8, -1)))  5.6 us
  transfers between devices with their start and end apart: 20, of which 10 were waited for; matrix products, arithmetic and copies ran while one was open for 1% of the time, Pallas kernels for 5%

profile of v5, /device:TPU:6, one launch (start us, length us, event | category | flops | bytes accessed | tf_op | source)
XLA Modules:
  0.0 164.4 jit_solution(5620516375374708253)
XLA Ops:
  7.2 12.5 %all_gather.17 = bf16[2,576,256]{2,1,0:T(8,128)(2,1)} all-gather(bf16[1,576,256]{2,1,0:T(8,128)(2,1)} %bitcast.8), channel_id=1, replica_groups=mesh['xh'=2,'y'=8,'c'=2,'xl'=2,'z'=8] {'xh'}, dimensions={0}, use_global_device_ids=true | all-gather | bytes 884736 | tf_op jit(solution)/shard_map/all_gather | solution.py:282
  21.3 7.4 %all-gather = bf16[544,384]{1,0:T(8,128)(2,1)S(1)} all-gather(bf16[272,384]{1,0:T(8,128)(2,1)S(1)} %pad_maximum_fusion), channel_id=2, replica_groups=mesh['xh'=2,'y'=8,'c'=2,'xl'=2,'z'=8] {'xl'}, dimensions={0}, use_global_device_ids=true | all-gather | bytes 626688 | tf_op jit(solution)/shard_map/all_gather | solution.py:286
  28.8 10.5 %collective-permute-start.1 = (bf16[2,272,384]{2,1,0:T(8,128)(2,1)S(1)}, bf16[2,272,384]{2,1,0:T(8,128)(2,1)S(1)}, u32[]{:S(2)}, u32[]{:S(2)}) collective-permute-start(bf16[2,272,384]{2,1,0:T(8,128)(2,1)S(1)} %bitcast.3), channel_id=1, source_target_pairs={{0,7},{1,0},{2,1},{3,2},{4,3},{5,4},{6,5},{7,6},{8,15},{9,8},{10,9... | collective-permute-start | bytes 1253384 | tf_op jit(solution)/shard_map/ppermute | solution.py:291
  39.3 1.9 %collective-permute-start = (bf16[2,272,384]{2,1,0:T(8,128)(2,1)S(1)}, bf16[2,272,384]{2,1,0:T(8,128)(2,1)S(1)}, u32[]{:S(2)}, u32[]{:S(2)}) collective-permute-start(bf16[2,272,384]{2,1,0:T(8,128)(2,1)S(1)} %bitcast.4), channel_id=1, source_target_pairs={{0,1},{1,2},{2,3},{3,4},{4,5},{5,6},{6,7},{7,0},{8,9},{9,10},{10,1... | collective-permute-start | bytes 1253384 | tf_op jit(solution)/shard_map/ppermute | solution.py:290
  41.2 5.5 %collective-permute-done.1.refs_4_ = bf16[2,272,384]{2,1,0:T(8,128)(2,1)S(1)} collective-permute-done((bf16[2,272,384]{2,1,0:T(8,128)(2,1)S(1)}, bf16[2,272,384]{2,1,0:T(8,128)(2,1)S(1)}, u32[]{:S(2)}, u32[]{:S(2)}) %collective-permute-start.1) | collective-permute-done | bytes 417824 | tf_op jit(solution)/shard_map/ppermute | solution.py:291
  46.7 5.6 %collective-permute-start.3 = (bf16[2,272,384]{2,1,0:T(8,128)(2,1)S(1)}, bf16[2,272,384]{2,1,0:T(8,128)(2,1)S(1)}, u32[]{:S(2)}, u32[]{:S(2)}) collective-permute-start(bf16[2,272,384]{2,1,0:T(8,128)(2,1)S(1)} %collective-permute-done.1.refs_4_), channel_id=1, source_target_pairs={{0,7},{1,0},{2,1},{3,2},{4,3},{5,4},{6,5},{7,6},{8,15},{9,8},{10,9... | collective-permute-start | bytes 1253384 | tf_op jit(solution)/shard_map/ppermute | solution.py:291
  52.3 1.9 %collective-permute-start.2 = (bf16[2,272,384]{2,1,0:T(8,128)(2,1)S(1)}, bf16[2,272,384]{2,1,0:T(8,128)(2,1)S(1)}, u32[]{:S(2)}, u32[]{:S(2)}) collective-permute-start(bf16[2,272,384]{2,1,0:T(8,128)(2,1)S(1)} %collective-permute-done.refs_3_), channel_id=1, source_target_pairs={{0,1},{1,2},{2,3},{3,4},{4,5},{5,6},{6,7},{7,0},{8,9},{9,10},{10,1... | collective-permute-start | bytes 1253384 | tf_op jit(solution)/shard_map/ppermute | solution.py:290
  54.3 4.6 %collective-permute-done.3.refs_6_ = bf16[2,272,384]{2,1,0:T(8,128)(2,1)S(1)} collective-permute-done((bf16[2,272,384]{2,1,0:T(8,128)(2,1)S(1)}, bf16[2,272,384]{2,1,0:T(8,128)(2,1)S(1)}, u32[]{:S(2)}, u32[]{:S(2)}) %collective-permute-start.3) | collective-permute-done | bytes 417824 | tf_op jit(solution)/shard_map/ppermute | solution.py:291
  58.9 5.6 %collective-permute-start.5 = (bf16[2,272,384]{2,1,0:T(8,128)(2,1)S(1)}, bf16[2,272,384]{2,1,0:T(8,128)(2,1)S(1)}, u32[]{:S(2)}, u32[]{:S(2)}) collective-permute-start(bf16[2,272,384]{2,1,0:T(8,128)(2,1)S(1)} %collective-permute-done.3.refs_6_), channel_id=1, source_target_pairs={{0,7},{1,0},{2,1},{3,2},{4,3},{5,4},{6,5},{7,6},{8,15},{9,8},{10,9... | collective-permute-start | bytes 1253384 | tf_op jit(solution)/shard_map/ppermute | solution.py:291
  64.5 1.9 %collective-permute-start.4 = (bf16[2,272,384]{2,1,0:T(8,128)(2,1)S(1)}, bf16[2,272,384]{2,1,0:T(8,128)(2,1)S(1)}, u32[]{:S(2)}, u32[]{:S(2)}) collective-permute-start(bf16[2,272,384]{2,1,0:T(8,128)(2,1)S(1)} %collective-permute-done.2.refs_5_), channel_id=1, source_target_pairs={{0,1},{1,2},{2,3},{3,4},{4,5},{5,6},{6,7},{7,0},{8,9},{9,10},{10,1... | collective-permute-start | bytes 1253384 | tf_op jit(solution)/shard_map/ppermute | solution.py:290
  66.4 3.8 %collective-permute-done.5.refs_8_ = bf16[2,272,384]{2,1,0:T(8,128)(2,1)S(1)} collective-permute-done((bf16[2,272,384]{2,1,0:T(8,128)(2,1)S(1)}, bf16[2,272,384]{2,1,0:T(8,128)(2,1)S(1)}, u32[]{:S(2)}, u32[]{:S(2)}) %collective-permute-start.5) | collective-permute-done | bytes 417824 | tf_op jit(solution)/shard_map/ppermute | solution.py:291
  70.3 5.6 %collective-permute-start.7 = (bf16[1,272,384]{2,1,0:T(8,128)(2,1)S(1)}, bf16[1,272,384]{2,1,0:T(8,128)(2,1)S(1)}, u32[]{:S(2)}, u32[]{:S(2)}) collective-permute-start(bf16[1,272,384]{2,1,0:T(8,128)(2,1)S(1)} %slice.9), channel_id=1, source_target_pairs={{0,7},{1,0},{2,1},{3,2},{4,3},{5,4},{6,5},{7,6},{8,15},{9,8},{10,9... | collective-permute-start | bytes 626696 | tf_op jit(solution)/shard_map/ppermute | solution.py:294
  75.9 1.9 %collective-permute-start.6 = (bf16[1,272,384]{2,1,0:T(8,128)(2,1)S(1)}, bf16[1,272,384]{2,1,0:T(8,128)(2,1)S(1)}, u32[]{:S(2)}, u32[]{:S(2)}) collective-permute-start(bf16[1,272,384]{2,1,0:T(8,128)(2,1)S(1)} %slice.8), channel_id=1, source_target_pairs={{0,1},{1,2},{2,3},{3,4},{4,5},{5,6},{6,7},{7,0},{8,9},{9,10},{10,1... | collective-permute-start | bytes 626696 | tf_op jit(solution)/shard_map/ppermute | solution.py:293
  79.2 5.6 %collective-permute-done.6.refs_9_ = bf16[1,272,384]{2,1,0:T(8,128)(2,1)S(1)} collective-permute-done((bf16[1,272,384]{2,1,0:T(8,128)(2,1)S(1)}, bf16[1,272,384]{2,1,0:T(8,128)(2,1)S(1)}, u32[]{:S(2)}, u32[]{:S(2)}) %collective-permute-start.6) | collective-permute-done | bytes 208928 | tf_op jit(solution)/shard_map/ppermute | solution.py:293
  86.4 2.9 %normalise.1 = (bf16[17,272,384]{2,1,0:T(8,128)(2,1)S(1)}, f32[2,256,128]{2,1,0:T(8,128)S(1)}) custom-call(f32[2,128]{1,0:T(2,128)S(1)} %copy-done.3, bf16[256,256]{1,0:T(8,128)(2,1)S(1)} %copy-done.2, bf16[2,272,384]{2,1,0:T(8,128)(2,1)S(1)} %bitcast.5, bf16[2,272,384]{2,1,0:T(8,128)(2,1)S(1)} %collective-permute-done.refs_3_, ...), custom_call_target="tpu_custom_call" | custom-call | tf_op jit(solution)/shard_map/normalise/pallas_call | solution.py:298
  89.3 1.9 %copy-done = bf16[17,272,384]{2,1,0:T(8,128)(2,1)} copy-done((bf16[17,272,384]{2,1,0:T(8,128)(2,1)}, bf16[17,272,384]{2,1,0:T(8,128)(2,1)S(1)}, u32[]{:S(2)}) %copy-start) | copy-done | bytes 3551256
  91.2 9.5 %core.1 = (bf16[256,256]{1,0:T(8,128)(2,1)}, bf16[1,272,384]{2,1,0:T(8,128)(2,1)S(1)}, bf16[1,272,384]{2,1,0:T(8,128)(2,1)S(1)}, bf16[2,272,384]{2,1,0:T(8,128)(...) custom-call(bf16[17,272,384]{2,1,0:T(8,128)(2,1)} %copy-done, ...), custom_call_target="tpu_custom_call" | custom-call | tf_op jit(solution)/shard_map/core/pallas_call | solution.py:318
  100.8 2.1 %collective-permute-start.13 = (bf16[1,272,384]{2,1,0:T(8,128)(2,1)S(1)}, bf16[1,272,384]{2,1,0:T(8,128)(2,1)S(1)}, u32[]{:S(2)}, u32[]{:S(2)}) collective-permute-start(bf16[1,272,384]{2,1,0:T(8,128)(2,1)S(1)} %get-tuple-element.33), channel_id=1, source_target_pairs={{0,7},{1,0},{2,1},{3,2},{4,3},{5,4},{6,5},{7,6},{8,15},{9,8},{10,9... | collective-permute-start | bytes 626696 | tf_op jit(solution)/shard_map/ppermute | solution.py:367
  102.9 3.8 %collective-permute-start.9 = (bf16[1,272,384]{2,1,0:T(8,128)(2,1)S(1)}, bf16[1,272,384]{2,1,0:T(8,128)(2,1)S(1)}, u32[]{:S(2)}, u32[]{:S(2)}) collective-permute-start(bf16[1,272,384]{2,1,0:T(8,128)(2,1)S(1)} %get-tuple-element.28), channel_id=1, source_target_pairs={{0,1},{1,2},{2,3},{3,4},{4,5},{5,6},{6,7},{7,0},{8,9},{9,10},{10,1... | collective-permute-start | bytes 626696 | tf_op jit(solution)/shard_map/ppermute | solution.py:366
  108.7 4.7 %collective-permute-start.14 = (bf16[2,272,384]{2,1,0:T(8,128)(2,1)S(1)}, bf16[2,272,384]{2,1,0:T(8,128)(2,1)S(1)}, u32[]{:S(2)}, u32[]{:S(2)}) collective-permute-start(bf16[2,272,384]{2,1,0:T(8,128)(2,1)S(1)} %add_behind.3), channel_id=1, source_target_pairs={{0,7},{1,0},{2,1},{3,2},{4,3},{5,4},{6,5},{7,6},{8,15},{9,8},{10,9... | collective-permute-start | bytes 1253384 | tf_op jit(solution)/shard_map/ppermute | solution.py:367
  113.5 2.1 %collective-permute-start.10 = (bf16[2,272,384]{2,1,0:T(8,128)(2,1)S(1)}, bf16[2,272,384]{2,1,0:T(8,128)(2,1)S(1)}, u32[]{:S(2)}, u32[]{:S(2)}) collective-permute-start(bf16[2,272,384]{2,1,0:T(8,128)(2,1)S(1)} %add_ahead.3), channel_id=1, source_target_pairs={{0,1},{1,2},{2,3},{3,4},{4,5},{5,6},{6,7},{7,0},{8,9},{9,10},{10,1... | collective-permute-start | bytes 1253384 | tf_op jit(solution)/shard_map/ppermute | solution.py:366
  115.6 4.5 %rest.1 = (bf16[2,272,384]{2,1,0:T(8,128)(2,1)S(1)}, bf16[2,272,384]{2,1,0:T(8,128)(2,1)S(1)}, bf16[2,272,384]{2,1,0:T(8,128)(2,1)S(1)}, bf16[2,272,384]{2,1,0:T...) custom-call(bf16[256,768]{1,0:T(8,128)(2,1)S(1)} %get-tuple-element.24.grads_ref, ...), custom_call_target="tpu_custom_call" | custom-call | flops 1509949440 | bytes 6291456 | tf_op jit(solution)/shard_map/rest/pallas_call | solution.py:337
  122.0 5.6 %collective-permute-start.15 = (bf16[2,272,384]{2,1,0:T(8,128)(2,1)S(1)}, bf16[2,272,384]{2,1,0:T(8,128)(2,1)S(1)}, u32[]{:S(2)}, u32[]{:S(2)}) collective-permute-start(bf16[2,272,384]{2,1,0:T(8,128)(2,1)S(1)} %add_behind.4), channel_id=1, source_target_pairs={{0,7},{1,0},{2,1},{3,2},{4,3},{5,4},{6,5},{7,6},{8,15},{9,8},{10,9... | collective-permute-start | bytes 1253384 | tf_op jit(solution)/shard_map/ppermute | solution.py:367
  127.8 1.9 %collective-permute-start.11 = (bf16[2,272,384]{2,1,0:T(8,128)(2,1)S(1)}, bf16[2,272,384]{2,1,0:T(8,128)(2,1)S(1)}, u32[]{:S(2)}, u32[]{:S(2)}) collective-permute-start(bf16[2,272,384]{2,1,0:T(8,128)(2,1)S(1)} %add_ahead.4), channel_id=1, source_target_pairs={{0,1},{1,2},{2,3},{3,4},{4,5},{5,6},{6,7},{7,0},{8,9},{9,10},{10,1... | collective-permute-start | bytes 1253384 | tf_op jit(solution)/shard_map/ppermute | solution.py:366
  129.7 2.5 %collective-permute-start.8 = (bf16[272,384]{1,0:T(8,128)(2,1)S(1)}, bf16[272,384]{1,0:T(8,128)(2,1)S(1)}, u32[]{:S(2)}, u32[]{:S(2)}) collective-permute-start(bf16[272,384]{1,0:T(8,128)(2,1)S(1)} %get-tuple-element.27), channel_id=1, source_target_pairs={{0,8},{8,0},{1,9},{9,1},{2,10},{10,2},{3,11},{11,3},{4,12},{12,4},... | collective-permute-start | bytes 626696 | tf_op jit(solution)/shard_map/ppermute | solution.py:377
  132.2 3.0 %collective-permute-done.15.refs_0_ = bf16[2,272,384]{2,1,0:T(8,128)(2,1)S(1)} collective-permute-done((bf16[2,272,384]{2,1,0:T(8,128)(2,1)S(1)}, bf16[2,272,384]{2,1,0:T(8,128)(2,1)S(1)}, u32[]{:S(2)}, u32[]{:S(2)}) %collective-permute-start.15) | collective-permute-done | bytes 417824 | tf_op jit(solution)/shard_map/ppermute | solution.py:367
  135.3 5.6 %collective-permute-start.16 = (bf16[272,384]{1,0:T(8,128)(2,1)S(1)}, bf16[272,384]{1,0:T(8,128)(2,1)S(1)}, u32[]{:S(2)}, u32[]{:S(2)}) collective-permute-start(bf16[272,384]{1,0:T(8,128)(2,1)S(1)} %get-tuple-element.37), channel_id=1, source_target_pairs={{0,7},{1,0},{2,1},{3,2},{4,3},{5,4},{6,5},{7,6},{8,15},{9,8},{10,9... | collective-permute-start | bytes 626696 | tf_op jit(solution)/shard_map/ppermute | solution.py:379
  140.9 1.9 %collective-permute-start.18 = (bf16[272,384]{1,0:T(8,128)(2,1)S(1)}, bf16[272,384]{1,0:T(8,128)(2,1)S(1)}, u32[]{:S(2)}, u32[]{:S(2)}) collective-permute-start(bf16[272,384]{1,0:T(8,128)(2,1)S(1)} %get-tuple-element.39), channel_id=1, source_target_pairs={{0,15},{1,8},{2,9},{3,10},{4,11},{5,12},{6,13},{7,14},{8,7},{9,0},... | collective-permute-start | bytes 626696 | tf_op jit(solution)/shard_map/ppermute | solution.py:381
  143.0 3.7 %collective-permute-start.12 = (bf16[272,384]{1,0:T(8,128)(2,1)S(1)}, bf16[272,384]{1,0:T(8,128)(2,1)S(1)}, u32[]{:S(2)}, u32[]{:S(2)}) collective-permute-start(bf16[272,384]{1,0:T(8,128)(2,1)S(1)} %get-tuple-element.32), channel_id=1, source_target_pairs={{0,1},{1,2},{2,3},{3,4},{4,5},{5,6},{6,7},{7,0},{8,9},{9,10},{10,1... | collective-permute-start | bytes 626696 | tf_op jit(solution)/shard_map/ppermute | solution.py:378
  146.7 3.0 %collective-permute-start.17 = (bf16[272,384]{1,0:T(8,128)(2,1)S(1)}, bf16[272,384]{1,0:T(8,128)(2,1)S(1)}, u32[]{:S(2)}, u32[]{:S(2)}) collective-permute-start(bf16[272,384]{1,0:T(8,128)(2,1)S(1)} %get-tuple-element.38), channel_id=1, source_target_pairs={{0,9},{1,10},{2,11},{3,12},{4,13},{5,14},{6,15},{7,8},{8,1},{9,2},... | collective-permute-start | bytes 626696 | tf_op jit(solution)/shard_map/ppermute | solution.py:380
  149.8 3.8 %collective-permute-done.12.refs_5_ = bf16[272,384]{1,0:T(8,128)(2,1)S(1)} collective-permute-done((bf16[272,384]{1,0:T(8,128)(2,1)S(1)}, bf16[272,384]{1,0:T(8,128)(2,1)S(1)}, u32[]{:S(2)}, u32[]{:S(2)}) %collective-permute-start.12) | collective-permute-done | bytes 208928 | tf_op jit(solution)/shard_map/ppermute | solution.py:378
  153.6 2.9 %collective-permute-done.17.refs_7_ = bf16[272,384]{1,0:T(8,128)(2,1)S(1)} collective-permute-done((bf16[272,384]{1,0:T(8,128)(2,1)S(1)}, bf16[272,384]{1,0:T(8,128)(2,1)S(1)}, u32[]{:S(2)}, u32[]{:S(2)}) %collective-permute-start.17) | collective-permute-done | bytes 208928 | tf_op jit(solution)/shard_map/ppermute | solution.py:380
  (33 shorter events, 10.0 us)
Async XLA Ops:
  7.2 84.0 %all-gather.4.cloned.1.call-start = ((), (), s32[]{:S(2)}) async-start(), calls=%async_computation | async-start | bytes 10027008 | tf_op jit(solution)/shard_map/all_gather | solution.py:283
  28.8 17.9 %collective-permute-start.1 = (bf16[2,272,384]{2,1,0:T(8,128)(2,1)S(1)}, bf16[2,272,384]{2,1,0:T(8,128)(2,1)S(1)}, u32[]{:S(2)}, u32[]{:S(2)}) collective-permute-start(bf16[2,272,384]{2,1,0:T(8,128)(2,1)S(1)} %bitcast.3), channel_id=1, source_target_pairs={{0,7},{1,0},{2,1},{3,2},{4,3},{5,4},{6,5},{7,6},{8,15},{9,8},{10,9... | collective-permute-start | bytes 1253384 | tf_op jit(solution)/shard_map/ppermute | solution.py:291
  39.3 13.0 %collective-permute-start = (bf16[2,272,384]{2,1,0:T(8,128)(2,1)S(1)}, bf16[2,272,384]{2,1,0:T(8,128)(2,1)S(1)}, u32[]{:S(2)}, u32[]{:S(2)}) collective-permute-start(bf16[2,272,384]{2,1,0:T(8,128)(2,1)S(1)} %bitcast.4), channel_id=1, source_target_pairs={{0,1},{1,2},{2,3},{3,4},{4,5},{5,6},{6,7},{7,0},{8,9},{9,10},{10,1... | collective-permute-start | bytes 1253384 | tf_op jit(solution)/shard_map/ppermute | solution.py:290
  46.7 12.2 %collective-permute-start.3 = (bf16[2,272,384]{2,1,0:T(8,128)(2,1)S(1)}, bf16[2,272,384]{2,1,0:T(8,128)(2,1)S(1)}, u32[]{:S(2)}, u32[]{:S(2)}) collective-permute-start(bf16[2,272,384]{2,1,0:T(8,128)(2,1)S(1)} %collective-permute-done.1.refs_4_), channel_id=1, source_target_pairs={{0,7},{1,0},{2,1},{3,2},{4,3},{5,4},{6,5},{7,6},{8,15},{9,8},{10,9... | collective-permute-start | bytes 1253384 | tf_op jit(solution)/shard_map/ppermute | solution.py:291
  52.3 12.2 %collective-permute-start.2 = (bf16[2,272,384]{2,1,0:T(8,128)(2,1)S(1)}, bf16[2,272,384]{2,1,0:T(8,128)(2,1)S(1)}, u32[]{:S(2)}, u32[]{:S(2)}) collective-permute-start(bf16[2,272,384]{2,1,0:T(8,128)(2,1)S(1)} %collective-permute-done.refs_3_), channel_id=1, source_target_pairs={{0,1},{1,2},{2,3},{3,4},{4,5},{5,6},{6,7},{7,0},{8,9},{9,10},{10,1... | collective-permute-start | bytes 1253384 | tf_op jit(solution)/shard_map/ppermute | solution.py:290
  58.9 11.4 %collective-permute-start.5 = (bf16[2,272,384]{2,1,0:T(8,128)(2,1)S(1)}, bf16[2,272,384]{2,1,0:T(8,128)(2,1)S(1)}, u32[]{:S(2)}, u32[]{:S(2)}) collective-permute-start(bf16[2,272,384]{2,1,0:T(8,128)(2,1)S(1)} %collective-permute-done.3.refs_6_), channel_id=1, source_target_pairs={{0,7},{1,0},{2,1},{3,2},{4,3},{5,4},{6,5},{7,6},{8,15},{9,8},{10,9... | collective-permute-start | bytes 1253384 | tf_op jit(solution)/shard_map/ppermute | solution.py:291
  64.5 11.4 %collective-permute-start.4 = (bf16[2,272,384]{2,1,0:T(8,128)(2,1)S(1)}, bf16[2,272,384]{2,1,0:T(8,128)(2,1)S(1)}, u32[]{:S(2)}, u32[]{:S(2)}) collective-permute-start(bf16[2,272,384]{2,1,0:T(8,128)(2,1)S(1)} %collective-permute-done.2.refs_5_), channel_id=1, source_target_pairs={{0,1},{1,2},{2,3},{3,4},{4,5},{5,6},{6,7},{7,0},{8,9},{9,10},{10,1... | collective-permute-start | bytes 1253384 | tf_op jit(solution)/shard_map/ppermute | solution.py:290
  70.3 8.9 %collective-permute-start.7 = (bf16[1,272,384]{2,1,0:T(8,128)(2,1)S(1)}, bf16[1,272,384]{2,1,0:T(8,128)(2,1)S(1)}, u32[]{:S(2)}, u32[]{:S(2)}) collective-permute-start(bf16[1,272,384]{2,1,0:T(8,128)(2,1)S(1)} %slice.9), channel_id=1, source_target_pairs={{0,7},{1,0},{2,1},{3,2},{4,3},{5,4},{6,5},{7,6},{8,15},{9,8},{10,9... | collective-permute-start | bytes 626696 | tf_op jit(solution)/shard_map/ppermute | solution.py:294
  75.9 8.9 %collective-permute-start.6 = (bf16[1,272,384]{2,1,0:T(8,128)(2,1)S(1)}, bf16[1,272,384]{2,1,0:T(8,128)(2,1)S(1)}, u32[]{:S(2)}, u32[]{:S(2)}) collective-permute-start(bf16[1,272,384]{2,1,0:T(8,128)(2,1)S(1)} %slice.8), channel_id=1, source_target_pairs={{0,1},{1,2},{2,3},{3,4},{4,5},{5,6},{6,7},{7,0},{8,9},{9,10},{10,1... | collective-permute-start | bytes 626696 | tf_op jit(solution)/shard_map/ppermute | solution.py:293
  84.9 0.9 copy-start.2
  85.8 0.7 copy-start.3
  89.3 1.9 %copy-start = (bf16[17,272,384]{2,1,0:T(8,128)(2,1)}, bf16[17,272,384]{2,1,0:T(8,128)(2,1)S(1)}, u32[]{:S(2)}) copy-start(bf16[17,272,384]{2,1,0:T(8,128)(2,1)S(1)} %get-tuple-element.21.normed_hbm) | copy-start | bytes 10653700
  100.8 55.8 %copy-start.1 = (bf16[256,384]{1,0:T(8,128)(2,1)S(1)}, bf16[256,384]{1,0:T(8,128)(2,1)}, u32[]{:S(2)}) copy-start(bf16[256,384]{1,0:T(8,128)(2,1)} %refs_0_.3) | copy-start | bytes 589828
  100.8 7.8 %collective-permute-start.13 = (bf16[1,272,384]{2,1,0:T(8,128)(2,1)S(1)}, bf16[1,272,384]{2,1,0:T(8,128)(2,1)S(1)}, u32[]{:S(2)}, u32[]{:S(2)}) collective-permute-start(bf16[1,272,384]{2,1,0:T(8,128)(2,1)S(1)} %get-tuple-element.33), channel_id=1, source_target_pairs={{0,7},{1,0},{2,1},{3,2},{4,3},{5,4},{6,5},{7,6},{8,15},{9,8},{10,9... | collective-permute-start | bytes 626696 | tf_op jit(solution)/shard_map/ppermute | solution.py:367
  102.9 10.5 %collective-permute-start.9 = (bf16[1,272,384]{2,1,0:T(8,128)(2,1)S(1)}, bf16[1,272,384]{2,1,0:T(8,128)(2,1)S(1)}, u32[]{:S(2)}, u32[]{:S(2)}) collective-permute-start(bf16[1,272,384]{2,1,0:T(8,128)(2,1)S(1)} %get-tuple-element.28), channel_id=1, source_target_pairs={{0,1},{1,2},{2,3},{3,4},{4,5},{5,6},{6,7},{7,0},{8,9},{9,10},{10,1... | collective-permute-start | bytes 626696 | tf_op jit(solution)/shard_map/ppermute | solution.py:366
  108.7 13.2 %collective-permute-start.14 = (bf16[2,272,384]{2,1,0:T(8,128)(2,1)S(1)}, bf16[2,272,384]{2,1,0:T(8,128)(2,1)S(1)}, u32[]{:S(2)}, u32[]{:S(2)}) collective-permute-start(bf16[2,272,384]{2,1,0:T(8,128)(2,1)S(1)} %add_behind.3), channel_id=1, source_target_pairs={{0,7},{1,0},{2,1},{3,2},{4,3},{5,4},{6,5},{7,6},{8,15},{9,8},{10,9... | collective-permute-start | bytes 1253384 | tf_op jit(solution)/shard_map/ppermute | solution.py:367
  113.5 14.1 %collective-permute-start.10 = (bf16[2,272,384]{2,1,0:T(8,128)(2,1)S(1)}, bf16[2,272,384]{2,1,0:T(8,128)(2,1)S(1)}, u32[]{:S(2)}, u32[]{:S(2)}) collective-permute-start(bf16[2,272,384]{2,1,0:T(8,128)(2,1)S(1)} %add_ahead.3), channel_id=1, source_target_pairs={{0,1},{1,2},{2,3},{3,4},{4,5},{5,6},{6,7},{7,0},{8,9},{9,10},{10,1... | collective-permute-start | bytes 1253384 | tf_op jit(solution)/shard_map/ppermute | solution.py:366
  122.0 13.2 %collective-permute-start.15 = (bf16[2,272,384]{2,1,0:T(8,128)(2,1)S(1)}, bf16[2,272,384]{2,1,0:T(8,128)(2,1)S(1)}, u32[]{:S(2)}, u32[]{:S(2)}) collective-permute-start(bf16[2,272,384]{2,1,0:T(8,128)(2,1)S(1)} %add_behind.4), channel_id=1, source_target_pairs={{0,7},{1,0},{2,1},{3,2},{4,3},{5,4},{6,5},{7,6},{8,15},{9,8},{10,9... | collective-permute-start | bytes 1253384 | tf_op jit(solution)/shard_map/ppermute | solution.py:367
  127.8 15.1 %collective-permute-start.11 = (bf16[2,272,384]{2,1,0:T(8,128)(2,1)S(1)}, bf16[2,272,384]{2,1,0:T(8,128)(2,1)S(1)}, u32[]{:S(2)}, u32[]{:S(2)}) collective-permute-start(bf16[2,272,384]{2,1,0:T(8,128)(2,1)S(1)} %add_ahead.4), channel_id=1, source_target_pairs={{0,1},{1,2},{2,3},{3,4},{4,5},{5,6},{6,7},{7,0},{8,9},{9,10},{10,1... | collective-permute-start | bytes 1253384 | tf_op jit(solution)/shard_map/ppermute | solution.py:366
  129.7 20.1 %collective-permute-start.8 = (bf16[272,384]{1,0:T(8,128)(2,1)S(1)}, bf16[272,384]{1,0:T(8,128)(2,1)S(1)}, u32[]{:S(2)}, u32[]{:S(2)}) collective-permute-start(bf16[272,384]{1,0:T(8,128)(2,1)S(1)} %get-tuple-element.27), channel_id=1, source_target_pairs={{0,8},{8,0},{1,9},{9,1},{2,10},{10,2},{3,11},{11,3},{4,12},{12,4},... | collective-permute-start | bytes 626696 | tf_op jit(solution)/shard_map/ppermute | solution.py:377
  135.3 14.5 %collective-permute-start.16 = (bf16[272,384]{1,0:T(8,128)(2,1)S(1)}, bf16[272,384]{1,0:T(8,128)(2,1)S(1)}, u32[]{:S(2)}, u32[]{:S(2)}) collective-permute-start(bf16[272,384]{1,0:T(8,128)(2,1)S(1)} %get-tuple-element.37), channel_id=1, source_target_pairs={{0,7},{1,0},{2,1},{3,2},{4,3},{5,4},{6,5},{7,6},{8,15},{9,8},{10,9... | collective-permute-start | bytes 626696 | tf_op jit(solution)/shard_map/ppermute | solution.py:379
  140.9 8.9 %collective-permute-start.18 = (bf16[272,384]{1,0:T(8,128)(2,1)S(1)}, bf16[272,384]{1,0:T(8,128)(2,1)S(1)}, u32[]{:S(2)}, u32[]{:S(2)}) collective-permute-start(bf16[272,384]{1,0:T(8,128)(2,1)S(1)} %get-tuple-element.39), channel_id=1, source_target_pairs={{0,15},{1,8},{2,9},{3,10},{4,11},{5,12},{6,13},{7,14},{8,7},{9,0},... | collective-permute-start | bytes 626696 | tf_op jit(solution)/shard_map/ppermute | solution.py:381
  143.0 10.6 %collective-permute-start.12 = (bf16[272,384]{1,0:T(8,128)(2,1)S(1)}, bf16[272,384]{1,0:T(8,128)(2,1)S(1)}, u32[]{:S(2)}, u32[]{:S(2)}) collective-permute-start(bf16[272,384]{1,0:T(8,128)(2,1)S(1)} %get-tuple-element.32), channel_id=1, source_target_pairs={{0,1},{1,2},{2,3},{3,4},{4,5},{5,6},{6,7},{7,0},{8,9},{9,10},{10,1... | collective-permute-start | bytes 626696 | tf_op jit(solution)/shard_map/ppermute | solution.py:378
  146.7 9.8 %collective-permute-start.17 = (bf16[272,384]{1,0:T(8,128)(2,1)S(1)}, bf16[272,384]{1,0:T(8,128)(2,1)S(1)}, u32[]{:S(2)}, u32[]{:S(2)}) collective-permute-start(bf16[272,384]{1,0:T(8,128)(2,1)S(1)} %get-tuple-element.38), channel_id=1, source_target_pairs={{0,9},{1,10},{2,11},{3,12},{4,13},{5,14},{6,15},{7,8},{8,1},{9,2},... | collective-permute-start | bytes 626696 | tf_op jit(solution)/shard_map/ppermute | solution.py:380
Sparse Core Ops, SparseCore 0:
  19.8 67.4 all-gather.3
